TPU v7x, 32 devices: a whole 2x2x4 slice. The times are simulated.
32 devices in a mesh: head: 4 (over y, core), blk: 8 (over z, x).
Axes of the slice: x: 2, y: 2, z: 4, core: 2. Of those that a mesh axis runs over, the one named last changes fastest.
Arguments:
- first_half: bfloat16 [6144, 1024], P(('head', 'blk')), may hold values from -6 to 6
- second_half: bfloat16 [6144, 1024], P(('head', 'blk')), may hold values from -6 to 6
- grad_first: bfloat16 [6144, 1024], P(('head', 'blk')), may hold values from -6 to 6
- grad_second: bfloat16 [6144, 1024], P(('head', 'blk')), may hold values from -6 to 6
- qk_weight: bfloat16 [1024, 1024], P(('head', 'blk')), may hold values from -0.375 to 0.375
- value_weight: bfloat16 [1024, 1024], P(('head', 'blk')), may hold values from -0.1875 to 0.1875
- out_weight: bfloat16 [1024, 1024], P(('head', 'blk')), may hold values from -1.5 to 1.5
- attn_gain: bfloat16 [1024], P(('head', 'blk')), may hold values from 0.5 to 1.5
- ffn_gain: bfloat16 [1024], P(('head', 'blk')), may hold values from 0.5 to 1.5
- up_weight: bfloat16 [1024, 4096], P(None, ('head', 'blk')), may hold values from -0.1875 to 0.1875
- down_weight: bfloat16 [4096, 1024], P(('head', 'blk')), may hold values from -0.09375 to 0.09375
- stretch_ids: int32 [4, 6144], replicated, may hold values from 0 to 95, as said below
Outputs:
- y_first: bfloat16 [6144, 1024], P(('head', 'blk'))
- y_second: bfloat16 [6144, 1024], P(('head', 'blk'))
- grad_first_half: bfloat16 [6144, 1024], P(('head', 'blk'))
- grad_second_half: bfloat16 [6144, 1024], P(('head', 'blk'))
- grad_qk_weight: float32 [1024, 1024], P(('head', 'blk'))
- grad_value_weight: float32 [1024, 1024], P(('head', 'blk'))
- grad_out_weight: float32 [1024, 1024], P(('head', 'blk'))
- grad_attn_gain: float32 [1024], P(('head', 'blk'))
- grad_ffn_gain: float32 [1024], P(('head', 'blk'))
- grad_up_weight: float32 [1024, 4096], P(None, ('head', 'blk'))
- grad_down_weight: float32 [4096, 1024], P(('head', 'blk'))
Inputs may be any that keep to these rules, and one draw needn't show every extreme that they name: `stretch_ids`: in each of the 4 rounds every stretch number from 0 to 95 is held by exactly 64 tokens. In each round, of the tokens k * 192 to (k + 1) * 192 - 1 at most 6 have stretch numbers in any one range m * 3 to (m + 1) * 3 - 1, and some range holds exactly 6 of them.
All inputs are finite; a program needn't handle non-finite values.
Results may differ from a plain program's by a relative error of at most 0.017.
Values may be sent and summed in bfloat16 or wider, within the bound.
No kernel may reach another device: no remote copies, remote signals or barrier semaphores. Data moves between devices by JAX's collectives and lax.ppermute only.
A program may use at most 128 MiB of HBM per device.

v0:
```python
import jax
import jax.numpy as jnp
from jax import lax
from jax.sharding import PartitionSpec as P

NH = 8
DH = 128
STRETCH = 64


def shifted(value, axis, by):
    devices = lax.axis_size(axis)
    return lax.ppermute(value, axis, [(i, (i + by) % devices) for i in range(devices)])


def layer_norm(values, gains):
    average = jnp.mean(values, axis=-1, keepdims=True)
    centred = values - average
    variance = jnp.mean(centred * centred, axis=-1, keepdims=True)
    return centred * lax.rsqrt(variance + 1e-05) * gains


def key_norm(queries):
    return (
        queries
        * lax.rsqrt(jnp.mean(queries * queries, axis=-1, keepdims=True) + 1e-06)
        * queries.shape[-1] ** (-0.5)
    )


def row_norm(queries):
    return jnp.sqrt(jnp.sum(queries * queries, axis=-1) + 1e-06)


def group_ids(stretch_ids, heads_count, cycle_count, local_rows, cycle_index):
    shaped = stretch_ids.reshape(stretch_ids.shape[0], heads_count, cycle_count, local_rows)
    picked = lax.dynamic_slice_in_dim(shaped, cycle_index, 1, 2)
    places = (
        jnp.arange(heads_count, dtype=jnp.int32)[:, None] * cycle_count + cycle_index
    ) * local_rows
    places = places + jnp.arange(local_rows, dtype=jnp.int32)[None, :]
    return (picked.reshape(stretch_ids.shape[0], heads_count * local_rows), places.reshape(-1))


def pair_counts(query_ids, query_places, key_ids, key_places, nchunk):
    previous = (query_ids + nchunk - 1) % nchunk
    same_stretch = key_ids[:, None, :] == query_ids[:, :, None]
    before = key_ids[:, None, :] == previous[:, :, None]
    counts = jnp.sum((same_stretch | before).astype(jnp.float32), axis=0)
    return counts * (query_places[:, None] != key_places[None, :]).astype(jnp.float32)


def forward_block(queries, query_norms, counts, key_block, value_block):
    scores = jnp.einsum("qhd,khd->hqk", queries, key_block, preferred_element_type=jnp.float32)
    weights = counts[None] * jnp.exp(scores - query_norms.T[:, :, None])
    summed = jnp.einsum(
        "hqk,khd->qhd",
        weights.astype(jnp.bfloat16),
        value_block,
        preferred_element_type=jnp.float32,
    )
    return (jnp.sum(weights, axis=-1), summed)


def backward_block(queries, query_norms, counts, key_block, value_block, grad_summed, grad_totals):
    scores = jnp.einsum("qhd,khd->hqk", queries, key_block, preferred_element_type=jnp.float32)
    weights = counts[None] * jnp.exp(scores - query_norms.T[:, :, None])
    grad_weights = jnp.einsum(
        "qhd,khd->hqk", grad_summed, value_block, preferred_element_type=jnp.float32
    )
    grad_scores_f = weights * (grad_weights + grad_totals[:, :, None])
    grad_scores = grad_scores_f.astype(jnp.bfloat16)
    grad_norms = -jnp.sum(grad_scores_f, axis=-1)
    grad_values = jnp.einsum(
        "hqk,qhd->khd",
        weights.astype(jnp.bfloat16),
        grad_summed,
        preferred_element_type=jnp.float32,
    )
    grad_direct = jnp.einsum(
        "hqk,khd->qhd", grad_scores, key_block, preferred_element_type=jnp.float32
    )
    grad_keys = jnp.einsum("hqk,qhd->khd", grad_scores, queries, preferred_element_type=jnp.float32)
    return (grad_norms, grad_direct, grad_keys, grad_values)


def feed_forward(normed_ffn, grad_output, up_part, down_part):
    pre_act = jnp.dot(normed_ffn, up_part, preferred_element_type=jnp.float32)
    hidden_f, gelu_back = jax.vjp(jax.nn.gelu, pre_act)
    hidden = hidden_f.astype(jnp.bfloat16)
    ffn_result = jnp.dot(hidden, down_part, preferred_element_type=jnp.float32)
    grad_hidden = jnp.dot(grad_output, down_part.T, preferred_element_type=jnp.float32)
    grad_pre = gelu_back(grad_hidden)[0].astype(jnp.bfloat16)
    grad_normed = jnp.dot(grad_pre, up_part.T, preferred_element_type=jnp.float32)
    grad_up = jnp.dot(normed_ffn.T, grad_pre, preferred_element_type=jnp.float32)
    grad_down = jnp.dot(hidden.T, grad_output, preferred_element_type=jnp.float32)
    return (ffn_result, grad_normed, grad_up, grad_down)


def per_device(
    first_half,
    second_half,
    grad_first,
    grad_second,
    qk_weight,
    value_weight,
    out_weight,
    attn_gain,
    ffn_gain,
    up_weight,
    down_weight,
    stretch_ids,
):
    heads_count = lax.axis_size("head")
    cycle_count = lax.axis_size("blk")
    cycle_index = lax.axis_index("blk")
    local_rows = first_half.shape[0]
    model_width = first_half.shape[1]
    group_rows = local_rows * heads_count
    local_heads = NH // heads_count
    nchunk = stretch_ids.shape[1] // STRETCH
    full_qk, full_value, full_out, full_attn_gain, full_ffn_gain, up_part, down_part = (
        lax.all_gather(qk_weight, ("head", "blk"), axis=0, tiled=True),
        lax.all_gather(value_weight, ("head", "blk"), axis=0, tiled=True),
        lax.all_gather(out_weight, ("head", "blk"), axis=0, tiled=True),
        lax.all_gather(attn_gain, ("head", "blk"), axis=0, tiled=True),
        lax.all_gather(ffn_gain, ("head", "blk"), axis=0, tiled=True),
        lax.all_gather(up_weight, ("head", "blk"), axis=1, tiled=True),
        lax.all_gather(down_weight, ("head", "blk"), axis=0, tiled=True),
    )
    second_f = second_half.astype(jnp.float32)
    normed_f, attn_norm_back = jax.vjp(layer_norm, second_f, full_attn_gain.astype(jnp.float32))
    normed = normed_f.astype(jnp.bfloat16)
    query_tok = jnp.dot(normed, full_qk, preferred_element_type=jnp.float32).astype(jnp.bfloat16)
    value_tok = jnp.dot(normed, full_value, preferred_element_type=jnp.float32).astype(jnp.bfloat16)
    query_heads = query_tok.reshape(local_rows, NH, DH)
    value_heads = value_tok.reshape(local_rows, NH, DH)
    queries, values = (
        lax.all_to_all(query_heads, "head", split_axis=1, concat_axis=0, tiled=True),
        lax.all_to_all(value_heads, "head", split_axis=1, concat_axis=0, tiled=True),
    )
    query_f = queries.astype(jnp.float32)
    key_f, key_back = jax.vjp(key_norm, query_f)
    keys = key_f.astype(jnp.bfloat16)
    query_norms, norm_back = jax.vjp(row_norm, query_f)
    query_ids, query_places = group_ids(
        stretch_ids, heads_count, cycle_count, local_rows, cycle_index
    )

    def counts_for(cycle_step):
        source_index = (cycle_index - cycle_step + cycle_count) % cycle_count
        key_ids, key_places = group_ids(
            stretch_ids, heads_count, cycle_count, local_rows, source_index
        )
        return pair_counts(query_ids, query_places, key_ids, key_places, nchunk)

    def rotate(key_block, value_block):
        return shifted((key_block, value_block), "blk", 1)

    def forward_step(cycle_step, carried):
        key_block, value_block, totals, summed = carried
        part_totals, part_summed = forward_block(
            queries, query_norms, counts_for(cycle_step), key_block, value_block
        )
        key_next, value_next = rotate(key_block, value_block)
        return (key_next, value_next, totals + part_totals, summed + part_summed)

    initial = (
        keys,
        values,
        jnp.zeros((local_heads, group_rows), jnp.float32),
        jnp.zeros((group_rows, local_heads, DH), jnp.float32),
    )
    key_block, value_block, totals, summed = lax.fori_loop(
        0, cycle_count - 1, forward_step, initial
    )
    part_totals, part_summed = forward_block(
        queries, query_norms, counts_for(cycle_count - 1), key_block, value_block
    )
    totals = totals + part_totals
    summed = summed + part_summed
    attended = summed / totals.T[:, :, None]
    attn_tok = lax.all_to_all(
        attended.astype(jnp.bfloat16), "head", split_axis=0, concat_axis=1, tiled=True
    ).reshape(local_rows, model_width)
    first_out = first_half.astype(jnp.float32) + jnp.dot(
        attn_tok, full_out, preferred_element_type=jnp.float32
    )
    normed_ffn_f, ffn_norm_back = jax.vjp(layer_norm, first_out, full_ffn_gain.astype(jnp.float32))
    normed_ffn = normed_ffn_f.astype(jnp.bfloat16)
    ffn_result, grad_normed_ffn, grad_up, grad_down = feed_forward(
        normed_ffn, grad_second, up_part, down_part
    )
    second_out = second_f + ffn_result
    grad_mid_ffn, grad_ffn_gain = ffn_norm_back(grad_normed_ffn)
    grad_mid = grad_first.astype(jnp.float32) + grad_mid_ffn
    grad_mid_low = grad_mid.astype(jnp.bfloat16)
    grad_out = jnp.dot(attn_tok.T, grad_mid_low, preferred_element_type=jnp.float32)
    grad_attn_tok = jnp.dot(grad_mid_low, full_out.T, preferred_element_type=jnp.float32).astype(
        jnp.bfloat16
    )
    grad_attn = lax.all_to_all(
        grad_attn_tok.reshape(local_rows, NH, DH), "head", split_axis=1, concat_axis=0, tiled=True
    )
    grad_attn_f = grad_attn.astype(jnp.float32)
    grad_summed = (grad_attn_f / totals.T[:, :, None]).astype(jnp.bfloat16)
    grad_totals = (-jnp.sum(grad_attn_f * attended, axis=-1) / totals.T).T

    def pass_grads(grad_keys, grad_values):
        return (
            shifted(grad_keys.astype(jnp.bfloat16), "blk", 1).astype(grad_keys.dtype),
            shifted(grad_values.astype(jnp.bfloat16), "blk", 1).astype(grad_values.dtype),
        )

    def backward_step(cycle_step, carried):
        key_block, value_block, grad_keys, grad_values, grad_norms, grad_direct = carried
        pieces = backward_block(
            queries,
            query_norms,
            counts_for(cycle_step),
            key_block,
            value_block,
            grad_summed,
            grad_totals,
        )
        key_next, value_next = rotate(key_block, value_block)
        grad_keys, grad_values = pass_grads(grad_keys + pieces[2], grad_values + pieces[3])
        return (
            key_next,
            value_next,
            grad_keys,
            grad_values,
            grad_norms + pieces[0],
            grad_direct + pieces[1],
        )

    zero_rows = jnp.zeros((group_rows, local_heads, DH), jnp.float32)
    initial = (
        keys,
        values,
        zero_rows,
        zero_rows,
        jnp.zeros((local_heads, group_rows), jnp.float32),
        zero_rows,
    )
    carried = lax.fori_loop(0, cycle_count - 1, backward_step, initial)
    pieces = backward_block(
        queries,
        query_norms,
        counts_for(cycle_count - 1),
        carried[0],
        carried[1],
        grad_summed,
        grad_totals,
    )
    grad_keys, grad_values = pass_grads(carried[2] + pieces[2], carried[3] + pieces[3])
    grad_norms = carried[4] + pieces[0]
    grad_direct = carried[5] + pieces[1]
    grad_queries = grad_direct + norm_back(grad_norms.T)[0] + key_back(grad_keys)[0]
    grad_q_tok, grad_v_tok = (
        lax.all_to_all(
            grad_queries.astype(jnp.bfloat16), "head", split_axis=0, concat_axis=1, tiled=True
        ),
        lax.all_to_all(
            grad_values.astype(jnp.bfloat16), "head", split_axis=0, concat_axis=1, tiled=True
        ),
    )
    grad_q_tok = grad_q_tok.reshape(local_rows, model_width)
    grad_v_tok = grad_v_tok.reshape(local_rows, model_width)
    grad_normed = jnp.dot(grad_q_tok, full_qk.T, preferred_element_type=jnp.float32) + jnp.dot(
        grad_v_tok, full_value.T, preferred_element_type=jnp.float32
    )
    grad_qk = jnp.dot(normed.T, grad_q_tok, preferred_element_type=jnp.float32)
    grad_value = jnp.dot(normed.T, grad_v_tok, preferred_element_type=jnp.float32)
    grad_second_attn, grad_attn_gain = attn_norm_back(grad_normed)
    grad_second_total = grad_second.astype(jnp.float32) + grad_second_attn
    sum_qk, sum_value, sum_out, sum_attn_gain, sum_ffn_gain, sum_up, sum_down = (
        lax.psum_scatter(grad_qk, ("head", "blk"), scatter_dimension=0, tiled=True),
        lax.psum_scatter(grad_value, ("head", "blk"), scatter_dimension=0, tiled=True),
        lax.psum_scatter(grad_out, ("head", "blk"), scatter_dimension=0, tiled=True),
        lax.psum_scatter(grad_attn_gain, ("head", "blk"), scatter_dimension=0, tiled=True),
        lax.psum_scatter(grad_ffn_gain, ("head", "blk"), scatter_dimension=0, tiled=True),
        lax.psum_scatter(grad_up, ("head", "blk"), scatter_dimension=1, tiled=True),
        lax.psum_scatter(grad_down, ("head", "blk"), scatter_dimension=0, tiled=True),
    )
    return (
        first_out.astype(jnp.bfloat16),
        second_out.astype(jnp.bfloat16),
        grad_mid.astype(jnp.bfloat16),
        grad_second_total.astype(jnp.bfloat16),
        sum_qk,
        sum_value,
        sum_out,
        sum_attn_gain,
        sum_ffn_gain,
        sum_up,
        sum_down,
    )


def solution(mesh):
    return jax.shard_map(
        per_device,
        mesh=mesh,
        in_specs=(
            P(("head", "blk"), None),
            P(("head", "blk"), None),
            P(("head", "blk"), None),
            P(("head", "blk"), None),
            P(("head", "blk"), None),
            P(("head", "blk"), None),
            P(("head", "blk"), None),
            P(("head", "blk")),
            P(("head", "blk")),
            P(None, ("head", "blk")),
            P(("head", "blk"), None),
            P(),
        ),
        out_specs=(
            P(("head", "blk"), None),
            P(("head", "blk"), None),
            P(("head", "blk"), None),
            P(("head", "blk"), None),
            P(("head", "blk"), None),
            P(("head", "blk"), None),
            P(("head", "blk"), None),
            P(("head", "blk")),
            P(("head", "blk")),
            P(None, ("head", "blk")),
            P(("head", "blk"), None),
        ),
        check_vma=False,
    )
```

profile of v0, /device:TPU:0, one launch (start us, length us, event | category | flops | bytes accessed | tf_op | source)
XLA Modules:
  0.0 1847.8 jit_solution(9138488192577167350)
XLA Ops:
  12.8 42.1 %all-reduce.5 = (bf16[1024]{0:T(1024)(128)(2,1)S(1)}, bf16[1024]{0:T(1024)(128)(2,1)}) all-reduce(bf16[1024]{0:T(1024)(128)(2,1)S(1)} %dynamic-update-slice, bf16[1024]{0:T(1024)(128)(2,1)S(1)} %dynamic-update-slice.1), channel_id=1, replica_groups=mesh['head'=4,'blk'=8] {'head','blk'}, use_global_device_ids=true, to_apply=%add | all-reduce | flops 2048 | bytes 8192
  63.2 7.1 all-gather.6.cloned.1.call-done
  82.4 46.4 %all-gather.8.cloned.1.call-done = bf16[1024,1024]{1,0:T(8,128)(2,1)} async-done(((bf16[32,1024]{1,0:T(8,128)(2,1)}), bf16[1024,1024]{1,0:T(8,128)(2,1)}) %all-gather.8.cloned.1.call-update) | async-done | bytes 2097168 | tf_op jit(solution)/shard_map/all_gather | solution.py:124
  145.9 168.0 %while.56 = (s32[]{:T(128)}, bf16[768,2,128]{2,0,1:T(8,128)(2,1)}, bf16[768,2,128]{2,0,1:T(8,128)(2,1)}, f32[2,768]{1,0:T(2,128)S(1)}, f32[768,2,128]{2,0,1:T(8,...) while((s32[]{:T(128)}, bf16[768,2,128]{2,0,1:T(8,128)(2,1)}, ...), condition=%wide.wide.region_6.7_spmd.clone, body=%wide.wide.region_3.6_spmd.clone.sunk | while | flops 623861760 | bytes 40083980 | solution.py:174
  162.5 9.1 collective-permute-done.1
  185.3 7.1 collective-permute-done
  192.4 7.0 collective-permute-done.1
  215.5 10.7 collective-permute-done.1
  282.0 10.9 collective-permute-done.1
  307.1 6.7 collective-permute-done.1
  326.1 6.7 all-to-all-done.2
  336.1 7.9 fusion.118
  344.0 84.8 %all-gather.12.cloned.1.call-done = bf16[1024,4096]{1,0:T(8,128)(2,1)} async-done(((bf16[1024,128]{1,0:T(8,128)(2,1)}), bf16[1024,4096]{1,0:T(8,128)(2,1)}) %all-gather.12.cloned.1.call-update) | async-done | bytes 8388624 | tf_op jit(solution)/shard_map/all_gather | solution.py:128
  428.8 10.0 fusion.44
  458.7 328.1 %while.57 = (s32[]{:T(128)}, bf16[768,2,128]{2,0,1:T(8,128)(2,1)}, bf16[768,2,128]{2,0,1:T(8,128)(2,1)}, f32[768,2,128]{2,0,1:T(8,128)}, f32[768,2,128]{2,0,1:T(...) while((s32[]{:T(128)}, bf16[768,2,128]{2,0,1:T(8,128)(2,1)}, ...), condition=%wide.wide.region_17.18_spmd.clone, body=%wide.wide.region_14.17_spmd.clone.sunk | while | flops 1534944768 | bytes 84966120 | solution.py:246
  490.5 7.1 collective-permute-done.4
  538.2 6.5 collective-permute-done.4
  584.6 8.0 collective-permute-done.4
  631.9 6.7 collective-permute-done.4
  725.1 8.2 collective-permute-done.4
  794.4 12.5 collective-permute-done.6
  810.2 11.0 all_to_all.90
  836.3 13.4 collective-permute-done.7
  850.1 10.7 all_to_all.91
  866.9 8.2 fusion.102
  877.0 9.2 fusion.104
  886.2 6.4 fusion.68
  895.9 38.0 %all-reduce.4 = (f32[1024]{0:T(1024)S(1)}, f32[1024]{0:T(1024)S(1)}) all-reduce(f32[1024]{0:T(1024)S(1)} %get-tuple-element.1167, f32[1024]{0:T(1024)S(1)} %copy-done.54), channel_id=5, replica_groups=mesh['head'=4,'blk'=8] {'head','blk'}, use_global_device_ids=true, to_apply=%region_26.27.clone | all-reduce | flops 2048 | bytes 16384
  936.2 41.0 %reduce-scatter.6.cloned.1.call-done = f32[32,1024]{1,0:T(8,128)} async-done(((f32[1024,1024]{1,0:T(8,128)}), f32[32,1024]{1,0:T(8,128)}) %reduce-scatter.6.cloned.1.call-update) | async-done | bytes 131088 | tf_op jit(solution)/shard_map/reduce_scatter | solution.py:278
  977.3 144.7 %reduce-scatter.8.cloned.1.call-done = f32[32,1024]{1,0:T(8,128)} async-done(((f32[1024,1024]{1,0:T(8,128)}), f32[32,1024]{1,0:T(8,128)}) %reduce-scatter.8.cloned.1.call-update) | async-done | bytes 131088 | tf_op jit(solution)/shard_map/reduce_scatter | solution.py:279
  1121.9 358.5 %reduce-scatter.12.cloned.1.call-done = f32[1024,128]{1,0:T(8,128)} async-done(((f32[1024,4096]{1,0:T(8,128)}), f32[1024,128]{1,0:T(8,128)}) %reduce-scatter.12.cloned.1.call-update) | async-done | bytes 524304 | tf_op jit(solution)/shard_map/reduce_scatter | solution.py:283
  1480.4 360.1 %reduce-scatter.14.cloned.1.call-done = f32[128,1024]{1,0:T(8,128)} async-done(((f32[4096,1024]{1,0:T(8,128)}), f32[128,1024]{1,0:T(8,128)}) %reduce-scatter.14.cloned.1.call-update) | async-done | bytes 524304 | tf_op jit(solution)/shard_map/reduce_scatter | solution.py:284
  (698 shorter events, 524.6 us)
Async XLA Ops:
  7.2 63.1 %all-gather.6.cloned.1.call-start = ((), (), s32[]{:S(2)}) async-start(), calls=%async_computation.11 | async-start | bytes 2162688 | tf_op jit(solution)/shard_map/all_gather | solution.py:123
  7.9 120.9 %all-gather.8.cloned.1.call-start = ((), (), s32[]{:S(2)}) async-start(), calls=%async_computation.12 | async-start | bytes 2162688 | tf_op jit(solution)/shard_map/all_gather | solution.py:124
  8.7 324.8 %all-gather.10.cloned.1.call-start = ((), (), s32[]{:S(2)}) async-start(), calls=%async_computation.13 | async-start | bytes 2162688 | tf_op jit(solution)/shard_map/all_gather | solution.py:125
  9.4 326.7 %all-gather.14.cloned.1.call-start = ((), (), s32[]{:S(2)}) async-start(), calls=%async_computation.15 | async-start | bytes 8650752 | tf_op jit(solution)/shard_map/all_gather | solution.py:129
  10.0 418.8 %all-gather.12.cloned.1.call-start = ((), (), s32[]{:S(2)}) async-start(), calls=%async_computation.14 | async-start | bytes 8650752 | tf_op jit(solution)/shard_map/all_gather | solution.py:128
  73.4 58.5 %all-to-all-start = ((bf16[192,8,128]{2,0,1:T(8,128)(2,1)}), bf16[192,8,128]{2,0,1:T(8,128)(2,1)S(1)}, u32[]{:S(2)}, u32[]{:S(2)}) async-start(bf16[192,8,128]{2,0,1:T(8,128)(2,1)} %bitcast.147), calls=%async_computation | async-start | bytes 786432 | tf_op jit(solution)/shard_map/all_to_all | solution.py:139
  149.3 22.3 %collective-permute-start.1 = (bf16[768,2,128]{2,0,1:T(8,128)(2,1)S(1)}, bf16[768,2,128]{2,0,1:T(8,128)(2,1)}, u32[]{:S(2)}, u32[]{:S(2)}) collective-permute-start(bf16[768,2,128]{2,0,1:T(8,128)(2,1)S(1)} %copy.206), channel_id=1, source_target_pairs={{0,1},{1,2},{2,3},{3,4},{4,5},{5,6},{6,7},{7,0},{8,9},{9,10},{10,1... | collective-permute-start | bytes 1179656 | tf_op jit(solution)/shard_map/while/body/eval_jaxpr/ppermute | solution.py:13
  173.6 25.8 %collective-permute-start.1 = (bf16[768,2,128]{2,0,1:T(8,128)(2,1)S(1)}, bf16[768,2,128]{2,0,1:T(8,128)(2,1)}, u32[]{:S(2)}, u32[]{:S(2)}) collective-permute-start(bf16[768,2,128]{2,0,1:T(8,128)(2,1)S(1)} %copy.206), channel_id=1, source_target_pairs={{0,1},{1,2},{2,3},{3,4},{4,5},{5,6},{6,7},{7,0},{8,9},{9,10},{10,1... | collective-permute-start | bytes 1179656 | tf_op jit(solution)/shard_map/while/body/eval_jaxpr/ppermute | solution.py:13
  201.4 24.8 %collective-permute-start.1 = (bf16[768,2,128]{2,0,1:T(8,128)(2,1)S(1)}, bf16[768,2,128]{2,0,1:T(8,128)(2,1)}, u32[]{:S(2)}, u32[]{:S(2)}) collective-permute-start(bf16[768,2,128]{2,0,1:T(8,128)(2,1)S(1)} %copy.206), channel_id=1, source_target_pairs={{0,1},{1,2},{2,3},{3,4},{4,5},{5,6},{6,7},{7,0},{8,9},{9,10},{10,1... | collective-permute-start | bytes 1179656 | tf_op jit(solution)/shard_map/while/body/eval_jaxpr/ppermute | solution.py:13
  260.8 21.2 %collective-permute-start = (bf16[768,2,128]{2,0,1:T(8,128)(2,1)S(1)}, bf16[768,2,128]{2,0,1:T(8,128)(2,1)}, u32[]{:S(2)}, u32[]{:S(2)}) collective-permute-start(bf16[768,2,128]{2,0,1:T(8,128)(2,1)S(1)} %copy.205), channel_id=1, source_target_pairs={{0,1},{1,2},{2,3},{3,4},{4,5},{5,6},{6,7},{7,0},{8,9},{9,10},{10,1... | collective-permute-start | bytes 1179656 | tf_op jit(solution)/shard_map/while/body/eval_jaxpr/ppermute | solution.py:13
  261.8 31.2 %collective-permute-start.1 = (bf16[768,2,128]{2,0,1:T(8,128)(2,1)S(1)}, bf16[768,2,128]{2,0,1:T(8,128)(2,1)}, u32[]{:S(2)}, u32[]{:S(2)}) collective-permute-start(bf16[768,2,128]{2,0,1:T(8,128)(2,1)S(1)} %copy.206), channel_id=1, source_target_pairs={{0,1},{1,2},{2,3},{3,4},{4,5},{5,6},{6,7},{7,0},{8,9},{9,10},{10,1... | collective-permute-start | bytes 1179656 | tf_op jit(solution)/shard_map/while/body/eval_jaxpr/ppermute | solution.py:13
  449.8 486.4 %reduce-scatter.10.cloned.1.call-start = ((), (), s32[]{:S(2)}) async-start(), calls=%async_computation.18 | async-start | bytes 4325376 | tf_op jit(solution)/shard_map/reduce_scatter | solution.py:280
  452.6 524.7 %reduce-scatter.6.cloned.1.call-start = ((), (), s32[]{:S(2)}) async-start(), calls=%async_computation.16 | async-start | bytes 4325376 | tf_op jit(solution)/shard_map/reduce_scatter | solution.py:278
  459.7 45.8 %collective-permute-start.2 = (bf16[768,2,128]{2,0,1:T(8,128)(2,1)S(1)}, bf16[768,2,128]{2,0,1:T(8,128)(2,1)}, u32[]{:S(2)}, u32[]{:S(2)}) collective-permute-start(bf16[768,2,128]{2,0,1:T(8,128)(2,1)S(1)} %copy.222), channel_id=1, source_target_pairs={{0,1},{1,2},{2,3},{3,4},{4,5},{5,6},{6,7},{7,0},{8,9},{9,10},{10,1... | collective-permute-start | bytes 1179656 | tf_op jit(solution)/shard_map/while/body/eval_jaxpr/ppermute | solution.py:13
  462.8 42.7 %collective-permute-start.3 = (bf16[768,2,128]{2,0,1:T(8,128)(2,1)}, bf16[768,2,128]{2,0,1:T(8,128)(2,1)}, u32[]{:S(2)}, u32[]{:S(2)}) collective-permute-start(bf16[768,2,128]{2,0,1:T(8,128)(2,1)} %copy.223), channel_id=1, source_target_pairs={{0,1},{1,2},{2,3},{3,4},{4,5},{5,6},{6,7},{7,0},{8,9},{9,10},{10,1... | collective-permute-start | bytes 1179656 | tf_op jit(solution)/shard_map/while/body/eval_jaxpr/ppermute | solution.py:13
  483.0 21.5 %collective-permute-start.5 = (bf16[768,2,128]{2,0,1:T(8,128)(2,1)}, bf16[768,2,128]{2,0,1:T(8,128)(2,1)S(1)}, u32[]{:S(2)}, u32[]{:S(2)}) collective-permute-start(bf16[768,2,128]{2,0,1:T(8,128)(2,1)} %fusion.229), channel_id=1, source_target_pairs={{0,1},{1,2},{2,3},{3,4},{4,5},{5,6},{6,7},{7,0},{8,9},{9,10},{10,1... | collective-permute-start | bytes 1179656 | tf_op jit(solution)/shard_map/while/body/eval_jaxpr/ppermute | solution.py:13
  506.5 46.5 %collective-permute-start.2 = (bf16[768,2,128]{2,0,1:T(8,128)(2,1)S(1)}, bf16[768,2,128]{2,0,1:T(8,128)(2,1)}, u32[]{:S(2)}, u32[]{:S(2)}) collective-permute-start(bf16[768,2,128]{2,0,1:T(8,128)(2,1)S(1)} %copy.222), channel_id=1, source_target_pairs={{0,1},{1,2},{2,3},{3,4},{4,5},{5,6},{6,7},{7,0},{8,9},{9,10},{10,1... | collective-permute-start | bytes 1179656 | tf_op jit(solution)/shard_map/while/body/eval_jaxpr/ppermute | solution.py:13
  508.3 44.7 %collective-permute-start.3 = (bf16[768,2,128]{2,0,1:T(8,128)(2,1)}, bf16[768,2,128]{2,0,1:T(8,128)(2,1)}, u32[]{:S(2)}, u32[]{:S(2)}) collective-permute-start(bf16[768,2,128]{2,0,1:T(8,128)(2,1)} %copy.223), channel_id=1, source_target_pairs={{0,1},{1,2},{2,3},{3,4},{4,5},{5,6},{6,7},{7,0},{8,9},{9,10},{10,1... | collective-permute-start | bytes 1179656 | tf_op jit(solution)/shard_map/while/body/eval_jaxpr/ppermute | solution.py:13
  554.0 46.6 %collective-permute-start.2 = (bf16[768,2,128]{2,0,1:T(8,128)(2,1)S(1)}, bf16[768,2,128]{2,0,1:T(8,128)(2,1)}, u32[]{:S(2)}, u32[]{:S(2)}) collective-permute-start(bf16[768,2,128]{2,0,1:T(8,128)(2,1)S(1)} %copy.222), channel_id=1, source_target_pairs={{0,1},{1,2},{2,3},{3,4},{4,5},{5,6},{6,7},{7,0},{8,9},{9,10},{10,1... | collective-permute-start | bytes 1179656 | tf_op jit(solution)/shard_map/while/body/eval_jaxpr/ppermute | solution.py:13
  558.1 42.5 %collective-permute-start.3 = (bf16[768,2,128]{2,0,1:T(8,128)(2,1)}, bf16[768,2,128]{2,0,1:T(8,128)(2,1)}, u32[]{:S(2)}, u32[]{:S(2)}) collective-permute-start(bf16[768,2,128]{2,0,1:T(8,128)(2,1)} %copy.223), channel_id=1, source_target_pairs={{0,1},{1,2},{2,3},{3,4},{4,5},{5,6},{6,7},{7,0},{8,9},{9,10},{10,1... | collective-permute-start | bytes 1179656 | tf_op jit(solution)/shard_map/while/body/eval_jaxpr/ppermute | solution.py:13
  579.5 20.1 %collective-permute-start.5 = (bf16[768,2,128]{2,0,1:T(8,128)(2,1)}, bf16[768,2,128]{2,0,1:T(8,128)(2,1)S(1)}, u32[]{:S(2)}, u32[]{:S(2)}) collective-permute-start(bf16[768,2,128]{2,0,1:T(8,128)(2,1)} %fusion.229), channel_id=1, source_target_pairs={{0,1},{1,2},{2,3},{3,4},{4,5},{5,6},{6,7},{7,0},{8,9},{9,10},{10,1... | collective-permute-start | bytes 1179656 | tf_op jit(solution)/shard_map/while/body/eval_jaxpr/ppermute | solution.py:13
  601.6 44.3 %collective-permute-start.2 = (bf16[768,2,128]{2,0,1:T(8,128)(2,1)S(1)}, bf16[768,2,128]{2,0,1:T(8,128)(2,1)}, u32[]{:S(2)}, u32[]{:S(2)}) collective-permute-start(bf16[768,2,128]{2,0,1:T(8,128)(2,1)S(1)} %copy.222), channel_id=1, source_target_pairs={{0,1},{1,2},{2,3},{3,4},{4,5},{5,6},{6,7},{7,0},{8,9},{9,10},{10,1... | collective-permute-start | bytes 1179656 | tf_op jit(solution)/shard_map/while/body/eval_jaxpr/ppermute | solution.py:13
  603.9 42.1 %collective-permute-start.3 = (bf16[768,2,128]{2,0,1:T(8,128)(2,1)}, bf16[768,2,128]{2,0,1:T(8,128)(2,1)}, u32[]{:S(2)}, u32[]{:S(2)}) collective-permute-start(bf16[768,2,128]{2,0,1:T(8,128)(2,1)} %copy.223), channel_id=1, source_target_pairs={{0,1},{1,2},{2,3},{3,4},{4,5},{5,6},{6,7},{7,0},{8,9},{9,10},{10,1... | collective-permute-start | bytes 1179656 | tf_op jit(solution)/shard_map/while/body/eval_jaxpr/ppermute | solution.py:13
  646.9 46.5 %collective-permute-start.2 = (bf16[768,2,128]{2,0,1:T(8,128)(2,1)S(1)}, bf16[768,2,128]{2,0,1:T(8,128)(2,1)}, u32[]{:S(2)}, u32[]{:S(2)}) collective-permute-start(bf16[768,2,128]{2,0,1:T(8,128)(2,1)S(1)} %copy.222), channel_id=1, source_target_pairs={{0,1},{1,2},{2,3},{3,4},{4,5},{5,6},{6,7},{7,0},{8,9},{9,10},{10,1... | collective-permute-start | bytes 1179656 | tf_op jit(solution)/shard_map/while/body/eval_jaxpr/ppermute | solution.py:13
  649.9 43.6 %collective-permute-start.3 = (bf16[768,2,128]{2,0,1:T(8,128)(2,1)}, bf16[768,2,128]{2,0,1:T(8,128)(2,1)}, u32[]{:S(2)}, u32[]{:S(2)}) collective-permute-start(bf16[768,2,128]{2,0,1:T(8,128)(2,1)} %copy.223), channel_id=1, source_target_pairs={{0,1},{1,2},{2,3},{3,4},{4,5},{5,6},{6,7},{7,0},{8,9},{9,10},{10,1... | collective-permute-start | bytes 1179656 | tf_op jit(solution)/shard_map/while/body/eval_jaxpr/ppermute | solution.py:13
  694.4 46.6 %collective-permute-start.2 = (bf16[768,2,128]{2,0,1:T(8,128)(2,1)S(1)}, bf16[768,2,128]{2,0,1:T(8,128)(2,1)}, u32[]{:S(2)}, u32[]{:S(2)}) collective-permute-start(bf16[768,2,128]{2,0,1:T(8,128)(2,1)S(1)} %copy.222), channel_id=1, source_target_pairs={{0,1},{1,2},{2,3},{3,4},{4,5},{5,6},{6,7},{7,0},{8,9},{9,10},{10,1... | collective-permute-start | bytes 1179656 | tf_op jit(solution)/shard_map/while/body/eval_jaxpr/ppermute | solution.py:13
  698.6 42.4 %collective-permute-start.3 = (bf16[768,2,128]{2,0,1:T(8,128)(2,1)}, bf16[768,2,128]{2,0,1:T(8,128)(2,1)}, u32[]{:S(2)}, u32[]{:S(2)}) collective-permute-start(bf16[768,2,128]{2,0,1:T(8,128)(2,1)} %copy.223), channel_id=1, source_target_pairs={{0,1},{1,2},{2,3},{3,4},{4,5},{5,6},{6,7},{7,0},{8,9},{9,10},{10,1... | collective-permute-start | bytes 1179656 | tf_op jit(solution)/shard_map/while/body/eval_jaxpr/ppermute | solution.py:13
  742.0 44.8 %collective-permute-start.2 = (bf16[768,2,128]{2,0,1:T(8,128)(2,1)S(1)}, bf16[768,2,128]{2,0,1:T(8,128)(2,1)}, u32[]{:S(2)}, u32[]{:S(2)}) collective-permute-start(bf16[768,2,128]{2,0,1:T(8,128)(2,1)S(1)} %copy.222), channel_id=1, source_target_pairs={{0,1},{1,2},{2,3},{3,4},{4,5},{5,6},{6,7},{7,0},{8,9},{9,10},{10,1... | collective-permute-start | bytes 1179656 | tf_op jit(solution)/shard_map/while/body/eval_jaxpr/ppermute | solution.py:13
  744.6 42.2 %collective-permute-start.3 = (bf16[768,2,128]{2,0,1:T(8,128)(2,1)}, bf16[768,2,128]{2,0,1:T(8,128)(2,1)}, u32[]{:S(2)}, u32[]{:S(2)}) collective-permute-start(bf16[768,2,128]{2,0,1:T(8,128)(2,1)} %copy.223), channel_id=1, source_target_pairs={{0,1},{1,2},{2,3},{3,4},{4,5},{5,6},{6,7},{7,0},{8,9},{9,10},{10,1... | collective-permute-start | bytes 1179656 | tf_op jit(solution)/shard_map/while/body/eval_jaxpr/ppermute | solution.py:13
  827.8 294.1 %reduce-scatter.8.cloned.1.call-start = ((), (), s32[]{:S(2)}) async-start(), calls=%async_computation.17 | async-start | bytes 4325376 | tf_op jit(solution)/shard_map/reduce_scatter | solution.py:279
  865.3 615.1 %reduce-scatter.12.cloned.1.call-start = ((), (), s32[]{:S(2)}) async-start(), calls=%async_computation.19 | async-start | bytes 17301504 | tf_op jit(solution)/shard_map/reduce_scatter | solution.py:283
  875.2 965.3 %reduce-scatter.14.cloned.1.call-start = ((), (), s32[]{:S(2)}) async-start(), calls=%async_computation.20 | async-start | bytes 17301504 | tf_op jit(solution)/shard_map/reduce_scatter | solution.py:284
  (133 other events, 1791.9 us)
Sparse Core Ops, SparseCore 0:
  11.0 59.2 all-gather.5
  73.3 55.4 all-gather.7
  131.8 63.1 all-gather.9
  197.8 134.4 all-gather.13
  335.0 93.7 all-gather.11
  453.1 363.9 reduce-scatter.9
  827.9 149.3 reduce-scatter.5
  980.1 141.7 reduce-scatter.7
  1124.8 355.5 reduce-scatter.11
  1483.1 357.3 reduce-scatter.13
where the time goes:
time: 1860 us; the launch traced here: 1850 us
  waiting for transfers between devices  1240 us (67%)
  matrix products  196 us (11%)
  local copies, waits for them, and re-layouts  124 us (7%)
  other arithmetic  118 us (6%)
  blocking collectives  102 us (5%)
  starting transfers between devices  54.7 us (3%)
    reduce_scatter x1, waiting for transfers between devices, per_device(): lax.psum_scatter(grad_down, ('head', 'blk'), scatter_dimension=0, tiled=T...  360 us
    reduce_scatter x1, waiting for transfers between devices, per_device(): lax.psum_scatter(grad_up, ('head', 'blk'), scatter_dimension=1, tiled=True)  358 us
    ppermute x44, waiting for transfers between devices, shifted(): lax.ppermute(value, axis, [(i, (i + by) % devices) for i in range(devices)])  176 us
    reduce_scatter x1, waiting for transfers between devices, per_device(): lax.psum_scatter(grad_value, ('head', 'blk'), scatter_dimension=0, tiled=...  145 us
    all_gather x1, waiting for transfers between devices, per_device(): lax.all_gather(up_weight, ('head', 'blk'), axis=1, tiled=True)  84.8 us
    unnamed x2, blocking collectives  80.1 us
    all_gather x1, waiting for transfers between devices, per_device(): lax.all_gather(value_weight, ('head', 'blk'), axis=0, tiled=True)  46.4 us
    while x140, local copies, waits for them, and re-layouts  44.4 us
  transfers between devices with their start and end apart: 58, of which 37 were waited for; matrix products, arithmetic and copies ran while one was open for 22% of the time, Pallas kernels for 0%

commit v1 on v0

--- a/solution.py
+++ b/solution.py
@@ -1,6 +1,10 @@
+import functools
+
 import jax
 import jax.numpy as jnp
 from jax import lax
+from jax.experimental import pallas as pl
+from jax.experimental.pallas import tpu as pltpu
 from jax.sharding import PartitionSpec as P
 
 NH = 8
@@ -97,7 +101,7 @@
     return (ffn_result, grad_normed, grad_up, grad_down)
 
 
-def per_device(
+def ring_plan(
     first_half,
     second_half,
     grad_first,
@@ -298,36 +302,622 @@
     )
 
 
+BITS = ("y", "core", "z_hi", "z_lo", "x")
+Y, CORE, Z_HI, Z_LO, X = 16, 8, 4, 2, 1
+HEAD_AXES = ("core", "z_hi", "x")
+LOG2E = 1.4426950408889634
+HIGH_BITS = -2139062144
+NT = (((1,), (1,)), ((), ()))
+NN = (((1,), (0,)), ((), ()))
+TN = (((0,), (0,)), ((), ()))
+F32, BF16, I32 = jnp.float32, jnp.bfloat16, jnp.int32
+VMEM = pl.BlockSpec(memory_space=pltpu.VMEM)
+SMEM = pl.BlockSpec(memory_space=pltpu.SMEM)
+
+
+def dot(left, right, dims=NN):
+    return lax.dot_general(left, right, dims, preferred_element_type=F32)
+
+
+def swap(value, mask):
+    return lax.ppermute(value, BITS, [(i, i ^ mask) for i in range(32)])
+
+
+def after(value, *others):
+    return lax.optimization_barrier((value, *others))[0]
+
+
+def shaped(*shape, dtype=BF16):
+    return jax.ShapeDtypeStruct(shape, dtype)
+
+
+def call(kernel, inputs, out_shape, name, flops, mib=40, specs=None):
+    flat = jax.tree.leaves(out_shape)
+    moved = sum(a.size * a.dtype.itemsize for a in [*inputs, *flat])
+    return pl.pallas_call(
+        kernel,
+        in_specs=specs or [VMEM] * len(inputs),
+        out_specs=jax.tree.map(lambda _: VMEM, out_shape),
+        out_shape=out_shape,
+        compiler_params=pltpu.CompilerParams(vmem_limit_bytes=mib * 2**20),
+        cost_estimate=pl.CostEstimate(flops=flops, bytes_accessed=moved, transcendentals=0),
+        name=name,
+    )(*inputs)
+
+
+def with_cores(near):
+    return near + [swap(part, CORE) for part in near]
+
+
+def gather_xy(value):
+    return with_cores([value, swap(value, X), swap(value, Y), swap(value, X | Y)])
+
+
+def gather_xz(value):
+    over_z = swap(value, Z_HI)
+    return with_cores([value, swap(value, X), over_z, swap(over_z, X)])
+
+
+def scatter_xy(blocks):
+    arrived = [swap(block, CORE) for block in blocks[4:]]
+    sums = [
+        (near.astype(F32) + far.astype(F32)).astype(BF16)
+        for near, far in zip(blocks[1:4], arrived[1:], strict=True)
+    ]
+    sent = [swap(part, mask) for part, mask in zip(sums, (X, Y, X | Y), strict=True)]
+    return [blocks[0], arrived[0], *sent]
+
+
+def normalised(values):
+    centred = values - jnp.mean(values, axis=-1, keepdims=True)
+    rstd = lax.rsqrt(jnp.mean(centred * centred, axis=-1, keepdims=True) + 1e-05)
+    return centred * rstd, rstd
+
+
+def norm_back(scaled_grads, xhat, rstd):
+    return rstd * (
+        scaled_grads
+        - jnp.mean(scaled_grads, axis=-1, keepdims=True)
+        - xhat * jnp.mean(scaled_grads * xhat, axis=-1, keepdims=True)
+    )
+
+
+def to_row(column_ref, row_ref):
+    for i in range(row_ref.shape[1] // 128):
+        chunk = slice(i * 128, (i + 1) * 128)
+        square = jnp.broadcast_to(column_ref[chunk, :], (128, 128))
+        row_ref[:, chunk] = square.T[0:8, :]
+
+
+def project_kernel(*refs):
+    blocks, (gain_ref, weight_ref), outs = refs[:8], refs[8:10], refs[10:]
+    normed_ref, q_ref, k_ref, v_ref, norm_ref, row_ref = outs
+    weight = weight_ref[...]
+    gain = gain_ref[0:1, :]
+    for i, block in enumerate(blocks):
+        rows = pl.ds(i * block.shape[0], block.shape[0])
+        normed = (normalised(block[...].astype(F32))[0] * gain).astype(BF16)
+        normed_ref[rows, :] = normed
+        both = dot(normed, weight)
+        queries = both[:, :DH].astype(BF16)
+        q_ref[rows, :] = queries
+        v_ref[rows, :] = both[:, DH:].astype(BF16)
+        query_f = queries.astype(F32)
+        squares = jnp.sum(query_f * query_f, axis=-1, keepdims=True)
+        k_ref[rows, :] = (query_f * lax.rsqrt(squares / DH + 1e-06) * DH ** (-0.5)).astype(BF16)
+        norm_ref[rows, :] = jnp.sqrt(squares + 1e-06) * LOG2E
+    to_row(norm_ref, row_ref)
+
+
+def pair_count(one, other, neighbour, diagonal):
+    high = jnp.int32(HIGH_BITS)
+    match = ((high - (one ^ other)) | (high - (one ^ neighbour))) & high
+    counts = lax.population_count(match)
+    if diagonal is not None:
+        across = lax.broadcasted_iota(I32, counts.shape, 0) - lax.broadcasted_iota(
+            I32, counts.shape, 1
+        )
+        counts = jnp.where(across == diagonal, 0, counts)
+    return counts.astype(F32)
+
+
+def forward_kernel(*refs, tile, own, first, last):
+    q_ref, n_ref, qid_ref, k_ref, v_ref, kid_ref = refs[:6]
+    acc_in = None if first else refs[6]
+    head_ref = refs[6 + (not first)] if last else None
+    acc_ref = refs[-2] if last else refs[-1]
+    step = pl.program_id(0)
+
+    @pl.when(step == 0)
+    def _():
+        acc_ref[...] = jnp.zeros_like(acc_ref) if first else acc_in[...]
+
+    keys = k_ref[...]
+    count = keys.shape[0]
+    values = jnp.concatenate([v_ref[...], jnp.ones((count, DH), BF16)], axis=1)
+    for i in range(q_ref.shape[0] // tile):
+        rows = slice(i * tile, (i + 1) * tile)
+        scores = dot(q_ref[rows, :], keys, NT)
+        powers = jnp.exp2(scores * LOG2E - n_ref[rows, :])
+        diagonal = step * count - i * tile if own else None
+        counts = pair_count(qid_ref[rows, :], kid_ref[0:1, :], kid_ref[2:3, :], diagonal)
+        acc_ref[rows, :] += dot((powers * counts).astype(BF16), values)
+
+    if last:
+        send_ref = refs[-1]
+        rows = send_ref.shape[1]
+
+        @pl.when(step == pl.num_programs(0) - 1)
+        def _():
+            for j in range(NH):
+                block = acc_ref[j * rows : (j + 1) * rows, :]
+                send_ref[head_ref[0] ^ j] = (block[:, :DH] / block[:, DH:]).astype(BF16)
+
+
+def forward_call(queries, norms, ids, keys, values, part, acc, head=None, tk=768, tile=256):
+    nq, nk = queries.shape[0], keys.shape[0]
+    steps = nk // tk
+    column = pl.BlockSpec((nq, 1), lambda j: (0, 0))
+    full = pl.BlockSpec((nq, DH), lambda j: (0, 0))
+    keyed = pl.BlockSpec((tk, DH), lambda j: (j, 0))
+    wide = pl.BlockSpec((nq, 2 * DH), lambda j: (0, 0))
+    listed = pl.BlockSpec((8, tk), lambda j: (0, part * steps + j))
+    inputs = [queries, norms, ids[0], keys, values, ids[1]]
+    specs = [full, column, column, keyed, keyed, listed]
+    out_shape, out_specs = [shaped(nq, 2 * DH, dtype=F32)], [wide]
+    if acc is not None:
+        inputs.append(acc)
+        specs.append(wide)
+    if head is not None:
+        inputs.append(head)
+        specs.append(SMEM)
+        out_shape.append(shaped(NH, nq // NH, DH))
+        out_specs.append(pl.BlockSpec((NH, nq // NH, DH), lambda j: (0, 0, 0)))
+    return pl.pallas_call(
+        functools.partial(
+            forward_kernel,
+            tile=tile,
+            own=part == 0,
+            first=acc is None,
+            last=head is not None,
+        ),
+        grid=(steps,),
+        in_specs=specs,
+        out_specs=out_specs,
+        out_shape=out_shape,
+        input_output_aliases={} if acc is None else {6: 0},
+        compiler_params=pltpu.CompilerParams(vmem_limit_bytes=40 * 2**20),
+        cost_estimate=pl.CostEstimate(
+            flops=32 * nq * nk * DH, bytes_accessed=2 * nq * nk, transcendentals=nq * nk
+        ),
+        name="attention_forward",
+    )(*inputs)
+
+
+def backward_kernel(*refs, tile, own, first):
+    q_ref, g_ref, n_ref, t_ref, qid_ref, k_ref, v_ref, kid_ref = refs[:8]
+    dq_ref, dk_ref, dv_ref = refs[-3:]
+    step = pl.program_id(0)
+
+    @pl.when(step == 0)
+    def _():
+        dq_ref[...] = jnp.zeros_like(dq_ref) if first else refs[8][...]
+
+    keys, values, key_ids = k_ref[...], v_ref[...], kid_ref[...]
+    count = keys.shape[0]
+    wide_keys = jnp.concatenate([keys, jnp.ones(keys.shape, BF16)], axis=1)
+    grad_keys = jnp.zeros(keys.shape, F32)
+    grad_values = jnp.zeros(keys.shape, F32)
+    for i in range(q_ref.shape[0] // tile):
+        rows = slice(i * tile, (i + 1) * tile)
+        queries, grads = q_ref[rows, :], g_ref[rows, :]
+        scores = dot(keys, queries, NT)
+        powers = jnp.exp2(scores * LOG2E - n_ref[0:1, rows])
+        diagonal = i * tile - step * count if own else None
+        weights = powers * pair_count(key_ids, qid_ref[0:1, rows], qid_ref[1:2, rows], diagonal)
+        grad_weights = dot(values, grads, NT)
+        grad_scores = (weights * (grad_weights + t_ref[0:1, rows])).astype(BF16)
+        grad_values = grad_values + dot(weights.astype(BF16), grads)
+        grad_keys = grad_keys + dot(grad_scores, queries)
+        dq_ref[rows, :] += dot(grad_scores, wide_keys, TN)
+    dk_ref[...] = grad_keys.astype(BF16)
+    dv_ref[...] = grad_values.astype(BF16)
+
+
+def backward_call(queries, grads, norms, terms, ids, keys, values, part, acc, tk=768, tile=256):
+    nq, nk = queries.shape[0], keys.shape[0]
+    steps = nk // tk
+    full = pl.BlockSpec((nq, DH), lambda j: (0, 0))
+    row = pl.BlockSpec((8, nq), lambda j: (0, 0))
+    keyed = pl.BlockSpec((tk, DH), lambda j: (j, 0))
+    wide = pl.BlockSpec((nq, 2 * DH), lambda j: (0, 0))
+    listed = pl.BlockSpec((tk, 1), lambda j: (part * steps + j, 0))
+    more = [] if acc is None else [acc]
+    return pl.pallas_call(
+        functools.partial(backward_kernel, tile=tile, own=part == 0, first=acc is None),
+        grid=(steps,),
+        in_specs=[full, full, row, row, row, keyed, keyed, listed] + [wide] * len(more),
+        out_specs=[wide, keyed, keyed],
+        out_shape=[shaped(nq, 2 * DH, dtype=F32), shaped(nk, DH), shaped(nk, DH)],
+        input_output_aliases={8: 0} if more else {},
+        compiler_params=pltpu.CompilerParams(vmem_limit_bytes=40 * 2**20),
+        cost_estimate=pl.CostEstimate(
+            flops=40 * nq * nk * DH, bytes_accessed=2 * nq * nk, transcendentals=nq * nk
+        ),
+        name="attention_backward",
+    )(queries, grads, norms, terms, ids[1], keys, values, ids[0], *more)
+
+
+def out_kernel(attn_ref, half_ref, weight_ref, gain_ref, low_ref, out_ref, normed_ref):
+    attn = jnp.concatenate([attn_ref[h] for h in range(NH)], axis=1)
+    first_out = half_ref[...].astype(F32) + dot(attn, weight_ref[...])
+    out_ref[...] = first_out
+    low_ref[...] = first_out.astype(BF16)
+    normed_ref[...] = (normalised(first_out)[0] * gain_ref[0:1, :]).astype(BF16)
+
+
+def hidden_back_kernel(*refs):
+    blocks, weight_ref, out_ref = refs[:8], refs[8], refs[9]
+    down = weight_ref[:, weight_ref.shape[1] // 2 :]
+    for i, block in enumerate(blocks):
+        rows = pl.ds(i * block.shape[0], block.shape[0])
+        out_ref[rows, :] = dot(block[...], down, NT)
+
+
+def ffn_kernel(*refs):
+    blocks, (back_ref, weight_ref), outs = refs[:8], refs[8:10], refs[10:]
+    hidden_ref, grad_ref = outs[8:]
+    up = weight_ref[:, : weight_ref.shape[1] // 2]
+    slope = 0.7978845608028654
+    for i, block in enumerate(blocks):
+        rows = pl.ds(i * block.shape[0], block.shape[0])
+        v = dot(block[...], up, NT)
+        square = v * v
+        t = jnp.tanh(slope * v * (1.0 + 0.044715 * square))
+        half = 0.5 * (1.0 + t)
+        hidden_ref[rows, :] = (v * half).astype(BF16)
+        back = half + 0.5 * v * (1.0 - t * t) * slope * (1.0 + 3 * 0.044715 * square)
+        grad = (back_ref[rows, :] * back).astype(BF16)
+        grad_ref[rows, :] = grad
+        outs[i][...] = dot(grad, up).astype(BF16)
+
+
+def ffn_rest_kernel(*refs):
+    blocks, grads = refs[:8], refs[8:16]
+    hidden_ref, grad_ref, weight_ref = refs[16:19]
+    outs, sum_ref = refs[19:27], refs[27]
+    width = weight_ref.shape[1] // 2
+    down = weight_ref[:, width:]
+    for i in range(8):
+        rows = pl.ds(i * blocks[i].shape[0], blocks[i].shape[0])
+        outs[i][...] = dot(hidden_ref[rows, :], down).astype(BF16)
+    inputs = jnp.concatenate([block[...] for block in blocks], axis=0)
+    sum_ref[:, :width] = dot(grad_ref[...], inputs, TN).astype(BF16)
+    cotangents = jnp.concatenate([block[...] for block in grads], axis=0)
+    sum_ref[:, width:] = dot(hidden_ref[...], cotangents, TN).astype(BF16)
+
+
+def mid_kernel(*refs):
+    parts, rest, outs = refs[:5], refs[5:9], refs[9:]
+    out_ref, first_ref, gain_ref, weight_ref = rest
+    mid_ref, send_ref, gain_sum_ref = outs
+    xhat, rstd = normalised(out_ref[...])
+    grads = sum(part[...].astype(F32) for part in parts)
+    gain_sum_ref[...] = jnp.broadcast_to(
+        jnp.sum(grads * xhat, axis=0, keepdims=True), gain_sum_ref.shape
+    )
+    mid = first_ref[...].astype(F32) + norm_back(grads * gain_ref[0:1, :], xhat, rstd)
+    mid = mid.astype(BF16)
+    mid_ref[...] = mid
+    grad_attn = dot(mid, weight_ref[...], NT).astype(BF16)
+    for h in range(NH):
+        send_ref[h] = grad_attn[:, h * DH : (h + 1) * DH]
+
+
+def turn_kernel(arrived_ref, acc_ref, head_ref, grads_ref, row_ref, attn_ref, column_ref):
+    rows = arrived_ref.shape[1]
+    for j in range(NH):
+        place = slice(j * rows, (j + 1) * rows)
+        block = acc_ref[place, :]
+        totals = block[:, DH:]
+        attended = block[:, :DH] / totals
+        attn_ref[place, :] = attended.astype(BF16)
+        grad_attn = arrived_ref[head_ref[0] ^ j].astype(F32)
+        grads_ref[place, :] = (grad_attn / totals).astype(BF16)
+        column_ref[place, :] = (
+            -jnp.sum(grad_attn * attended, axis=-1, keepdims=True) / totals[:, :1]
+        )
+    to_row(column_ref, row_ref)
+
+
+def gather_grads_kernel(*refs):
+    direct_ref, q_ref, n_ref, head_ref = refs[:4]
+    key_refs, value_refs = refs[4:7], refs[7:10]
+    send_ref, both_ref = refs[10:]
+    rows = send_ref.shape[1]
+    for j in range(NH):
+        place = slice(j * rows, (j + 1) * rows)
+        grad_keys = sum(ref[place, :].astype(F32) for ref in key_refs)
+        grad_values = sum(ref[place, :].astype(F32) for ref in value_refs)
+        queries = q_ref[place, :].astype(F32)
+        inverse = lax.rsqrt(jnp.mean(queries * queries, axis=-1, keepdims=True) + 1e-06)
+        mean_part = jnp.mean(grad_keys * queries, axis=-1, keepdims=True)
+        grad_norms = -direct_ref[place, DH:]
+        grad_queries = (
+            direct_ref[place, :DH]
+            + grad_norms * queries * (LOG2E / n_ref[place, :])
+            + (inverse * DH ** (-0.5)) * (grad_keys - queries * (inverse * inverse * mean_part))
+        )
+        both = jnp.concatenate([grad_queries.astype(BF16), grad_values.astype(BF16)], axis=1)
+        both_ref[place, :] = both
+        send_ref[head_ref[0] ^ j] = both
+
+
+def last_kernel(arrived_ref, half_ref, grad_ref, gain_ref, weight_ref, out_ref):
+    width = half_ref.shape[1]
+    grad_q = jnp.concatenate([arrived_ref[h][:, :DH] for h in range(NH)], axis=1)
+    grad_v = jnp.concatenate([arrived_ref[h][:, DH:] for h in range(NH)], axis=1)
+    grads = dot(grad_q, weight_ref[:, :width], NT) + dot(grad_v, weight_ref[:, width:], NT)
+    xhat, rstd = normalised(half_ref[...].astype(F32))
+    out_ref[...] = (
+        grad_ref[...].astype(F32) + norm_back(grads * gain_ref[0:1, :], xhat, rstd)
+    ).astype(BF16)
+
+
+def cube_plan(
+    first_half,
+    second_half,
+    grad_first,
+    grad_second,
+    qk_weight,
+    value_weight,
+    out_weight,
+    attn_gain,
+    ffn_gain,
+    up_weight,
+    down_weight,
+    stretch_ids,
+):
+    y, core, z_hi, z_lo, x = (lax.axis_index(name) for name in BITS)
+    head = (core * 4 + z_hi * 2 + x).astype(I32).reshape(1)
+    rows, width = first_half.shape
+    wide_rows = rows * 8
+    own_rows = qk_weight.shape[0]
+    rounds, tokens = stretch_ids.shape
+    nchunk = tokens // STRETCH
+    row_block = shaped(rows, width)
+
+    gains = jnp.concatenate([attn_gain, ffn_gain, jnp.zeros((128 - 2 * own_rows,), BF16)])
+    gains = jnp.broadcast_to(gains.astype(F32), (32, 1, 128))
+    gains = lax.all_to_all(gains, BITS, 0, 0, tiled=True).reshape(32, 128)
+    attn_gain_row = jnp.broadcast_to(gains[:, :own_rows].reshape(1, width), (8, width))
+    ffn_gain_row = jnp.broadcast_to(
+        gains[:, own_rows : 2 * own_rows].reshape(1, width), (8, width)
+    )
+    columns = jnp.stack([qk_weight, value_weight]).reshape(2, own_rows, NH, DH)
+    columns = columns.transpose(2, 1, 0, 3).reshape(NH, own_rows, 2 * DH)
+    heads_of = [((d >> 3) & 1) * 4 + ((d >> 2) & 1) * 2 + (d & 1) for d in range(32)]
+    columns = jnp.stack([columns[h] for h in heads_of])
+    columns = lax.all_to_all(columns, BITS, 0, 0, tiled=True).reshape(width, 2 * DH)
+    blocks = gather_xz(second_half)
+
+    out_full = lax.all_gather(out_weight, BITS, axis=0, tiled=True)
+    ffn_weights = lax.all_gather(
+        jnp.concatenate([up_weight.T, down_weight], axis=1), ("z_hi", "z_lo"), axis=0, tiled=True
+    )
+    qv_full = lax.all_gather(
+        jnp.concatenate([qk_weight, value_weight], axis=1), BITS, axis=0, tiled=True
+    )
+
+    ids = stretch_ids.reshape(rounds, 2, 2, 2, 2, 2, rows)
+    for axis, bit in enumerate((y, core, z_hi, z_lo, x), 1):
+        ids = jnp.where(bit == 1, jnp.flip(ids, axis), ids)
+    ids = ids.transpose(0, 4, 1, 2, 3, 5, 6).reshape(rounds, tokens)
+
+    def packed(numbers):
+        return sum(numbers[r] << (8 * r) for r in range(rounds))
+
+    ids_row = packed(ids)
+    ids_rows = jnp.concatenate(
+        [
+            ids_row[None],
+            packed((ids + nchunk - 1) % nchunk)[None],
+            packed((ids + 1) % nchunk)[None],
+            jnp.zeros((5, tokens), I32),
+        ]
+    )
+    ids_both = (ids_row[:, None], ids_rows)
+
+    normed, queries, keys, values, norms, norm_row = call(
+        project_kernel,
+        [*blocks, attn_gain_row, columns],
+        [
+            shaped(wide_rows, width),
+            *[shaped(wide_rows, DH)] * 3,
+            shaped(wide_rows, 1, dtype=F32),
+            shaped(8, wide_rows, dtype=F32),
+        ],
+        "project",
+        8 * wide_rows * width * DH,
+    )
+    key_y, value_z = swap(keys, Y), swap(values, Z_LO)
+    key_z, value_y = swap(keys, Z_LO), swap(values, Y)
+    key_yz, value_yz = swap(key_y, Z_LO), swap(value_z, Y)
+    key_parts = [keys, key_y, key_z, key_yz]
+    value_parts = [values, value_y, value_z, value_yz]
+    acc = None
+    for part in range(4):
+        acc, *attn_send = forward_call(
+            queries,
+            norms,
+            ids_both,
+            key_parts[part],
+            value_parts[part],
+            part,
+            acc,
+            head if part == 3 else None,
+        )
+    attn_tok = lax.all_to_all(attn_send[0], HEAD_AXES, 0, 0, tiled=True)
+
+    y_first, first_out, normed_ffn = call(
+        out_kernel,
+        [attn_tok, first_half, out_full, ffn_gain_row],
+        [row_block, shaped(rows, width, dtype=F32), row_block],
+        "project_out",
+        2 * rows * width * width,
+    )
+    units = ffn_weights.shape[0]
+    ffn_flops = 2 * wide_rows * width * units
+    cotangents = gather_xy(grad_second)
+    hidden_back = call(
+        hidden_back_kernel,
+        [*cotangents, ffn_weights],
+        shaped(wide_rows, units, dtype=F32),
+        "hidden_back",
+        ffn_flops,
+    )
+    ffn_in = gather_xy(normed_ffn)
+    *grad_blocks, hidden, grad_pre = call(
+        ffn_kernel,
+        [*ffn_in, hidden_back, ffn_weights],
+        [row_block] * 8 + [shaped(wide_rows, units)] * 2,
+        "feed_forward",
+        3 * ffn_flops,
+    )
+    grad_parts = scatter_xy(grad_blocks)
+    *ffn_blocks, grad_ffn = call(
+        ffn_rest_kernel,
+        [*ffn_in, *cotangents, hidden, grad_pre, ffn_weights],
+        [row_block] * 8 + [shaped(units, 2 * width)],
+        "feed_forward_rest",
+        4 * ffn_flops,
+    )
+    grad_mid, grad_attn, gain_sum = call(
+        mid_kernel,
+        [*grad_parts, first_out, grad_first, ffn_gain_row, out_full],
+        [row_block, shaped(NH, rows, DH), shaped(8, width, dtype=F32)],
+        "mid",
+        2 * rows * width * width,
+    )
+
+    grad_attn = lax.all_to_all(grad_attn, HEAD_AXES, 0, 0, tiled=True)
+    grads, term_row, attn, _ = call(
+        turn_kernel,
+        [grad_attn, acc, head],
+        [
+            shaped(wide_rows, DH),
+            shaped(8, wide_rows, dtype=F32),
+            shaped(wide_rows, DH),
+            shaped(wide_rows, 1, dtype=F32),
+        ],
+        "turn",
+        wide_rows * DH,
+        specs=[VMEM, VMEM, SMEM],
+    )
+
+    def backward(part, acc):
+        return backward_call(
+            queries,
+            grads,
+            norm_row,
+            term_row,
+            ids_both,
+            key_parts[part],
+            value_parts[part],
+            part,
+            acc,
+        )
+
+    direct, far_key, far_value = backward(3, None)
+    far_key, far_value = swap(far_key, Y), swap(far_value, Z_LO)
+    direct, z_key, z_value = backward(2, direct)
+    z_value = swap(z_value, Z_LO)
+    direct = after(direct, far_key, far_value)
+    direct, y_key, y_value = backward(1, direct)
+    y_key = swap(y_key, Y)
+    z_key = swap((z_key.astype(F32) + far_key.astype(F32)).astype(BF16), Z_LO)
+    y_value = swap((y_value.astype(F32) + far_value.astype(F32)).astype(BF16), Y)
+    direct, grad_keys, grad_values = backward(0, direct)
+
+    ffn_blocks = [after(block, grad_attn) for block in ffn_blocks]
+    second_out = second_half.astype(F32) + sum(
+        part.astype(F32) for part in scatter_xy(ffn_blocks)
+    )
+    grad_ffn = lax.psum_scatter(
+        grad_ffn, ("z_hi", "z_lo"), scatter_dimension=0, tiled=True
+    ).astype(F32)
+    gain_sum = after(gain_sum, grad_attn)[0].reshape(32, 1, own_rows)
+    gain_sum = jnp.pad(gain_sum, ((0, 0), (0, 0), (0, 128 - own_rows)))
+    gain_sum = lax.all_to_all(gain_sum, BITS, 0, 0, tiled=True)
+    grad_ffn_gain = jnp.sum(gain_sum, axis=(0, 1))[:own_rows]
+
+    def halve(value, axis, bit, mask):
+        keep = lax.dynamic_index_in_dim(value, bit, axis, keepdims=False)
+        send = lax.dynamic_index_in_dim(value, 1 - bit, axis, keepdims=False)
+        return keep + swap(send.astype(BF16), mask).astype(F32)
+
+    grad_mid_all = jnp.concatenate(gather_xz(after(grad_mid, grad_attn)), axis=0)
+    grad_out = dot(attn, grad_mid_all, TN).reshape(2, 2, DH // 4, width)
+    grad_out = halve(halve(grad_out, 1, y, Y), 0, z_lo, Z_LO)
+    owners = []
+    for d in range(32):
+        dy, dc, dh, dl, dx = ((d >> s) & 1 for s in (4, 3, 2, 1, 0))
+        owners.append((d, dc * 16 + dh * 8 + dx * 4 + dl * 2 + dy))
+    grad_out = lax.ppermute(grad_out.astype(BF16), BITS, owners).astype(F32)
+
+    send, grad_both = call(
+        gather_grads_kernel,
+        [direct, queries, norms, head, grad_keys, y_key, z_key, grad_values, y_value, z_value],
+        [shaped(NH, rows, 2 * DH), shaped(wide_rows, 2 * DH)],
+        "gather_grads",
+        wide_rows * DH,
+        specs=[VMEM] * 3 + [SMEM] + [VMEM] * 6,
+    )
+    arrived = lax.all_to_all(send, HEAD_AXES, 0, 0, tiled=True)
+    grad_second_half = call(
+        last_kernel,
+        [arrived, second_half, grad_second, attn_gain_row, qv_full],
+        row_block,
+        "last",
+        4 * rows * width * width,
+    )
+
+    grad_rows = dot(normed, grad_both, TN).reshape(2, 2, 2, 2, 2, own_rows, 2 * DH)
+    grad_rows = halve(halve(grad_rows, 0, y, Y), 2, z_lo, Z_LO)
+    grad_rows = grad_rows.reshape(8, own_rows, 2 * DH).astype(BF16)
+    grad_rows = lax.all_to_all(grad_rows, HEAD_AXES, 0, 0, tiled=True).astype(F32)
+    grad_qk = grad_rows[:, :, :DH].transpose(1, 0, 2).reshape(own_rows, width)
+    grad_value = grad_rows[:, :, DH:].transpose(1, 0, 2).reshape(own_rows, width)
+    grad_attn_gain = jnp.sum(
+        qk_weight.astype(F32) * grad_qk + value_weight.astype(F32) * grad_value, axis=-1
+    ) / attn_gain.astype(F32)
+
+    return (
+        y_first,
+        second_out.astype(BF16),
+        grad_mid,
+        grad_second_half,
+        grad_qk,
+        grad_value,
+        grad_out,
+        grad_attn_gain,
+        grad_ffn_gain,
+        grad_ffn[:, :width].T,
+        grad_ffn[:, width:],
+    )
+
+
 def solution(mesh):
+    if dict(mesh.shape) == {"head": 4, "blk": 8}:
+        plan, axes = cube_plan, BITS
+        mesh = jax.sharding.Mesh(mesh.devices.reshape((2,) * 5), BITS)
+    else:
+        plan, axes = ring_plan, ("head", "blk")
+    by_row, by_column, vector = P(axes, None), P(None, axes), P(axes)
     return jax.shard_map(
-        per_device,
+        plan,
         mesh=mesh,
-        in_specs=(
-            P(("head", "blk"), None),
-            P(("head", "blk"), None),
-            P(("head", "blk"), None),
-            P(("head", "blk"), None),
-            P(("head", "blk"), None),
-            P(("head", "blk"), None),
-            P(("head", "blk"), None),
-            P(("head", "blk")),
-            P(("head", "blk")),
-            P(None, ("head", "blk")),
-            P(("head", "blk"), None),
-            P(),
-        ),
-        out_specs=(
-            P(("head", "blk"), None),
-            P(("head", "blk"), None),
-            P(("head", "blk"), None),
-            P(("head", "blk"), None),
-            P(("head", "blk"), None),
-            P(("head", "blk"), None),
-            P(("head", "blk"), None),
-            P(("head", "blk")),
-            P(("head", "blk")),
-            P(None, ("head", "blk")),
-            P(("head", "blk"), None),
-        ),
+        in_specs=(by_row,) * 7 + (vector, vector, by_column, by_row, P()),
+        out_specs=(by_row,) * 7 + (vector, vector, by_column, by_row),
         check_vma=False,
     )

time: 1860 us -> 446 us (0.24)
  waiting for transfers between devices: 1240 us -> 173 us
  matrix products: 196 us -> 1.6 us
  blocking collectives: 102 us -> 0 us
  other arithmetic: 118 us -> 17 us
  Pallas kernels: 0 us -> 89.6 us
  local copies, waits for them, and re-layouts: 124 us -> 72.4 us
    reduce_scatter x5 -> x1, waiting for transfers between devices: 904 us -> 0.01 us  [cube_plan(): lax.psum_scatter(grad_ffn, ('z_hi', 'z_lo'), scatter_dimension=0, tiled=T...]
    dot_general x71 -> x2, matrix products: 196 us -> 1.6 us  [dot(): return lax.dot_general(left, right, dims, preferred_element_type=F32)]
    all_gather x5 -> x3, waiting for transfers between devices: 138 us -> 0.01 us  [the longest x1 0.01 us: cube_plan(): out_full = lax.all_gather(out_weight, BITS, axis=0, tiled=True)]
    pallas_call x0 -> x17, Pallas kernels: none -> 89.6 us  [the longest x9 40.9 us: call(): pl.pallas_call(kernel, in_specs=specs or [VMEM] * len(inputs), out_specs=...]
    unnamed x2 -> x0, blocking collectives: 80.1 us -> none
    while x142 -> x0, local copies, waits for them, and re-layouts: 46.9 us -> none
    unnamed x112 -> x203, local copies, waits for them, and re-layouts: 13.4 us -> 58.5 us
    reduce_sum x23 -> x2, other arithmetic: 37.3 us -> 1.39 us  [the longest x1 0.83 us: cube_plan(): jnp.sum(qk_weight.astype(F32) * grad_qk + value_weight.astype(F32) * grad...]
  transfers between devices with their start and end apart: 58 -> 70, of which waited for: 37 -> 22; matrix products, arithmetic and copies ran while one was open for 22% -> 12% of each run, Pallas kernels for 0% -> 20%
where the time goes in v1:
time: 446 us; the launch traced here: 440 us
  waiting for transfers between devices  173 us (39%)
  Pallas kernels  89.6 us (20%)
  local copies, waits for them, and re-layouts  72.4 us (16%)
  starting transfers between devices  71.2 us (16%)
  other arithmetic  17 us (4%)
  between operations  15.3 us (3%)
    ppermute x58, waiting for transfers between devices, swap(): return lax.ppermute(value, BITS, [(i, i ^ mask) for i in range(32)])  149 us
    unnamed x203, local copies, waits for them, and re-layouts  58.5 us
    ppermute x58, starting transfers between devices, swap(): return lax.ppermute(value, BITS, [(i, i ^ mask) for i in range(32)])  43.3 us
    pallas_call x9, Pallas kernels, call(): pl.pallas_call(kernel, in_specs=specs or [VMEM] * len(inputs), out_specs=...  40.9 us
    pallas_call x4, Pallas kernels, backward_call(): pl.pallas_call(functools.partial(backward_kernel, tile=tile, own=part ==...  29.1 us
    pallas_call x4, Pallas kernels, forward_call(): pl.pallas_call(functools.partial(forward_kernel, tile=tile, own=part == 0...  19.6 us
    all_to_all x1, waiting for transfers between devices, cube_plan(): lax.all_to_all(columns, BITS, 0, 0, tiled=True).reshape(width, 2 * DH)  11.8 us
  transfers between devices with their start and end apart: 70, of which 22 were waited for; matrix products, arithmetic and copies ran while one was open for 12% of the time, Pallas kernels for 20%

profile of v1, /device:TPU:0, one launch (start us, length us, event | category | flops | bytes accessed | tf_op | source)
XLA Modules:
  0.0 439.7 jit_solution(12624749053291305848)
XLA Ops:
  10.9 4.1 collective-permute-start.1
  48.8 7.8 %collective-permute-done.2.refs_3_ = bf16[192,1024]{1,0:T(8,128)(2,1)} collective-permute-done((bf16[192,1024]{1,0:T(8,128)(2,1)}, bf16[192,1024]{1,0:T(8,128)(2,1)}, u32[]{:S(2)}, u32[]{:S(2)}) %collective-permute-start.2) | collective-permute-done | bytes 393248 | tf_op jit(solution)/shard_map/ppermute | solution.py:323
  56.7 6.1 %all-to-all-start.1 = ((bf16[32,32,256]{2,1,0:T(8,128)(2,1)}), bf16[32,32,256]{2,1,0:T(8,128)(2,1)}, u32[]{:S(2)}, u32[]{:S(2)}) async-start(bf16[32,32,256]{2,1,0:T(8,128)(2,1)} %constant_dynamic-update-slice_fusion), calls=%async_computation.1 | async-start | bytes 1048576 | tf_op jit(solution)/shard_map/all_to_all | solution.py:701
  68.7 11.8 %all-to-all-done.1 = bf16[32,32,256]{2,1,0:T(8,128)(2,1)} async-done(((bf16[32,32,256]{2,1,0:T(8,128)(2,1)}), bf16[32,32,256]{2,1,0:T(8,128)(2,1)}, u32[]{:S(2)}, u32[]{:S(2)}) %all-to-all-start.1) | async-done | bytes 524320 | tf_op jit(solution)/shard_map/all_to_all | solution.py:701
  80.5 5.6 %project.1 = (bf16[1536,1024]{1,0:T(8,128)(2,1)S(1)}, bf16[1536,128]{1,0:T(8,128)(2,1)S(1)}, bf16[1536,128]{1,0:T(8,128)(2,1)S(1)}, bf16[1536,128]{1,0:T(8,128)(...) custom-call(bf16[192,1024]{1,0:T(8,128)(2,1)S(1)} %copy-done.9, bf16[192,1024]{1,0:T(8,128)(2,1)} %collective-permute-done.refs_1_, ...), custom_call_target="tpu_custom_call" | custom-call | flops 1610612736 | bytes 8083456 | tf_op jit(solution)/shard_map/project/pallas_call | solution.py:337
  92.6 5.2 %attention_forward.4.refs_6_ = f32[1536,256]{1,0:T(8,128)S(1)} custom-call(bf16[1536,128]{1,0:T(8,128)(2,1)S(1)} %get-tuple-element.72.refs_0_.refs_1_, f32[1536,1]{1,0:T(8,128)S(1)} %get-tuple-element.73.refs_1_.refs_2_, s32[6144,1]{1,0:T(8,128)S(1)} %add.235.refs_2_.refs_7_, bf16[1536,128]{1,0:T(8,128)(2,1)S(1)} %get-tuple-element.74.refs_3_.refs_5_, ...), custom_call_target="tpu_custom_call" | custom-call | flops 9663676416 | bytes 4718592 | tf_op jit(solution)/shard_map/attention_forward/pallas_call | solution.py:476
  97.9 22.5 %collective-permute-done.9.refs_4_.refs_6_ = bf16[1536,128]{1,0:T(8,128)(2,1)S(1)} collective-permute-done((bf16[1536,128]{1,0:T(8,128)(2,1)S(1)}, bf16[1536,128]{1,0:T(8,128)(2,1)S(1)}, u32[]{:S(2)}, u32[]{:S(2)}) %collective-permute-start.9) | collective-permute-done | bytes 393248 | tf_op jit(solution)/shard_map/ppermute | solution.py:323
  120.6 4.6 %attention_forward.5.refs_6_ = f32[1536,256]{1,0:T(8,128)S(1)} custom-call(bf16[1536,128]{1,0:T(8,128)(2,1)S(1)} %get-tuple-element.72.refs_0_.refs_1_, f32[1536,1]{1,0:T(8,128)S(1)} %get-tuple-element.73.refs_1_.refs_2_, s32[6144,1]{1,0:T(8,128)S(1)} %add.235.refs_2_.refs_7_, ...), custom_call_target="tpu_custom_call", output_to_operand_aliasing={{}: (6, {})} | custom-call | flops 9663676416 | bytes 4718592 | tf_op jit(solution)/shard_map/attention_forward/pallas_call | solution.py:476
  125.3 10.7 %collective-permute-done.11.refs_3_.refs_5_ = bf16[1536,128]{1,0:T(8,128)(2,1)S(1)} collective-permute-done((bf16[1536,128]{1,0:T(8,128)(2,1)S(1)}, bf16[1536,128]{1,0:T(8,128)(2,1)S(1)}, u32[]{:S(2)}, u32[]{:S(2)}) %collective-permute-start.11) | collective-permute-done | bytes 393248 | tf_op jit(solution)/shard_map/ppermute | solution.py:323
  135.9 5.0 %attention_forward.6.refs_6_ = f32[1536,256]{1,0:T(8,128)S(1)} custom-call(bf16[1536,128]{1,0:T(8,128)(2,1)S(1)} %get-tuple-element.72.refs_0_.refs_1_, f32[1536,1]{1,0:T(8,128)S(1)} %get-tuple-element.73.refs_1_.refs_2_, s32[6144,1]{1,0:T(8,128)S(1)} %add.235.refs_2_.refs_7_, ...), custom_call_target="tpu_custom_call", output_to_operand_aliasing={{}: (6, {})} | custom-call | flops 9663676416 | bytes 4718592 | tf_op jit(solution)/shard_map/attention_forward/pallas_call | solution.py:476
  144.4 4.7 %attention_forward.7 = (f32[1536,256]{1,0:T(8,128)S(1)}, bf16[8,192,128]{2,1,0:T(8,128)(2,1)S(1)}) custom-call(bf16[1536,128]{1,0:T(8,128)(2,1)S(1)} %get-tuple-element.72.refs_0_.refs_1_, f32[1536,1]{1,0:T(8,128)S(1)} %get-tuple-element.73.refs_1_.refs_2_, s32[6144,1]{1,0:T(8,128)S(1)} %add.235.refs_2_.refs_7_, ...), custom_call_target="tpu_custom_call", output_to_operand_aliasing={{0}: (6, {})} | custom-call | flops 9663676416 | bytes 4718592 | tf_op jit(solution)/shard_map/attention_forward/pallas_call | solution.py:476
  151.0 4.1 all-to-all-start.2
  158.7 13.7 %collective-permute-done.20.refs_1_.refs_9_ = bf16[192,1024]{1,0:T(8,128)(2,1)} collective-permute-done((bf16[192,1024]{1,0:T(8,128)(2,1)S(1)}, bf16[192,1024]{1,0:T(8,128)(2,1)}, u32[]{:S(2)}, u32[]{:S(2)}) %collective-permute-start.20) | collective-permute-done | bytes 393248 | tf_op jit(solution)/shard_map/ppermute | solution.py:323
  184.4 8.4 %collective-permute-done.13.refs_1_ = bf16[192,1024]{1,0:T(8,128)(2,1)} collective-permute-done((bf16[192,1024]{1,0:T(8,128)(2,1)}, bf16[192,1024]{1,0:T(8,128)(2,1)}, u32[]{:S(2)}, u32[]{:S(2)}) %collective-permute-start.13) | collective-permute-done | bytes 393248 | tf_op jit(solution)/shard_map/ppermute | solution.py:323
  193.3 11.9 %collective-permute-done.15.refs_3_ = bf16[192,1024]{1,0:T(8,128)(2,1)} collective-permute-done((bf16[192,1024]{1,0:T(8,128)(2,1)}, bf16[192,1024]{1,0:T(8,128)(2,1)}, u32[]{:S(2)}, u32[]{:S(2)}) %collective-permute-start.15) | collective-permute-done | bytes 393248 | tf_op jit(solution)/shard_map/ppermute | solution.py:323
  208.5 4.6 %hidden_back.1.refs_8_ = f32[1536,512]{1,0:T(8,128)S(1)} custom-call(bf16[192,1024]{1,0:T(8,128)(2,1)S(1)} %copy-done.6, bf16[192,1024]{1,0:T(8,128)(2,1)} %collective-permute-done.20.refs_1_.refs_9_, bf16[192,1024]{1,0:T(8,128)(2,1)} %collective-permute-done.21.refs_2_.refs_10_, bf16[192,1024]{1,0:T(8,128)(2,1)} %collective-permute-done.22.refs_3_.refs_11_, ...), custom_call_target="tpu_custom_call" | custom-call | flops 1610612736 | bytes 8388608 | tf_op jit(solution)/shard_map/hidden_back/pallas_call | solution.py:337
  214.9 9.8 %feed_forward.1 = (bf16[192,1024]{1,0:T(8,128)(2,1)S(1)}, bf16[192,1024]{1,0:T(8,128)(2,1)S(1)}, bf16[192,1024]{1,0:T(8,128)(2,1)S(1)}, bf16[192,1024]{1,0:T(8,1...) custom-call(bf16[192,1024]{1,0:T(8,128)(2,1)} %get-tuple-element.78., ...), custom_call_target="tpu_custom_call" | custom-call | flops 4831838208 | bytes 14680064 | tf_op jit(solution)/shard_map/feed_forward/pallas_call | solution.py:337
  231.8 9.0 %collective-permute-done.33.refs_4_ = bf16[192,1024]{1,0:T(8,128)(2,1)S(1)} collective-permute-done((bf16[192,1024]{1,0:T(8,128)(2,1)S(1)}, bf16[192,1024]{1,0:T(8,128)(2,1)S(1)}, u32[]{:S(2)}, u32[]{:S(2)}) %collective-permute-start.33) | collective-permute-done | bytes 393248 | tf_op jit(solution)/shard_map/ppermute | solution.py:323
  240.7 7.5 %collective-permute-done.31.refs_3_ = bf16[192,1024]{1,0:T(8,128)(2,1)S(1)} collective-permute-done((bf16[192,1024]{1,0:T(8,128)(2,1)S(1)}, bf16[192,1024]{1,0:T(8,128)(2,1)S(1)}, u32[]{:S(2)}, u32[]{:S(2)}) %collective-permute-start.31) | collective-permute-done | bytes 393248 | tf_op jit(solution)/shard_map/ppermute | solution.py:323
  251.7 4.1 all-to-all-start.3
  259.8 9.7 %feed_forward_rest.1 = (bf16[192,1024]{1,0:T(8,128)(2,1)S(1)}, bf16[192,1024]{1,0:T(8,128)(2,1)S(1)}, bf16[192,1024]{1,0:T(8,128)(2,1)S(1)}, bf16[192,1024]{1,0:...) custom-call(bf16[192,1024]{1,0:T(8,128)(2,1)} %get-tuple-element.78., ...), custom_call_target="tpu_custom_call" | custom-call | flops 6442450944 | bytes 16777216 | tf_op jit(solution)/shard_map/feed_forward_rest/pallas_call | solution.py:337
  293.5 7.1 %attention_backward.4 = (f32[1536,256]{1,0:T(8,128)S(1)}, bf16[1536,128]{1,0:T(8,128)(2,1)S(1)}, bf16[1536,128]{1,0:T(8,128)(2,1)S(1)}) custom-call(bf16[1536,128]{1,0:T(8,128)(2,1)S(1)} %copy-done.31, bf16[1536,128]{1,0:T(8,128)(2,1)S(1)} %get-tuple-element.109.refs_1_, f32[8,1536]{1,0:T(8,128)S(1)} %copy-done.71, ...), custom_call_target="tpu_custom_call" | custom-call | flops 12079595520 | bytes 4718592 | tf_op jit(solution)/shard_map/attention_backward/pallas_call | solution.py:536
  303.8 7.2 %attention_backward.5 = (f32[1536,256]{1,0:T(8,128)S(1)}, bf16[1536,128]{1,0:T(8,128)(2,1)S(1)}, bf16[1536,128]{1,0:T(8,128)(2,1)S(1)}) custom-call(bf16[1536,128]{1,0:T(8,128)(2,1)S(1)} %copy-done.31, bf16[1536,128]{1,0:T(8,128)(2,1)S(1)} %get-tuple-element.109.refs_1_, f32[8,1536]{1,0:T(8,128)S(1)} %copy-done.71, ...), custom_call_target="tpu_custom_call", output_to_operand_aliasing={{0}: (8, {})} | custom-call | flops 12079595520 | bytes 4718592 | tf_op jit(solution)/shard_map/attention_backward/pallas_call | solution.py:536
  311.7 22.4 %collective-permute-done.42 = bf16[1536,128]{1,0:T(8,128)(2,1)S(1)} collective-permute-done((bf16[1536,128]{1,0:T(8,128)(2,1)S(1)}, bf16[1536,128]{1,0:T(8,128)(2,1)S(1)}, u32[]{:S(2)}, u32[]{:S(2)}) %collective-permute-start.42) | collective-permute-done | bytes 393248 | tf_op jit(solution)/shard_map/ppermute | solution.py:323
  334.3 7.2 %attention_backward.6 = (f32[1536,256]{1,0:T(8,128)S(1)}, bf16[1536,128]{1,0:T(8,128)(2,1)S(1)}, bf16[1536,128]{1,0:T(8,128)(2,1)S(1)}) custom-call(bf16[1536,128]{1,0:T(8,128)(2,1)S(1)} %copy-done.31, bf16[1536,128]{1,0:T(8,128)(2,1)S(1)} %get-tuple-element.109.refs_1_, f32[8,1536]{1,0:T(8,128)S(1)} %copy-done.71, ...), custom_call_target="tpu_custom_call", output_to_operand_aliasing={{0}: (8, {})} | custom-call | flops 12079595520 | bytes 4718592 | tf_op jit(solution)/shard_map/attention_backward/pallas_call | solution.py:536
  341.5 7.7 %attention_backward.7 = (f32[1536,256]{1,0:T(8,128)S(1)}, bf16[1536,128]{1,0:T(8,128)(2,1)S(1)}, bf16[1536,128]{1,0:T(8,128)(2,1)S(1)}) custom-call(bf16[1536,128]{1,0:T(8,128)(2,1)S(1)} %copy-done.31, bf16[1536,128]{1,0:T(8,128)(2,1)S(1)} %get-tuple-element.109.refs_1_, f32[8,1536]{1,0:T(8,128)S(1)} %copy-done.71, ...), custom_call_target="tpu_custom_call", output_to_operand_aliasing={{0}: (8, {})} | custom-call | flops 12079595520 | bytes 4718592 | tf_op jit(solution)/shard_map/attention_backward/pallas_call | solution.py:536
  356.3 5.2 %collective-permute-done.45.refs_8_ = bf16[1536,128]{1,0:T(8,128)(2,1)S(1)} collective-permute-done((bf16[1536,128]{1,0:T(8,128)(2,1)S(1)}, bf16[1536,128]{1,0:T(8,128)(2,1)S(1)}, u32[]{:S(2)}, u32[]{:S(2)}) %collective-permute-start.45) | collective-permute-done | bytes 393248 | tf_op jit(solution)/shard_map/ppermute | solution.py:323
  362.9 6.5 %collective-permute-done.43.refs_5_ = bf16[1536,128]{1,0:T(8,128)(2,1)S(1)} collective-permute-done((bf16[1536,128]{1,0:T(8,128)(2,1)S(1)}, bf16[1536,128]{1,0:T(8,128)(2,1)S(1)}, u32[]{:S(2)}, u32[]{:S(2)}) %collective-permute-start.43) | collective-permute-done | bytes 393248 | tf_op jit(solution)/shard_map/ppermute | solution.py:323
  375.0 6.1 %collective-permute-done.47 = bf16[2,2,2,2,32,256]{5,4,3,2,1,0:T(8,128)(2,1)S(1)} collective-permute-done((bf16[2,2,2,2,32,256]{5,4,3,2,1,0:T(8,128)(2,1)S(1)}, bf16[2,2,2,2,32,256]{5,4,3,2,1,0:T(8,128)(2,1)S(1)}, u32[]{:S(2)}, u32[]{:S(2)}) %collective-permute-start.47) | collective-permute-done | bytes 262176 | tf_op jit(solution)/shard_map/ppermute | solution.py:323
  396.1 3.9 all-to-all-done.5
  409.2 5.5 %collective-permute-done.57 = bf16[32,1024]{1,0:T(8,128)(2,1)S(1)} collective-permute-done((bf16[32,1024]{1,0:T(8,128)(2,1)S(1)}, bf16[32,1024]{1,0:T(8,128)(2,1)S(1)}, u32[]{:S(2)}, u32[]{:S(2)}) %collective-permute-start.57) | collective-permute-done | bytes 65568 | tf_op jit(solution)/shard_map/ppermute | solution.py:323
  417.5 7.6 %all-to-all-done.4.arrived_ref = bf16[8,192,256]{2,1,0:T(8,128)(2,1)S(1)} async-done(((bf16[8,192,256]{2,1,0:T(8,128)(2,1)}), bf16[8,192,256]{2,1,0:T(8,128)(2,1)S(1)}, u32[]{:S(2)}, u32[]{:S(2)}) %all-to-all-start.4) | async-done | bytes 786464 | tf_op jit(solution)/shard_map/all_to_all | solution.py:876
  (412 shorter events, 167.2 us)
Async XLA Ops:
  7.2 166.4 %all-gather.4.cloned.1.call-start = ((), (), s32[]{:S(2)}) async-start(), calls=%async_computation.8 | async-start | bytes 2162688 | tf_op jit(solution)/shard_map/all_gather | solution.py:704
  7.9 198.0 %all-gather.6.cloned.1.call-start = ((), (), s32[]{:S(2)}) async-start(), calls=%async_computation.9 | async-start | bytes 2621440 | tf_op jit(solution)/shard_map/all_gather | solution.py:705
  10.9 34.2 %collective-permute-start.1 = (bf16[192,1024]{1,0:T(8,128)(2,1)}, bf16[192,1024]{1,0:T(8,128)(2,1)}, u32[]{:S(2)}, u32[]{:S(2)}) collective-permute-start(bf16[192,1024]{1,0:T(8,128)(2,1)} %half_ref.3), channel_id=1, source_target_pairs={{0,4},{1,5},{2,6},{3,7},{4,0},{5,1},{6,2},{7,3},{8,12},{9,13},{10,... | collective-permute-start | bytes 1179656 | tf_op jit(solution)/shard_map/ppermute | solution.py:323
  15.0 33.4 %collective-permute-start = (bf16[192,1024]{1,0:T(8,128)(2,1)}, bf16[192,1024]{1,0:T(8,128)(2,1)}, u32[]{:S(2)}, u32[]{:S(2)}) collective-permute-start(bf16[192,1024]{1,0:T(8,128)(2,1)} %half_ref.3), channel_id=1, source_target_pairs={{0,1},{1,0},{2,3},{3,2},{4,5},{5,4},{6,7},{7,6},{8,9},{9,8},{10,11... | collective-permute-start | bytes 1179656 | tf_op jit(solution)/shard_map/ppermute | solution.py:323
  16.5 52.2 %collective-permute-start.3 = (bf16[192,1024]{1,0:T(8,128)(2,1)}, bf16[192,1024]{1,0:T(8,128)(2,1)}, u32[]{:S(2)}, u32[]{:S(2)}) collective-permute-start(bf16[192,1024]{1,0:T(8,128)(2,1)} %half_ref.3), channel_id=1, source_target_pairs={{0,8},{1,9},{2,10},{3,11},{4,12},{5,13},{6,14},{7,15},{8,0},{9,1},... | collective-permute-start | bytes 1179656 | tf_op jit(solution)/shard_map/ppermute | solution.py:323
  17.8 38.8 %all-to-all-start = ((f32[32,1,128]{2,1,0:T(1,128)}), f32[32,1,128]{2,1,0:T(1,128)S(1)}, u32[]{:S(2)}, u32[]{:S(2)}) async-start(f32[32,1,128]{2,1,0:T(1,128)} %broadcast_in_dim.28), calls=%async_computation | async-start | bytes 32768 | tf_op jit(solution)/shard_map/all_to_all | solution.py:692
  20.9 396.6 %all-gather.8.cloned.1.call-start = ((), (), s32[]{:S(2)}) async-start(), calls=%async_computation.10 | async-start | bytes 4325376 | tf_op jit(solution)/shard_map/all_gather | solution.py:708
  56.7 23.8 %collective-permute-start.6 = (bf16[192,1024]{1,0:T(8,128)(2,1)}, bf16[192,1024]{1,0:T(8,128)(2,1)}, u32[]{:S(2)}, u32[]{:S(2)}) collective-permute-start(bf16[192,1024]{1,0:T(8,128)(2,1)} %collective-permute-done.2.refs_3_), channel_id=1, source_target_pairs={{0,8},{1,9},{2,10},{3,11},{4,12},{5,13},{6,14},{7,15},{8,0},{9,1},... | collective-permute-start | bytes 1179656 | tf_op jit(solution)/shard_map/ppermute | solution.py:323
  56.7 23.8 %all-to-all-start.1 = ((bf16[32,32,256]{2,1,0:T(8,128)(2,1)}), bf16[32,32,256]{2,1,0:T(8,128)(2,1)}, u32[]{:S(2)}, u32[]{:S(2)}) async-start(bf16[32,32,256]{2,1,0:T(8,128)(2,1)} %constant_dynamic-update-slice_fusion), calls=%async_computation.1 | async-start | bytes 1048576 | tf_op jit(solution)/shard_map/all_to_all | solution.py:701
  88.5 32.1 %collective-permute-start.12 = (bf16[1536,128]{1,0:T(8,128)(2,1)S(1)}, bf16[1536,128]{1,0:T(8,128)(2,1)S(1)}, u32[]{:S(2)}, u32[]{:S(2)}) collective-permute-start(bf16[1536,128]{1,0:T(8,128)(2,1)S(1)} %get-tuple-element.75.refs_4_.refs_6_), channel_id=1, source_target_pairs={{0,16},{1,17},{2,18},{3,19},{4,20},{5,21},{6,22},{7,23},{8,24},{9,... | collective-permute-start | bytes 1179656 | tf_op jit(solution)/shard_map/ppermute | solution.py:323
  89.6 30.7 %collective-permute-start.9 = (bf16[1536,128]{1,0:T(8,128)(2,1)S(1)}, bf16[1536,128]{1,0:T(8,128)(2,1)S(1)}, u32[]{:S(2)}, u32[]{:S(2)}) collective-permute-start(bf16[1536,128]{1,0:T(8,128)(2,1)S(1)} %get-tuple-element.75.refs_4_.refs_6_), channel_id=1, source_target_pairs={{0,2},{1,3},{2,0},{3,1},{4,6},{5,7},{6,4},{7,5},{8,10},{9,11},{10,... | collective-permute-start | bytes 1179656 | tf_op jit(solution)/shard_map/ppermute | solution.py:323
  89.8 30.8 %collective-permute-start.7 = (bf16[1536,128]{1,0:T(8,128)(2,1)S(1)}, bf16[1536,128]{1,0:T(8,128)(2,1)S(1)}, u32[]{:S(2)}, u32[]{:S(2)}) collective-permute-start(bf16[1536,128]{1,0:T(8,128)(2,1)S(1)} %get-tuple-element.74.refs_3_.refs_5_), channel_id=1, source_target_pairs={{0,16},{1,17},{2,18},{3,19},{4,20},{5,21},{6,22},{7,23},{8,24},{9,... | collective-permute-start | bytes 1179656 | tf_op jit(solution)/shard_map/ppermute | solution.py:323
  90.6 45.3 %collective-permute-start.11 = (bf16[1536,128]{1,0:T(8,128)(2,1)S(1)}, bf16[1536,128]{1,0:T(8,128)(2,1)S(1)}, u32[]{:S(2)}, u32[]{:S(2)}) collective-permute-start(bf16[1536,128]{1,0:T(8,128)(2,1)S(1)} %get-tuple-element.74.refs_3_.refs_5_), channel_id=1, source_target_pairs={{0,2},{1,3},{2,0},{3,1},{4,6},{5,7},{6,4},{7,5},{8,10},{9,11},{10,... | collective-permute-start | bytes 1179656 | tf_op jit(solution)/shard_map/ppermute | solution.py:323
  120.6 23.7 %collective-permute-start.8 = (bf16[1536,128]{1,0:T(8,128)(2,1)S(1)}, bf16[1536,128]{1,0:T(8,128)(2,1)S(1)}, u32[]{:S(2)}, u32[]{:S(2)}) collective-permute-start(bf16[1536,128]{1,0:T(8,128)(2,1)S(1)} %collective-permute-done.7.refs_3_.refs_5_), channel_id=1, source_target_pairs={{0,2},{1,3},{2,0},{3,1},{4,6},{5,7},{6,4},{7,5},{8,10},{9,11},{10,... | collective-permute-start | bytes 1179656 | tf_op jit(solution)/shard_map/ppermute | solution.py:323
  151.0 22.5 %all-to-all-start.2 = ((bf16[8,192,128]{2,1,0:T(8,128)(2,1)}), bf16[8,192,128]{2,1,0:T(8,128)(2,1)}, u32[]{:S(2)}, u32[]{:S(2)}) async-start(bf16[8,192,128]{2,1,0:T(8,128)(2,1)} %copy-done.20), calls=%async_computation.2 | async-start | bytes 786432 | tf_op jit(solution)/shard_map/all_to_all | solution.py:760
  158.5 23.9 %collective-permute-start.22 = (bf16[192,1024]{1,0:T(8,128)(2,1)S(1)}, bf16[192,1024]{1,0:T(8,128)(2,1)}, u32[]{:S(2)}, u32[]{:S(2)}) collective-permute-start(bf16[192,1024]{1,0:T(8,128)(2,1)S(1)} %copy-done.6), channel_id=1, source_target_pairs={{0,17},{1,16},{2,19},{3,18},{4,21},{5,20},{6,23},{7,22},{8,25},{9,... | collective-permute-start | bytes 1179656 | tf_op jit(solution)/shard_map/ppermute | solution.py:323
  158.7 24.2 %collective-permute-start.23 = (bf16[192,1024]{1,0:T(8,128)(2,1)S(1)}, bf16[192,1024]{1,0:T(8,128)(2,1)}, u32[]{:S(2)}, u32[]{:S(2)}) collective-permute-start(bf16[192,1024]{1,0:T(8,128)(2,1)S(1)} %copy-done.6), channel_id=1, source_target_pairs={{0,8},{1,9},{2,10},{3,11},{4,12},{5,13},{6,14},{7,15},{8,0},{9,1},... | collective-permute-start | bytes 1179656 | tf_op jit(solution)/shard_map/ppermute | solution.py:323
  182.9 22.2 %collective-permute-start.15 = (bf16[192,1024]{1,0:T(8,128)(2,1)}, bf16[192,1024]{1,0:T(8,128)(2,1)}, u32[]{:S(2)}, u32[]{:S(2)}) collective-permute-start(bf16[192,1024]{1,0:T(8,128)(2,1)} %get-tuple-element.78.refs_0_), channel_id=1, source_target_pairs={{0,17},{1,16},{2,19},{3,18},{4,21},{5,20},{6,23},{7,22},{8,25},{9,... | collective-permute-start | bytes 1179656 | tf_op jit(solution)/shard_map/ppermute | solution.py:323
  183.9 31.0 %collective-permute-start.16 = (bf16[192,1024]{1,0:T(8,128)(2,1)}, bf16[192,1024]{1,0:T(8,128)(2,1)}, u32[]{:S(2)}, u32[]{:S(2)}) collective-permute-start(bf16[192,1024]{1,0:T(8,128)(2,1)} %get-tuple-element.78.refs_0_), channel_id=1, source_target_pairs={{0,8},{1,9},{2,10},{3,11},{4,12},{5,13},{6,14},{7,15},{8,0},{9,1},... | collective-permute-start | bytes 1179656 | tf_op jit(solution)/shard_map/ppermute | solution.py:323
  192.8 22.1 %collective-permute-start.17 = (bf16[192,1024]{1,0:T(8,128)(2,1)}, bf16[192,1024]{1,0:T(8,128)(2,1)}, u32[]{:S(2)}, u32[]{:S(2)}) collective-permute-start(bf16[192,1024]{1,0:T(8,128)(2,1)} %collective-permute-done.13.refs_1_), channel_id=1, source_target_pairs={{0,8},{1,9},{2,10},{3,11},{4,12},{5,13},{6,14},{7,15},{8,0},{9,1},... | collective-permute-start | bytes 1179656 | tf_op jit(solution)/shard_map/ppermute | solution.py:323
  251.7 23.8 %all-to-all-start.3 = ((bf16[8,192,128]{2,1,0:T(8,128)(2,1)}), bf16[8,192,128]{2,1,0:T(8,128)(2,1)}, u32[]{:S(2)}, u32[]{:S(2)}) async-start(bf16[8,192,128]{2,1,0:T(8,128)(2,1)} %copy-done.19), calls=%async_computation.3 | async-start | bytes 786432 | tf_op jit(solution)/shard_map/all_to_all | solution.py:803
  255.8 174.0 %reduce-scatter.2.cloned.1.call-start = ((), (), s32[]{:S(2)}) async-start(), calls=%async_computation.11 | async-start | bytes 2621440 | tf_op jit(solution)/shard_map/reduce_scatter | solution.py:846
  275.5 75.7 %collective-permute-start.49 = (bf16[192,1024]{1,0:T(8,128)(2,1)}, bf16[192,1024]{1,0:T(8,128)(2,1)}, u32[]{:S(2)}, u32[]{:S(2)}) collective-permute-start(bf16[192,1024]{1,0:T(8,128)(2,1)} %get-tuple-element.129), channel_id=1, source_target_pairs={{0,1},{1,0},{2,3},{3,2},{4,5},{5,4},{6,7},{7,6},{8,9},{9,8},{10,11... | collective-permute-start | bytes 1179656 | tf_op jit(solution)/shard_map/ppermute | solution.py:323
  277.4 77.1 %collective-permute-start.50 = (bf16[192,1024]{1,0:T(8,128)(2,1)}, bf16[192,1024]{1,0:T(8,128)(2,1)}, u32[]{:S(2)}, u32[]{:S(2)}) collective-permute-start(bf16[192,1024]{1,0:T(8,128)(2,1)} %get-tuple-element.129), channel_id=1, source_target_pairs={{0,4},{1,5},{2,6},{3,7},{4,0},{5,1},{6,2},{7,3},{8,12},{9,13},{10,... | collective-permute-start | bytes 1179656 | tf_op jit(solution)/shard_map/ppermute | solution.py:323
  282.5 106.5 %all-to-all-start.6 = ((f32[32,1,128]{2,1,0:T(1,128)}), f32[32,1,128]{2,1,0:T(1,128)S(1)}, u32[]{:S(2)}, u32[]{:S(2)}) async-start(f32[32,1,128]{2,1,0:T(1,128)} %pad.4), calls=%async_computation.6 | async-start | bytes 32768 | tf_op jit(solution)/shard_map/all_to_all | solution.py:851
  302.3 31.8 %collective-permute-start.42 = (bf16[1536,128]{1,0:T(8,128)(2,1)S(1)}, bf16[1536,128]{1,0:T(8,128)(2,1)S(1)}, u32[]{:S(2)}, u32[]{:S(2)}) collective-permute-start(bf16[1536,128]{1,0:T(8,128)(2,1)S(1)} %get-tuple-element.115), channel_id=1, source_target_pairs={{0,2},{1,3},{2,0},{3,1},{4,6},{5,7},{6,4},{7,5},{8,10},{9,11},{10,... | collective-permute-start | bytes 1179656 | tf_op jit(solution)/shard_map/ppermute | solution.py:323
  311.0 44.6 %collective-permute-start.46 = (bf16[1536,128]{1,0:T(8,128)(2,1)S(1)}, bf16[1536,128]{1,0:T(8,128)(2,1)S(1)}, u32[]{:S(2)}, u32[]{:S(2)}) collective-permute-start(bf16[1536,128]{1,0:T(8,128)(2,1)S(1)} %get-tuple-element.124), channel_id=1, source_target_pairs={{0,2},{1,3},{2,0},{3,1},{4,6},{5,7},{6,4},{7,5},{8,10},{9,11},{10,... | collective-permute-start | bytes 1179656 | tf_op jit(solution)/shard_map/ppermute | solution.py:323
  311.7 37.8 %collective-permute-start.35 = (bf16[192,1024]{1,0:T(8,128)(2,1)S(1)}, bf16[192,1024]{1,0:T(8,128)(2,1)S(1)}, u32[]{:S(2)}, u32[]{:S(2)}) collective-permute-start(bf16[192,1024]{1,0:T(8,128)(2,1)S(1)} %copy-done.63), channel_id=1, source_target_pairs={{0,8},{1,9},{2,10},{3,11},{4,12},{5,13},{6,14},{7,15},{8,0},{9,1},... | collective-permute-start | bytes 1179656 | tf_op jit(solution)/shard_map/ppermute | solution.py:323
  355.7 49.1 %collective-permute-start.34 = (bf16[192,1024]{1,0:T(8,128)(2,1)S(1)}, bf16[192,1024]{1,0:T(8,128)(2,1)}, u32[]{:S(2)}, u32[]{:S(2)}) collective-permute-start(bf16[192,1024]{1,0:T(8,128)(2,1)S(1)} %copy-done.55), channel_id=1, source_target_pairs={{0,8},{1,9},{2,10},{3,11},{4,12},{5,13},{6,14},{7,15},{8,0},{9,1},... | collective-permute-start | bytes 1179656 | tf_op jit(solution)/shard_map/ppermute | solution.py:323
  373.9 31.0 %collective-permute-start.36 = (bf16[192,1024]{1,0:T(8,128)(2,1)}, bf16[192,1024]{1,0:T(8,128)(2,1)}, u32[]{:S(2)}, u32[]{:S(2)}) collective-permute-start(bf16[192,1024]{1,0:T(8,128)(2,1)} %add_convert_fusion.5), channel_id=1, source_target_pairs={{0,1},{1,0},{2,3},{3,2},{4,5},{5,4},{6,7},{7,6},{8,9},{9,8},{10,11... | collective-permute-start | bytes 1179656 | tf_op jit(solution)/shard_map/ppermute | solution.py:323
  381.1 23.7 %collective-permute-start.38 = (bf16[192,1024]{1,0:T(8,128)(2,1)}, bf16[192,1024]{1,0:T(8,128)(2,1)}, u32[]{:S(2)}, u32[]{:S(2)}) collective-permute-start(bf16[192,1024]{1,0:T(8,128)(2,1)} %add_convert_fusion.4), channel_id=1, source_target_pairs={{0,16},{1,17},{2,18},{3,19},{4,20},{5,21},{6,22},{7,23},{8,24},{9,... | collective-permute-start | bytes 1179656 | tf_op jit(solution)/shard_map/ppermute | solution.py:323
  400.1 25.0 %all-to-all-start.4 = ((bf16[8,192,256]{2,1,0:T(8,128)(2,1)}), bf16[8,192,256]{2,1,0:T(8,128)(2,1)S(1)}, u32[]{:S(2)}, u32[]{:S(2)}) async-start(bf16[8,192,256]{2,1,0:T(8,128)(2,1)} %get-tuple-element.125), calls=%async_computation.4 | async-start | bytes 1572864 | tf_op jit(solution)/shard_map/all_to_all | solution.py:876
  (118 other events, 1334.1 us)
Sparse Core Ops, SparseCore 0:
  11.0 60.9 all-gather.3
  74.1 68.1 all-gather.5
  145.3 72.8 all-gather.7
  275.6 64.8 reduce-scatter.1

commit v2 on v1

--- a/solution.py
+++ b/solution.py
@@ -304,14 +304,15 @@
 
 BITS = ("y", "core", "z_hi", "z_lo", "x")
 Y, CORE, Z_HI, Z_LO, X = 16, 8, 4, 2, 1
-HEAD_AXES = ("core", "z_hi", "x")
+HEAD_AXES = ("z_hi", "z_lo", "x")
+PARTS = (0, CORE, Y, Y | CORE)
 LOG2E = 1.4426950408889634
 HIGH_BITS = -2139062144
 NT = (((1,), (1,)), ((), ()))
 NN = (((1,), (0,)), ((), ()))
 TN = (((0,), (0,)), ((), ()))
 F32, BF16, I32 = jnp.float32, jnp.bfloat16, jnp.int32
-VMEM = pl.BlockSpec(memory_space=pltpu.VMEM)
+LONG = pl.CostEstimate(flops=10**11, bytes_accessed=1, transcendentals=0)
 SMEM = pl.BlockSpec(memory_space=pltpu.SMEM)
 
 
@@ -331,31 +332,73 @@
     return jax.ShapeDtypeStruct(shape, dtype)
 
 
-def call(kernel, inputs, out_shape, name, flops, mib=40, specs=None):
-    flat = jax.tree.leaves(out_shape)
-    moved = sum(a.size * a.dtype.itemsize for a in [*inputs, *flat])
+class Far:
+    def __init__(self, value):
+        self.value = value
+
+
+def call(kernel, inputs, out_shape, name, far_out=(), mib=56, scalars=(), scratch=(), cost=LONG):
+    far_in = [i for i, a in enumerate(inputs) if isinstance(a, Far)]
+    arrays = [a.value if isinstance(a, Far) else a for a in inputs]
+    first_in, first_out = len(scalars), len(scalars) + len(arrays)
+    first_scratch = first_out + len(out_shape)
+    staged = [arrays[i] for i in far_in] + [out_shape[i] for i in far_out]
+
+    def body(*refs):
+        refs, sems = list(refs[:-1]), refs[-1]
+        own = refs[first_scratch : first_scratch + len(scratch)]
+        stages = refs[first_scratch + len(scratch) :]
+        copies = []
+        for k, i in enumerate(far_in):
+            copies.append(pltpu.make_async_copy(refs[first_in + i], stages[k], sems.at[k]))
+            refs[first_in + i] = stages[k]
+        for copy in copies:
+            copy.start()
+        for copy in copies:
+            copy.wait()
+        copies = []
+        for k, i in enumerate(far_out, len(far_in)):
+            copies.append(pltpu.make_async_copy(stages[k], refs[first_out + i], sems.at[k]))
+            refs[first_out + i] = stages[k]
+        kernel(*refs[:first_scratch], *own)
+        for copy in copies:
+            copy.start()
+        for copy in copies:
+            copy.wait()
+
+    near, far = pl.BlockSpec(memory_space=pltpu.VMEM), pl.BlockSpec(memory_space=pl.ANY)
     return pl.pallas_call(
-        kernel,
-        in_specs=specs or [VMEM] * len(inputs),
-        out_specs=jax.tree.map(lambda _: VMEM, out_shape),
+        body,
+        in_specs=[SMEM] * len(scalars) + [far if i in far_in else near for i in range(len(arrays))],
+        out_specs=[far if i in far_out else near for i in range(len(out_shape))],
         out_shape=out_shape,
+        scratch_shapes=[
+            *scratch,
+            *(pltpu.VMEM(a.shape, a.dtype) for a in staged),
+            pltpu.SemaphoreType.DMA((max(len(staged), 1),)),
+        ],
         compiler_params=pltpu.CompilerParams(vmem_limit_bytes=mib * 2**20),
-        cost_estimate=pl.CostEstimate(flops=flops, bytes_accessed=moved, transcendentals=0),
+        cost_estimate=cost,
         name=name,
-    )(*inputs)
+    )(*scalars, *arrays)
 
 
 def with_cores(near):
     return near + [swap(part, CORE) for part in near]
 
 
+def near_xy(value):
+    return [value, swap(value, X), swap(value, Y), swap(value, X | Y)]
+
+
 def gather_xy(value):
-    return with_cores([value, swap(value, X), swap(value, Y), swap(value, X | Y)])
-
-
-def gather_xz(value):
-    over_z = swap(value, Z_HI)
-    return with_cores([value, swap(value, X), over_z, swap(over_z, X)])
+    return with_cores(near_xy(value))
+
+
+def gather_zx(value):
+    low, high = swap(value, Z_LO), swap(value, Z_HI)
+    line = [value, low, high, swap(high, Z_LO)]
+    return [block for part in line for block in (part, swap(part, X))]
 
 
 def scatter_xy(blocks):
@@ -368,6 +411,25 @@
     return [blocks[0], arrived[0], *sent]
 
 
+def scatter_by_x(blocks):
+    arrived = [swap(block, CORE) for block in blocks[4:]]
+    own, one, two, both = (
+        near.astype(F32) + far.astype(F32) for near, far in zip(blocks[:4], arrived, strict=True)
+    )
+    own = own + swap(one.astype(BF16), X).astype(F32)
+    two = two + swap(both.astype(BF16), X).astype(F32)
+    return own + swap(two.astype(BF16), Y).astype(F32)
+
+
+def shares(value):
+    over_y = swap(value, Y)
+    return [value, swap(value, CORE), over_y, swap(over_y, CORE)]
+
+
+def sum_shares(blocks):
+    return [blocks[0]] + [swap(b, mask) for b, mask in zip(blocks[1:], PARTS[1:], strict=True)]
+
+
 def normalised(values):
     centred = values - jnp.mean(values, axis=-1, keepdims=True)
     rstd = lax.rsqrt(jnp.mean(centred * centred, axis=-1, keepdims=True) + 1e-05)
@@ -389,10 +451,44 @@
         row_ref[:, chunk] = square.T[0:8, :]
 
 
-def project_kernel(*refs):
-    blocks, (gain_ref, weight_ref), outs = refs[:8], refs[8:10], refs[10:]
-    normed_ref, q_ref, k_ref, v_ref, norm_ref, row_ref = outs
-    weight = weight_ref[...]
+def pack_kernel(*refs):
+    qk_ref, value_ref, out_ref, up_ref, down_ref, gain_ref, columns_ref, z_ref, qv_ref = refs
+    rows, width = qk_ref.shape
+    units = down_ref.shape[0]
+    for h in range(NH):
+        lanes = slice(h * DH, (h + 1) * DH)
+        columns_ref[h, :, :DH] = qk_ref[:, lanes]
+        columns_ref[h, :, DH : 2 * DH] = value_ref[:, lanes]
+        columns_ref[h, :, 2 * DH :] = gain_ref[...]
+    z_ref[:units, :width] = up_ref[...].astype(F32).T.astype(BF16)
+    z_ref[:units, width:] = down_ref[...]
+    z_ref[units:, :width] = out_ref[: rows // 2, :]
+    z_ref[units:, width:] = out_ref[rows // 2 :, :]
+    qv_ref[:, :width] = qk_ref[...]
+    qv_ref[:, width:] = value_ref[...]
+
+
+def column_kernel(row_ref, column_ref):
+    for i in range(row_ref.shape[1] // 128):
+        chunk = slice(i * 128, (i + 1) * 128)
+        square = jnp.broadcast_to(row_ref[0:1, chunk], (128, 128))
+        column_ref[chunk, :] = square.T[:, 0:1]
+
+
+def project_kernel(place_ref, *refs):
+    blocks, parts, outs = refs[:8], refs[8:12], refs[12:18]
+    weight_ref = refs[18]
+    normed_ref, q_ref, kv_ref, norm_ref, row_ref, gain_ref = outs
+    me = place_ref[0]
+    rows = parts[0].shape[1]
+    for part, mask in zip(parts, PARTS, strict=True):
+        for s in range(NH):
+            owner = ((me ^ mask) & (Y | CORE)) | s
+            weight_ref[pl.ds(pl.multiple_of(owner * rows, rows), rows), :] = part[s]
+    for i in range(weight_ref.shape[0] // 128):
+        chunk = slice(i * 128, (i + 1) * 128)
+        gain_ref[:, chunk] = weight_ref[chunk, 2 * DH :].astype(F32).T[0:8, :]
+    weight = weight_ref[:, : 2 * DH]
     gain = gain_ref[0:1, :]
     for i, block in enumerate(blocks):
         rows = pl.ds(i * block.shape[0], block.shape[0])
@@ -401,10 +497,10 @@
         both = dot(normed, weight)
         queries = both[:, :DH].astype(BF16)
         q_ref[rows, :] = queries
-        v_ref[rows, :] = both[:, DH:].astype(BF16)
         query_f = queries.astype(F32)
         squares = jnp.sum(query_f * query_f, axis=-1, keepdims=True)
-        k_ref[rows, :] = (query_f * lax.rsqrt(squares / DH + 1e-06) * DH ** (-0.5)).astype(BF16)
+        keys = (query_f * lax.rsqrt(squares / DH + 1e-06) * DH ** (-0.5)).astype(BF16)
+        kv_ref[rows, :] = jnp.concatenate([keys, both[:, DH:].astype(BF16)], axis=1)
         norm_ref[rows, :] = jnp.sqrt(squares + 1e-06) * LOG2E
     to_row(norm_ref, row_ref)
 
@@ -421,155 +517,184 @@
     return counts.astype(F32)
 
 
-def forward_kernel(*refs, tile, own, first, last):
-    q_ref, n_ref, qid_ref, k_ref, v_ref, kid_ref = refs[:6]
-    acc_in = None if first else refs[6]
-    head_ref = refs[6 + (not first)] if last else None
+def forward_kernel(*refs, tile, own, last):
+    q_ref, n_ref, qid_ref, kid_ref = refs[:4]
+    kv_refs = refs[4:6]
+    acc_in = None if own else refs[6]
+    place_ref = refs[6 + (not own)] if last else None
     acc_ref = refs[-2] if last else refs[-1]
     step = pl.program_id(0)
+    steps = pl.num_programs(0) // 2
 
     @pl.when(step == 0)
     def _():
-        acc_ref[...] = jnp.zeros_like(acc_ref) if first else acc_in[...]
-
-    keys = k_ref[...]
-    count = keys.shape[0]
-    values = jnp.concatenate([v_ref[...], jnp.ones((count, DH), BF16)], axis=1)
-    for i in range(q_ref.shape[0] // tile):
-        rows = slice(i * tile, (i + 1) * tile)
-        scores = dot(q_ref[rows, :], keys, NT)
-        powers = jnp.exp2(scores * LOG2E - n_ref[rows, :])
-        diagonal = step * count - i * tile if own else None
-        counts = pair_count(qid_ref[rows, :], kid_ref[0:1, :], kid_ref[2:3, :], diagonal)
-        acc_ref[rows, :] += dot((powers * counts).astype(BF16), values)
+        acc_ref[...] = jnp.zeros_like(acc_ref) if own else acc_in[...]
+
+    def part(kv_ref, diagonal_at):
+        count = kv_ref.shape[0]
+        keys = kv_ref[:, :DH]
+        values = jnp.concatenate([kv_ref[:, DH:], jnp.ones((count, DH), BF16)], axis=1)
+        for i in range(q_ref.shape[0] // tile):
+            rows = slice(i * tile, (i + 1) * tile)
+            scores = dot(q_ref[rows, :], keys, NT)
+            powers = jnp.exp2(scores * LOG2E - n_ref[rows, :])
+            diagonal = None if diagonal_at is None else diagonal_at * count - i * tile
+            counts = pair_count(qid_ref[rows, :], kid_ref[0:1, :], kid_ref[2:3, :], diagonal)
+            acc_ref[rows, :] += dot((powers * counts).astype(BF16), values)
+
+    @pl.when(step < steps)
+    def _():
+        part(kv_refs[0], step if own else None)
+
+    @pl.when(step >= steps)
+    def _():
+        part(kv_refs[1], None)
 
     if last:
         send_ref = refs[-1]
         rows = send_ref.shape[1]
 
-        @pl.when(step == pl.num_programs(0) - 1)
+        @pl.when(step == 2 * steps - 1)
         def _():
             for j in range(NH):
                 block = acc_ref[j * rows : (j + 1) * rows, :]
-                send_ref[head_ref[0] ^ j] = (block[:, :DH] / block[:, DH:]).astype(BF16)
-
-
-def forward_call(queries, norms, ids, keys, values, part, acc, head=None, tk=768, tile=256):
-    nq, nk = queries.shape[0], keys.shape[0]
+                send_ref[place_ref[1] ^ j] = (block[:, :DH] / block[:, DH:]).astype(BF16)
+
+
+def forward_call(queries, norms, ids, kv_pair, part, acc, place=None, tk=768, tile=256):
+    nq, nk = queries.shape[0], kv_pair[0].shape[0]
     steps = nk // tk
     column = pl.BlockSpec((nq, 1), lambda j: (0, 0))
     full = pl.BlockSpec((nq, DH), lambda j: (0, 0))
-    keyed = pl.BlockSpec((tk, DH), lambda j: (j, 0))
+    first = pl.BlockSpec((tk, 2 * DH), lambda j: (jnp.minimum(j, steps - 1), 0))
+    second = pl.BlockSpec((tk, 2 * DH), lambda j: (jnp.maximum(j - steps, 0), 0))
     wide = pl.BlockSpec((nq, 2 * DH), lambda j: (0, 0))
     listed = pl.BlockSpec((8, tk), lambda j: (0, part * steps + j))
-    inputs = [queries, norms, ids[0], keys, values, ids[1]]
-    specs = [full, column, column, keyed, keyed, listed]
+    inputs = [queries, norms, ids[0], ids[1], *kv_pair]
+    specs = [full, column, column, listed, first, second]
     out_shape, out_specs = [shaped(nq, 2 * DH, dtype=F32)], [wide]
     if acc is not None:
         inputs.append(acc)
         specs.append(wide)
-    if head is not None:
-        inputs.append(head)
+    if place is not None:
+        inputs.append(place)
         specs.append(SMEM)
         out_shape.append(shaped(NH, nq // NH, DH))
         out_specs.append(pl.BlockSpec((NH, nq // NH, DH), lambda j: (0, 0, 0)))
     return pl.pallas_call(
-        functools.partial(
-            forward_kernel,
-            tile=tile,
-            own=part == 0,
-            first=acc is None,
-            last=head is not None,
-        ),
-        grid=(steps,),
+        functools.partial(forward_kernel, tile=tile, own=acc is None, last=place is not None),
+        grid=(2 * steps,),
         in_specs=specs,
         out_specs=out_specs,
         out_shape=out_shape,
         input_output_aliases={} if acc is None else {6: 0},
-        compiler_params=pltpu.CompilerParams(vmem_limit_bytes=40 * 2**20),
-        cost_estimate=pl.CostEstimate(
-            flops=32 * nq * nk * DH, bytes_accessed=2 * nq * nk, transcendentals=nq * nk
-        ),
+        compiler_params=pltpu.CompilerParams(vmem_limit_bytes=56 * 2**20),
         name="attention_forward",
     )(*inputs)
 
 
-def backward_kernel(*refs, tile, own, first):
-    q_ref, g_ref, n_ref, t_ref, qid_ref, k_ref, v_ref, kid_ref = refs[:8]
-    dq_ref, dk_ref, dv_ref = refs[-3:]
+def backward_kernel(*refs, tile, own):
+    q_ref, g_ref, n_ref, t_ref, qid_ref, kid_ref = refs[:6]
+    kv_refs = refs[6:8]
+    dq_ref, *dkv_refs = refs[-3:]
     step = pl.program_id(0)
+    steps = pl.num_programs(0) // 2
 
     @pl.when(step == 0)
     def _():
-        dq_ref[...] = jnp.zeros_like(dq_ref) if first else refs[8][...]
-
-    keys, values, key_ids = k_ref[...], v_ref[...], kid_ref[...]
-    count = keys.shape[0]
-    wide_keys = jnp.concatenate([keys, jnp.ones(keys.shape, BF16)], axis=1)
-    grad_keys = jnp.zeros(keys.shape, F32)
-    grad_values = jnp.zeros(keys.shape, F32)
-    for i in range(q_ref.shape[0] // tile):
-        rows = slice(i * tile, (i + 1) * tile)
-        queries, grads = q_ref[rows, :], g_ref[rows, :]
-        scores = dot(keys, queries, NT)
-        powers = jnp.exp2(scores * LOG2E - n_ref[0:1, rows])
-        diagonal = i * tile - step * count if own else None
-        weights = powers * pair_count(key_ids, qid_ref[0:1, rows], qid_ref[1:2, rows], diagonal)
-        grad_weights = dot(values, grads, NT)
-        grad_scores = (weights * (grad_weights + t_ref[0:1, rows])).astype(BF16)
-        grad_values = grad_values + dot(weights.astype(BF16), grads)
-        grad_keys = grad_keys + dot(grad_scores, queries)
-        dq_ref[rows, :] += dot(grad_scores, wide_keys, TN)
-    dk_ref[...] = grad_keys.astype(BF16)
-    dv_ref[...] = grad_values.astype(BF16)
-
-
-def backward_call(queries, grads, norms, terms, ids, keys, values, part, acc, tk=768, tile=256):
-    nq, nk = queries.shape[0], keys.shape[0]
+        dq_ref[...] = refs[8][...] if own else jnp.zeros_like(dq_ref)
+
+    def part(kv_ref, dkv_ref, diagonal_at):
+        keys, values, key_ids = kv_ref[:, :DH], kv_ref[:, DH:], kid_ref[...]
+        count = keys.shape[0]
+        wide_keys = jnp.concatenate([keys, jnp.ones(keys.shape, BF16)], axis=1)
+        grad_keys = jnp.zeros(keys.shape, F32)
+        grad_values = jnp.zeros(keys.shape, F32)
+        for i in range(q_ref.shape[0] // tile):
+            rows = slice(i * tile, (i + 1) * tile)
+            queries, grads = q_ref[rows, :], g_ref[rows, :]
+            scores = dot(keys, queries, NT)
+            powers = jnp.exp2(scores * LOG2E - n_ref[0:1, rows])
+            diagonal = None if diagonal_at is None else i * tile - diagonal_at * count
+            counts = pair_count(key_ids, qid_ref[0:1, rows], qid_ref[1:2, rows], diagonal)
+            weights = powers * counts
+            grad_weights = dot(values, grads, NT)
+            grad_scores = (weights * (grad_weights + t_ref[0:1, rows])).astype(BF16)
+            grad_values = grad_values + dot(weights.astype(BF16), grads)
+            grad_keys = grad_keys + dot(grad_scores, queries)
+            dq_ref[rows, :] += dot(grad_scores, wide_keys, TN)
+        dkv_ref[...] = jnp.concatenate([grad_keys, grad_values], axis=1).astype(BF16)
+
+    @pl.when(step < steps)
+    def _():
+        part(kv_refs[0], dkv_refs[0], step if own else None)
+
+    @pl.when(step >= steps)
+    def _():
+        part(kv_refs[1], dkv_refs[1], None)
+
+
+def backward_call(queries, grads, norms, terms, ids, kv_pair, part, acc, tk=768, tile=256):
+    nq, nk = queries.shape[0], kv_pair[0].shape[0]
     steps = nk // tk
     full = pl.BlockSpec((nq, DH), lambda j: (0, 0))
     row = pl.BlockSpec((8, nq), lambda j: (0, 0))
-    keyed = pl.BlockSpec((tk, DH), lambda j: (j, 0))
+    first = pl.BlockSpec((tk, 2 * DH), lambda j: (jnp.minimum(j, steps - 1), 0))
+    second = pl.BlockSpec((tk, 2 * DH), lambda j: (jnp.maximum(j - steps, 0), 0))
     wide = pl.BlockSpec((nq, 2 * DH), lambda j: (0, 0))
     listed = pl.BlockSpec((tk, 1), lambda j: (part * steps + j, 0))
     more = [] if acc is None else [acc]
     return pl.pallas_call(
-        functools.partial(backward_kernel, tile=tile, own=part == 0, first=acc is None),
-        grid=(steps,),
-        in_specs=[full, full, row, row, row, keyed, keyed, listed] + [wide] * len(more),
-        out_specs=[wide, keyed, keyed],
-        out_shape=[shaped(nq, 2 * DH, dtype=F32), shaped(nk, DH), shaped(nk, DH)],
+        functools.partial(backward_kernel, tile=tile, own=acc is not None),
+        grid=(2 * steps,),
+        in_specs=[full, full, row, row, row, listed, first, second] + [wide] * len(more),
+        out_specs=[wide, first, second],
+        out_shape=[shaped(nq, 2 * DH, dtype=F32), *[shaped(nk, 2 * DH)] * 2],
         input_output_aliases={8: 0} if more else {},
-        compiler_params=pltpu.CompilerParams(vmem_limit_bytes=40 * 2**20),
-        cost_estimate=pl.CostEstimate(
-            flops=40 * nq * nk * DH, bytes_accessed=2 * nq * nk, transcendentals=nq * nk
-        ),
+        compiler_params=pltpu.CompilerParams(vmem_limit_bytes=56 * 2**20),
+        cost_estimate=LONG,
         name="attention_backward",
-    )(queries, grads, norms, terms, ids[1], keys, values, ids[0], *more)
-
-
-def out_kernel(attn_ref, half_ref, weight_ref, gain_ref, low_ref, out_ref, normed_ref):
+    )(queries, grads, norms, terms, ids[1], ids[0], *kv_pair, *more)
+
+
+def out_kernel(place_ref, attn_ref, half_ref, gain_ref, *refs):
+    parts, (low_ref, out_ref, normed_ref, weight_ref) = refs[:8], refs[8:]
+    rows, width = weight_ref.shape[0] // 32, weight_ref.shape[1]
+    masks = [core | near for core in (0, CORE) for near in (0, X, Y, X | Y)]
+    for part, mask in zip(parts, masks, strict=True):
+        for p in range(4):
+            start = pl.multiple_of((((place_ref[0] ^ mask) & (Y | CORE | X)) | (p * Z_LO)) * rows, rows)
+            weight_ref[pl.ds(start, rows // 2), :] = part[p, :, :width]
+            middle = pl.multiple_of(start + rows // 2, rows // 2)
+            weight_ref[pl.ds(middle, rows // 2), :] = part[p, :, width:]
     attn = jnp.concatenate([attn_ref[h] for h in range(NH)], axis=1)
     first_out = half_ref[...].astype(F32) + dot(attn, weight_ref[...])
     out_ref[...] = first_out
     low_ref[...] = first_out.astype(BF16)
-    normed_ref[...] = (normalised(first_out)[0] * gain_ref[0:1, :]).astype(BF16)
+    normed_ref[...] = (normalised(first_out)[0] * gain_ref[1:2, :]).astype(BF16)
+
+
+def ffn_part(z_ref, units, down):
+    width = z_ref.shape[2] // 2
+    lanes = slice(width, None) if down else slice(width)
+    return jnp.concatenate([z_ref[p, :units, lanes] for p in range(4)], axis=0)
 
 
 def hidden_back_kernel(*refs):
-    blocks, weight_ref, out_ref = refs[:8], refs[8], refs[9]
-    down = weight_ref[:, weight_ref.shape[1] // 2 :]
+    blocks, z_ref, out_ref = refs[:8], refs[8], refs[9]
+    down = ffn_part(z_ref, out_ref.shape[1] // 4, True)
     for i, block in enumerate(blocks):
         rows = pl.ds(i * block.shape[0], block.shape[0])
         out_ref[rows, :] = dot(block[...], down, NT)
 
 
 def ffn_kernel(*refs):
-    blocks, (back_ref, weight_ref), outs = refs[:8], refs[8:10], refs[10:]
+    blocks, back_ref, z_ref, outs = refs[:8], refs[8], refs[9], refs[10:]
     hidden_ref, grad_ref = outs[8:]
-    up = weight_ref[:, : weight_ref.shape[1] // 2]
+    up = ffn_part(z_ref, hidden_ref.shape[1] // 4, False)
     slope = 0.7978845608028654
-    for i, block in enumerate(blocks):
+    for i in (4, 5, 6, 7, 0, 1, 2, 3):
+        block = blocks[i]
         rows = pl.ds(i * block.shape[0], block.shape[0])
         v = dot(block[...], up, NT)
         square = v * v
@@ -583,14 +708,16 @@
 
 
 def ffn_rest_kernel(*refs):
-    blocks, grads = refs[:8], refs[8:16]
-    hidden_ref, grad_ref, weight_ref = refs[16:19]
-    outs, sum_ref = refs[19:27], refs[27]
-    width = weight_ref.shape[1] // 2
-    down = weight_ref[:, width:]
+    blocks, grads, z_ref = refs[:8], refs[8:16], refs[18]
+    hidden_ref, grad_ref = refs[16:18]
+    near_ref, far_ref, sum_ref = refs[19:]
+    width = sum_ref.shape[1] // 2
+    units = sum_ref.shape[0] // 4
+    down = ffn_part(z_ref, units, True)
     for i in range(8):
         rows = pl.ds(i * blocks[i].shape[0], blocks[i].shape[0])
-        outs[i][...] = dot(hidden_ref[rows, :], down).astype(BF16)
+        out = (near_ref, far_ref)[i // 4]
+        out[i % 4] = dot(hidden_ref[rows, :], down).astype(BF16)
     inputs = jnp.concatenate([block[...] for block in blocks], axis=0)
     sum_ref[:, :width] = dot(grad_ref[...], inputs, TN).astype(BF16)
     cotangents = jnp.concatenate([block[...] for block in grads], axis=0)
@@ -606,7 +733,7 @@
     gain_sum_ref[...] = jnp.broadcast_to(
         jnp.sum(grads * xhat, axis=0, keepdims=True), gain_sum_ref.shape
     )
-    mid = first_ref[...].astype(F32) + norm_back(grads * gain_ref[0:1, :], xhat, rstd)
+    mid = first_ref[...].astype(F32) + norm_back(grads * gain_ref[1:2, :], xhat, rstd)
     mid = mid.astype(BF16)
     mid_ref[...] = mid
     grad_attn = dot(mid, weight_ref[...], NT).astype(BF16)
@@ -614,15 +741,14 @@
         send_ref[h] = grad_attn[:, h * DH : (h + 1) * DH]
 
 
-def turn_kernel(arrived_ref, acc_ref, head_ref, grads_ref, row_ref, attn_ref, column_ref):
+def turn_kernel(place_ref, arrived_ref, acc_ref, grads_ref, row_ref, column_ref):
     rows = arrived_ref.shape[1]
     for j in range(NH):
         place = slice(j * rows, (j + 1) * rows)
         block = acc_ref[place, :]
         totals = block[:, DH:]
         attended = block[:, :DH] / totals
-        attn_ref[place, :] = attended.astype(BF16)
-        grad_attn = arrived_ref[head_ref[0] ^ j].astype(F32)
+        grad_attn = arrived_ref[place_ref[1] ^ j].astype(F32)
         grads_ref[place, :] = (grad_attn / totals).astype(BF16)
         column_ref[place, :] = (
             -jnp.sum(grad_attn * attended, axis=-1, keepdims=True) / totals[:, :1]
@@ -630,15 +756,41 @@
     to_row(column_ref, row_ref)
 
 
-def gather_grads_kernel(*refs):
-    direct_ref, q_ref, n_ref, head_ref = refs[:4]
-    key_refs, value_refs = refs[4:7], refs[7:10]
-    send_ref, both_ref = refs[10:]
+def grad_out_kernel(place_ref, attn_ref, mid_ref, gain_ref, keep_ref, send_ref):
+    width = mid_ref.shape[1]
+    heads = NH // 4
+    core = (place_ref[0] >> 3) & 1
+    gains = [
+        jnp.broadcast_to(gain_ref[0:1, h * DH : (h + 1) * DH], (DH, DH)).T for h in range(NH)
+    ]
+    for ref, bit in ((keep_ref, core), (send_ref, 1 - core)):
+        for i in range(NH // 2):
+            first, k = divmod(i, heads)
+            rows = slice(i * DH, (i + 1) * DH)
+            attn = attn_ref[(2 * first + bit) * heads + k]
+            ref[rows, :width] = dot(attn, mid_ref[...], TN).astype(BF16)
+            low, high = (gains[(2 * first + b) * heads + k] for b in range(2))
+            ref[rows, width:] = jnp.where(bit == 0, low, high).astype(BF16)
+
+
+def halve_kernel(place_ref, kept_ref, came_ref, keep_ref, send_ref, *, shift, blocks):
+    rows = kept_ref.shape[0] // (2 * blocks)
+    bit = (place_ref[0] >> shift) & 1
+    for i in range(blocks):
+        out = slice(i * rows, (i + 1) * rows)
+        for ref, half in ((keep_ref, bit), (send_ref, 1 - bit)):
+            start = pl.ds(pl.multiple_of((2 * i + half) * rows, rows), rows)
+            total = kept_ref[start, :].astype(F32) + came_ref[start, :].astype(F32)
+            ref[out, :] = total.astype(BF16)
+
+
+def gather_grads_kernel(place_ref, direct_ref, q_ref, n_ref, *refs):
+    kv_refs, (send_ref, both_ref) = refs[:3], refs[3:]
     rows = send_ref.shape[1]
     for j in range(NH):
         place = slice(j * rows, (j + 1) * rows)
-        grad_keys = sum(ref[place, :].astype(F32) for ref in key_refs)
-        grad_values = sum(ref[place, :].astype(F32) for ref in value_refs)
+        grad_kv = sum(ref[place, :].astype(F32) for ref in kv_refs)
+        grad_keys, grad_values = grad_kv[:, :DH], grad_kv[:, DH:]
         queries = q_ref[place, :].astype(F32)
         inverse = lax.rsqrt(jnp.mean(queries * queries, axis=-1, keepdims=True) + 1e-06)
         mean_part = jnp.mean(grad_keys * queries, axis=-1, keepdims=True)
@@ -650,7 +802,46 @@
         )
         both = jnp.concatenate([grad_queries.astype(BF16), grad_values.astype(BF16)], axis=1)
         both_ref[place, :] = both
-        send_ref[head_ref[0] ^ j] = both
+        send_ref[place_ref[1] ^ j] = both
+
+
+def project_back_kernel(place_ref, normed_ref, both_ref, *refs):
+    outs, sum_ref = refs[:4], refs[4]
+    sum_ref[...] = dot(normed_ref[...], both_ref[...], TN)
+    rows = outs[0].shape[1]
+    for out, mask in zip(outs, PARTS, strict=True):
+        for j in range(NH):
+            start = pl.multiple_of((place_ref[0] ^ mask ^ j) * rows, rows)
+            out[j] = sum_ref[pl.ds(start, rows), :].astype(BF16)
+
+
+def sum_kernel(place_ref, *refs):
+    parts, out = refs[:4], refs[4]
+    for j in range(NH):
+        out[place_ref[1] ^ j] = sum(part[j].astype(F32) for part in parts).astype(BF16)
+
+
+def own_rows_kernel(rows_ref, qk_ref, value_ref, gain_ref, *outs):
+    grad_qk_ref, grad_value_ref, grad_gain_ref = outs
+    for h in range(NH):
+        lanes = slice(h * DH, (h + 1) * DH)
+        grad_qk_ref[:, lanes] = rows_ref[h, :, :DH].astype(F32)
+        grad_value_ref[:, lanes] = rows_ref[h, :, DH:].astype(F32)
+    total = jnp.sum(
+        qk_ref[...].astype(F32) * grad_qk_ref[...]
+        + value_ref[...].astype(F32) * grad_value_ref[...],
+        axis=-1,
+        keepdims=True,
+    )
+    grad_gain_ref[...] = jnp.broadcast_to(
+        total / gain_ref[:, :1].astype(F32), grad_gain_ref.shape
+    )
+
+
+def unpack_kernel(sum_ref, up_ref, down_ref):
+    width = sum_ref.shape[1] // 2
+    up_ref[...] = sum_ref[:, :width].astype(F32).T
+    down_ref[...] = sum_ref[:, width:].astype(F32)
 
 
 def last_kernel(arrived_ref, half_ref, grad_ref, gain_ref, weight_ref, out_ref):
@@ -679,40 +870,40 @@
     stretch_ids,
 ):
     y, core, z_hi, z_lo, x = (lax.axis_index(name) for name in BITS)
-    head = (core * 4 + z_hi * 2 + x).astype(I32).reshape(1)
+    me = y * 16 + core * 8 + z_hi * 4 + z_lo * 2 + x
+    place = jnp.stack([me, me & 7]).astype(I32)
     rows, width = first_half.shape
     wide_rows = rows * 8
     own_rows = qk_weight.shape[0]
+    own_units = down_weight.shape[0]
+    units = own_units * 4
     rounds, tokens = stretch_ids.shape
     nchunk = tokens // STRETCH
     row_block = shaped(rows, width)
-
-    gains = jnp.concatenate([attn_gain, ffn_gain, jnp.zeros((128 - 2 * own_rows,), BF16)])
-    gains = jnp.broadcast_to(gains.astype(F32), (32, 1, 128))
-    gains = lax.all_to_all(gains, BITS, 0, 0, tiled=True).reshape(32, 128)
-    attn_gain_row = jnp.broadcast_to(gains[:, :own_rows].reshape(1, width), (8, width))
-    ffn_gain_row = jnp.broadcast_to(
-        gains[:, own_rows : 2 * own_rows].reshape(1, width), (8, width)
-    )
-    columns = jnp.stack([qk_weight, value_weight]).reshape(2, own_rows, NH, DH)
-    columns = columns.transpose(2, 1, 0, 3).reshape(NH, own_rows, 2 * DH)
-    heads_of = [((d >> 3) & 1) * 4 + ((d >> 2) & 1) * 2 + (d & 1) for d in range(32)]
-    columns = jnp.stack([columns[h] for h in heads_of])
-    columns = lax.all_to_all(columns, BITS, 0, 0, tiled=True).reshape(width, 2 * DH)
-    blocks = gather_xz(second_half)
-
-    out_full = lax.all_gather(out_weight, BITS, axis=0, tiled=True)
-    ffn_weights = lax.all_gather(
-        jnp.concatenate([up_weight.T, down_weight], axis=1), ("z_hi", "z_lo"), axis=0, tiled=True
-    )
-    qv_full = lax.all_gather(
-        jnp.concatenate([qk_weight, value_weight], axis=1), BITS, axis=0, tiled=True
-    )
+    acc_shape = shaped(rows, width, dtype=F32)
+
+    blocks = gather_zx(second_half)
+    gains = jnp.pad(jnp.stack([attn_gain, ffn_gain], axis=1), ((0, 0), (0, DH - 2)))
+    columns, z_rows, qv_rows = call(
+        pack_kernel,
+        [Far(a) for a in (qk_weight, value_weight, out_weight, up_weight, down_weight, gains)],
+        [
+            shaped(NH, own_rows, 3 * DH),
+            shaped(own_units + own_rows // 2, 2 * width),
+            shaped(own_rows, 2 * width),
+        ],
+        "pack",
+        cost=None,
+        far_out=(1, 2),
+    )
+    columns = shares(lax.all_to_all(columns, HEAD_AXES, 0, 0, tiled=True))
+    weights = lax.all_gather(after(z_rows, blocks[4]), ("z_hi", "z_lo"), axis=0)
+    cotangent_y = swap(grad_second, Y)
 
     ids = stretch_ids.reshape(rounds, 2, 2, 2, 2, 2, rows)
     for axis, bit in enumerate((y, core, z_hi, z_lo, x), 1):
         ids = jnp.where(bit == 1, jnp.flip(ids, axis), ids)
-    ids = ids.transpose(0, 4, 1, 2, 3, 5, 6).reshape(rounds, tokens)
+    ids = ids.reshape(rounds, tokens)
 
     def packed(numbers):
         return sum(numbers[r] << (8 * r) for r in range(rounds))
@@ -726,171 +917,204 @@
             jnp.zeros((5, tokens), I32),
         ]
     )
-    ids_both = (ids_row[:, None], ids_rows)
-
-    normed, queries, keys, values, norms, norm_row = call(
+    ids_column = call(
+        column_kernel, [Far(ids_rows)], [shaped(tokens, 1, dtype=I32)], "ids", far_out=(0,), cost=None
+    )[0]
+    ids_both = (ids_column, ids_rows)
+
+    columns[0] = after(columns[0], *ids_both)
+    normed, queries, kv, norms, norm_row, gain_rows = call(
         project_kernel,
-        [*blocks, attn_gain_row, columns],
+        [Far(blocks[0]), *blocks[1:], *columns],
         [
             shaped(wide_rows, width),
-            *[shaped(wide_rows, DH)] * 3,
+            shaped(wide_rows, DH),
+            shaped(wide_rows, 2 * DH),
             shaped(wide_rows, 1, dtype=F32),
             shaped(8, wide_rows, dtype=F32),
+            shaped(8, width, dtype=F32),
         ],
         "project",
-        8 * wide_rows * width * DH,
-    )
-    key_y, value_z = swap(keys, Y), swap(values, Z_LO)
-    key_z, value_y = swap(keys, Z_LO), swap(values, Y)
-    key_yz, value_yz = swap(key_y, Z_LO), swap(value_z, Y)
-    key_parts = [keys, key_y, key_z, key_yz]
-    value_parts = [values, value_y, value_z, value_yz]
-    acc = None
-    for part in range(4):
-        acc, *attn_send = forward_call(
-            queries,
-            norms,
-            ids_both,
-            key_parts[part],
-            value_parts[part],
-            part,
-            acc,
-            head if part == 3 else None,
-        )
-    attn_tok = lax.all_to_all(attn_send[0], HEAD_AXES, 0, 0, tiled=True)
-
-    y_first, first_out, normed_ffn = call(
-        out_kernel,
-        [attn_tok, first_half, out_full, ffn_gain_row],
-        [row_block, shaped(rows, width, dtype=F32), row_block],
-        "project_out",
-        2 * rows * width * width,
-    )
-    units = ffn_weights.shape[0]
-    ffn_flops = 2 * wide_rows * width * units
-    cotangents = gather_xy(grad_second)
+        cost=None,
+        far_out=range(6),
+        scalars=[place],
+        scratch=[pltpu.VMEM((width, 3 * DH), BF16)],
+    )
+    kv_parts = shares(kv)
+    acc, = forward_call(queries, norms, ids_both, kv_parts[:2], 0, None)
+    kv_parts[3] = swap(after(kv_parts[2], acc), CORE)
+    near, near_y = after(grad_second, kv_parts[3]), after(cotangent_y, kv_parts[3])
+    cotangents = [near, swap(near, X), near_y, swap(near_y, X)]
+    acc, attn_send = forward_call(queries, norms, ids_both, kv_parts[2:], 2, acc, place)
+    attn_send = after(attn_send, *cotangents)
+    out_parts = gather_xy(after(weights, attn_send)[:, own_units:])
+    cotangents = with_cores([after(a, attn_send) for a in cotangents])
+    qv_full = lax.all_gather(after(qv_rows, attn_send), BITS, axis=0, tiled=True)
+    attn_tok = lax.all_to_all(attn_send, HEAD_AXES, 0, 0, tiled=True)
+    units = own_units * 4
     hidden_back = call(
         hidden_back_kernel,
-        [*cotangents, ffn_weights],
-        shaped(wide_rows, units, dtype=F32),
+        [*map(Far, cotangents), Far(weights)],
+        [shaped(wide_rows, units, dtype=F32)],
         "hidden_back",
-        ffn_flops,
+        cost=None,
+        far_out=(0,),
+    )[0]
+    attn_tok = after(attn_tok, hidden_back)
+    y_first, first_out, normed_ffn, out_full = call(
+        out_kernel,
+        [attn_tok, Far(first_half), Far(gain_rows), *out_parts],
+        [row_block, acc_shape, row_block, shaped(width, width)],
+        "project_out",
+        cost=None,
+        far_out=(0, 1, 3),
+        scalars=[place],
     )
     ffn_in = gather_xy(normed_ffn)
     *grad_blocks, hidden, grad_pre = call(
         ffn_kernel,
-        [*ffn_in, hidden_back, ffn_weights],
+        [*ffn_in, Far(hidden_back), Far(weights)],
         [row_block] * 8 + [shaped(wide_rows, units)] * 2,
         "feed_forward",
-        3 * ffn_flops,
+        cost=None,
+        mib=44,
     )
     grad_parts = scatter_xy(grad_blocks)
-    *ffn_blocks, grad_ffn = call(
+    ffn_near, ffn_far, grad_ffn = call(
         ffn_rest_kernel,
-        [*ffn_in, *cotangents, hidden, grad_pre, ffn_weights],
-        [row_block] * 8 + [shaped(units, 2 * width)],
+        [*ffn_in, *map(Far, cotangents), hidden, grad_pre, Far(weights)],
+        [shaped(4, rows, width)] * 2 + [shaped(units, 2 * width)],
         "feed_forward_rest",
-        4 * ffn_flops,
+        cost=None,
+        far_out=range(3),
+        mib=48,
     )
     grad_mid, grad_attn, gain_sum = call(
         mid_kernel,
-        [*grad_parts, first_out, grad_first, ffn_gain_row, out_full],
+        [
+            *grad_parts,
+            *map(Far, (after(first_out, grad_ffn, qv_full), grad_first, gain_rows, out_full)),
+        ],
         [row_block, shaped(NH, rows, DH), shaped(8, width, dtype=F32)],
         "mid",
-        2 * rows * width * width,
+        cost=None,
+        far_out=(0,),
     )
 
     grad_attn = lax.all_to_all(grad_attn, HEAD_AXES, 0, 0, tiled=True)
-    grads, term_row, attn, _ = call(
+
+    out_width = width + DH
+    half = shaped(width // 2, out_width)
+    keep, move = call(
+        grad_out_kernel,
+        [Far(attn_tok), Far(grad_mid), Far(gain_sum)],
+        [half, half],
+        "grad_out",
+        far_out=(0,),
+        scalars=[place],
+    )
+
+    def halve(keep, came, shift, blocks):
+        half = shaped(keep.shape[0] // 2, out_width)
+        return call(
+            functools.partial(halve_kernel, shift=shift, blocks=blocks),
+            [Far(keep), came],
+            [half, half],
+            "halve",
+            far_out=(0,),
+            scalars=[place],
+        )
+
+    keep, move = halve(keep, swap(move, CORE), 4, 1)
+    came = swap(move, Y)
+    grads, term_row = call(
         turn_kernel,
-        [grad_attn, acc, head],
-        [
-            shaped(wide_rows, DH),
-            shaped(8, wide_rows, dtype=F32),
-            shaped(wide_rows, DH),
-            shaped(wide_rows, 1, dtype=F32),
-        ],
+        [after(grad_attn, move), Far(acc)],
+        [shaped(wide_rows, DH), shaped(8, wide_rows, dtype=F32)],
         "turn",
-        wide_rows * DH,
-        specs=[VMEM, VMEM, SMEM],
+        far_out=(0, 1),
+        scalars=[place],
+        scratch=[pltpu.VMEM((wide_rows, 1), F32)],
     )
 
     def backward(part, acc):
         return backward_call(
-            queries,
-            grads,
-            norm_row,
-            term_row,
-            ids_both,
-            key_parts[part],
-            value_parts[part],
-            part,
-            acc,
+            queries, grads, norm_row, term_row, ids_both, kv_parts[part : part + 2], part, acc
         )
 
-    direct, far_key, far_value = backward(3, None)
-    far_key, far_value = swap(far_key, Y), swap(far_value, Z_LO)
-    direct, z_key, z_value = backward(2, direct)
-    z_value = swap(z_value, Z_LO)
-    direct = after(direct, far_key, far_value)
-    direct, y_key, y_value = backward(1, direct)
-    y_key = swap(y_key, Y)
-    z_key = swap((z_key.astype(F32) + far_key.astype(F32)).astype(BF16), Z_LO)
-    y_value = swap((y_value.astype(F32) + far_value.astype(F32)).astype(BF16), Y)
-    direct, grad_keys, grad_values = backward(0, direct)
-
-    ffn_blocks = [after(block, grad_attn) for block in ffn_blocks]
-    second_out = second_half.astype(F32) + sum(
-        part.astype(F32) for part in scatter_xy(ffn_blocks)
-    )
+    ffn_far = swap(after(ffn_far, grads), CORE)
     grad_ffn = lax.psum_scatter(
         grad_ffn, ("z_hi", "z_lo"), scatter_dimension=0, tiled=True
-    ).astype(F32)
-    gain_sum = after(gain_sum, grad_attn)[0].reshape(32, 1, own_rows)
-    gain_sum = jnp.pad(gain_sum, ((0, 0), (0, 0), (0, 128 - own_rows)))
-    gain_sum = lax.all_to_all(gain_sum, BITS, 0, 0, tiled=True)
-    grad_ffn_gain = jnp.sum(gain_sum, axis=(0, 1))[:own_rows]
-
-    def halve(value, axis, bit, mask):
-        keep = lax.dynamic_index_in_dim(value, bit, axis, keepdims=False)
-        send = lax.dynamic_index_in_dim(value, 1 - bit, axis, keepdims=False)
-        return keep + swap(send.astype(BF16), mask).astype(F32)
-
-    grad_mid_all = jnp.concatenate(gather_xz(after(grad_mid, grad_attn)), axis=0)
-    grad_out = dot(attn, grad_mid_all, TN).reshape(2, 2, DH // 4, width)
-    grad_out = halve(halve(grad_out, 1, y, Y), 0, z_lo, Z_LO)
-    owners = []
-    for d in range(32):
-        dy, dc, dh, dl, dx = ((d >> s) & 1 for s in (4, 3, 2, 1, 0))
-        owners.append((d, dc * 16 + dh * 8 + dx * 4 + dl * 2 + dy))
-    grad_out = lax.ppermute(grad_out.astype(BF16), BITS, owners).astype(F32)
+    )
+    direct, over_y, far = backward(2, None)
+    far = swap(far, CORE)
+    keep, move = halve(keep, after(came, direct), 0, 4)
+    over_y = (over_y.astype(F32) + after(far, move).astype(F32)).astype(BF16)
+    direct = after(direct, over_y)
+    over_y = swap(over_y, Y)
+    came = swap(move, X)
+    direct, grad_kv, over_core = backward(0, direct)
+    direct = after(direct, grad_ffn)
+    over_core = swap(after(over_core, over_y), CORE)
 
     send, grad_both = call(
         gather_grads_kernel,
-        [direct, queries, norms, head, grad_keys, y_key, z_key, grad_values, y_value, z_value],
+        [*map(Far, (direct, queries, norms, grad_kv)), over_core, over_y],
         [shaped(NH, rows, 2 * DH), shaped(wide_rows, 2 * DH)],
         "gather_grads",
-        wide_rows * DH,
-        specs=[VMEM] * 3 + [SMEM] + [VMEM] * 6,
+        far_out=(1,),
+        scalars=[place],
     )
     arrived = lax.all_to_all(send, HEAD_AXES, 0, 0, tiled=True)
+
+    grad_rows = call(
+        project_back_kernel,
+        [Far(normed), Far(grad_both)],
+        [shaped(NH, own_rows, 2 * DH)] * 4,
+        "project_back",
+        scalars=[place],
+        scratch=[pltpu.VMEM((width, 2 * DH), F32)],
+    )
+    rows_parts = grad_rows
+    grad_rows = call(
+        sum_kernel,
+        [after(part, arrived) for part in sum_shares(grad_rows)],
+        [shaped(NH, own_rows, 2 * DH)],
+        "sum_rows",
+        scalars=[place],
+    )
+    rows_send = grad_rows[0]
+    grad_rows = lax.all_to_all(rows_send, HEAD_AXES, 0, 0, tiled=True)
     grad_second_half = call(
         last_kernel,
-        [arrived, second_half, grad_second, attn_gain_row, qv_full],
-        row_block,
+        [arrived, *map(Far, (second_half, grad_second, gain_rows, qv_full))],
+        [row_block],
         "last",
-        4 * rows * width * width,
-    )
-
-    grad_rows = dot(normed, grad_both, TN).reshape(2, 2, 2, 2, 2, own_rows, 2 * DH)
-    grad_rows = halve(halve(grad_rows, 0, y, Y), 2, z_lo, Z_LO)
-    grad_rows = grad_rows.reshape(8, own_rows, 2 * DH).astype(BF16)
-    grad_rows = lax.all_to_all(grad_rows, HEAD_AXES, 0, 0, tiled=True).astype(F32)
-    grad_qk = grad_rows[:, :, :DH].transpose(1, 0, 2).reshape(own_rows, width)
-    grad_value = grad_rows[:, :, DH:].transpose(1, 0, 2).reshape(own_rows, width)
-    grad_attn_gain = jnp.sum(
-        qk_weight.astype(F32) * grad_qk + value_weight.astype(F32) * grad_value, axis=-1
-    ) / attn_gain.astype(F32)
+        far_out=(0,),
+    )[0]
+
+    keep, move = halve(keep, after(came, rows_parts[0]), 1, 2)
+    keep, move = halve(keep, after(swap(move, Z_LO), rows_send), 2, 1)
+    grad_out = keep.astype(F32) + swap(move, Z_HI).astype(F32)
+    ffn_sum = after(ffn_near, rows_parts[0]).astype(F32) + ffn_far.astype(F32)
+    ffn_move = swap(ffn_sum[1::2].astype(BF16), X)
+    ffn_sum = ffn_sum[0::2] + after(ffn_move, rows_send).astype(F32)
+    ffn_sum = ffn_sum[0] + swap(ffn_sum[1].astype(BF16), Y).astype(F32)
+    second_out = second_half.astype(F32) + ffn_sum
+    grad_up, grad_down = call(
+        unpack_kernel,
+        [Far(after(grad_ffn, arrived))],
+        [shaped(width, own_units, dtype=F32), shaped(own_units, width, dtype=F32)],
+        "unpack",
+        far_out=(0, 1),
+    )
+    grad_qk, grad_value, grad_attn_gain = call(
+        own_rows_kernel,
+        [after(grad_rows, grad_second_half, grad_up), Far(qk_weight), Far(value_weight), Far(gains)],
+        [shaped(own_rows, width, dtype=F32)] * 2 + [shaped(own_rows, 128, dtype=F32)],
+        "own_rows",
+        far_out=(0, 1),
+    )
 
     return (
         y_first,
@@ -899,11 +1123,11 @@
         grad_second_half,
         grad_qk,
         grad_value,
-        grad_out,
-        grad_attn_gain,
-        grad_ffn_gain,
-        grad_ffn[:, :width].T,
-        grad_ffn[:, width:],
+        grad_out[:, :width],
+        grad_attn_gain[:, 0],
+        grad_out[:, width],
+        grad_up,
+        grad_down,
     )
 
 

time: 446 us -> 403 us (0.904)
  Pallas kernels: 89.6 us -> 164 us
  waiting for transfers between devices: 173 us -> 118 us
  local copies, waits for them, and re-layouts: 72.4 us -> 20.8 us
  starting transfers between devices: 71.2 us -> 63.8 us
    pallas_call x17 -> x24, Pallas kernels: 89.6 us -> 164 us  [the longest x20 102 us: call(): pl.pallas_call(body, in_specs=[SMEM] * len(scalars) + [far if i in far_in...]
    ppermute x58 -> x55, waiting for transfers between devices: 149 us -> 92.8 us  [swap(): return lax.ppermute(value, BITS, [(i, i ^ mask) for i in range(32)])]
    unnamed x203 -> x118, local copies, waits for them, and re-layouts: 58.5 us -> 12.2 us
    all_to_all x1, waiting for transfers between devices: 0.01 us -> 15.6 us  [cube_plan(): grad_attn = lax.all_to_all(grad_attn, HEAD_AXES, 0, 0, tiled=True)]
    all_to_all x5 -> x3, waiting for transfers between devices: 15.7 us -> 2.88 us  [the longest x1 2.87 us: cube_plan(): columns = shares(lax.all_to_all(columns, HEAD_AXES, 0, 0, tiled=True))]
    all_to_all x5 -> x3, starting transfers between devices: 19.2 us -> 12.6 us  [the longest x1 5 us: cube_plan(): attn_tok = lax.all_to_all(attn_send, HEAD_AXES, 0, 0, tiled=True)]
    add x2 -> x3, other arithmetic: 1.01 us -> 6.19 us  [the longest x1 3.93 us: cube_plan(): ffn_sum = after(ffn_near, rows_parts[0]).astype(F32) + ffn_far.astype(F32)]
    ppermute x58 -> x55, starting transfers between devices: 43.3 us -> 42.6 us  [swap(): return lax.ppermute(value, BITS, [(i, i ^ mask) for i in range(32)])]
  transfers between devices with their start and end apart: 70 -> 63, of which waited for: 22 -> 23; matrix products, arithmetic and copies ran while one was open for 12% -> 5% of each run, Pallas kernels for 20% -> 39%
where the time goes in v2:
time: 403 us; the launch traced here: 395 us
  Pallas kernels  164 us (41%)
  waiting for transfers between devices  118 us (29%)
  starting transfers between devices  63.8 us (16%)
  local copies, waits for them, and re-layouts  20.8 us (5%)
  between operations  15 us (4%)
  other arithmetic  13.1 us (3%)
    pallas_call x20, Pallas kernels, call(): pl.pallas_call(body, in_specs=[SMEM] * len(scalars) + [far if i in far_in...  102 us
    ppermute x55, waiting for transfers between devices, swap(): return lax.ppermute(value, BITS, [(i, i ^ mask) for i in range(32)])  92.8 us
    ppermute x55, starting transfers between devices, swap(): return lax.ppermute(value, BITS, [(i, i ^ mask) for i in range(32)])  42.6 us
    pallas_call x2, Pallas kernels, backward_call(): pl.pallas_call(functools.partial(backward_kernel, tile=tile, own=acc is n...  36 us
    pallas_call x2, Pallas kernels, forward_call(): pl.pallas_call(functools.partial(forward_kernel, tile=tile, own=acc is No...  26.2 us
    all_to_all x1, waiting for transfers between devices, cube_plan(): grad_attn = lax.all_to_all(grad_attn, HEAD_AXES, 0, 0, tiled=True)  15.6 us
    unnamed x118, local copies, waits for them, and re-layouts  12.2 us
  transfers between devices with their start and end apart: 63, of which 23 were waited for; matrix products, arithmetic and copies ran while one was open for 5% of the time, Pallas kernels for 39%

profile of v2, /device:TPU:0, one launch (start us, length us, event | category | flops | bytes accessed | tf_op | source)
XLA Modules:
  0.0 395.1 jit_solution(14576464096522229477)
XLA Ops:
  7.2 4.1 %collective-permute-start.3 = (bf16[192,1024]{1,0:T(8,128)(2,1)}, bf16[192,1024]{1,0:T(8,128)(2,1)S(1)}, u32[]{:S(2)}, u32[]{:S(2)}) collective-permute-start(bf16[192,1024]{1,0:T(8,128)(2,1)} %refs_1_.6), channel_id=1, source_target_pairs={{0,4},{1,5},{2,6},{3,7},{4,0},{5,1},{6,2},{7,3},{8,12},{9,13},{10,... | collective-permute-start | bytes 1179656 | tf_op jit(solution)/shard_map/ppermute | solution.py:324
  24.7 5.5 %collective-permute-done.3.refs_5_ = bf16[192,1024]{1,0:T(8,128)(2,1)S(1)} collective-permute-done((bf16[192,1024]{1,0:T(8,128)(2,1)}, bf16[192,1024]{1,0:T(8,128)(2,1)S(1)}, u32[]{:S(2)}, u32[]{:S(2)}) %collective-permute-start.3) | collective-permute-done | bytes 393248 | tf_op jit(solution)/shard_map/ppermute | solution.py:324
  48.5 8.4 %collective-permute-done.2.refs_4_ = bf16[192,1024]{1,0:T(8,128)(2,1)S(1)} collective-permute-done((bf16[192,1024]{1,0:T(8,128)(2,1)S(1)}, bf16[192,1024]{1,0:T(8,128)(2,1)S(1)}, u32[]{:S(2)}, u32[]{:S(2)}) %collective-permute-start.2) | collective-permute-done | bytes 393248 | tf_op jit(solution)/shard_map/ppermute | solution.py:324
  56.9 8.0 %collective-permute-done.6.refs_8_ = bf16[192,1024]{1,0:T(8,128)(2,1)S(1)} collective-permute-done((bf16[192,1024]{1,0:T(8,128)(2,1)S(1)}, bf16[192,1024]{1,0:T(8,128)(2,1)S(1)}, u32[]{:S(2)}, u32[]{:S(2)}) %collective-permute-start.6) | collective-permute-done | bytes 393248 | tf_op jit(solution)/shard_map/ppermute | solution.py:324
  65.7 8.0 %project.1 = (bf16[1536,1024]{1,0:T(8,128)(2,1)}, bf16[1536,128]{1,0:T(8,128)(2,1)}, bf16[1536,256]{1,0:T(8,128)(2,1)}, f32[1536,1]{1,0:T(8,128)}, f32[8,1536]{1,0:T(8,128)}, /*index=5*/f32[8,1024]{1,0:T(8,128)}) custom-call(s32[2]{0:T(128)} %pad_add_fusion.refs_0_.refs_7_, bf16[192,1024]{1,0:T(8,128)(2,1)} %refs_1_.6, bf16[192,1024]{1,0:T(8,128)(2,1)} %copy-done.35, ...), custom_call_target="tpu_custom_call" | custom-call | tf_op jit(solution)/shard_map/project/pallas_call | solution.py:370
  77.2 13.3 %attention_forward.2.refs_6_ = f32[1536,256]{1,0:T(8,128)} custom-call(bf16[1536,128]{1,0:T(8,128)(2,1)} %get-tuple-element.104.refs_0_.refs_2_, f32[1536,1]{1,0:T(8,128)} %get-tuple-element.105.refs_1_.refs_3_, s32[6144,1]{1,0:T(8,128)} %ids.1.refs_2_.refs_5_, s32[8,6144]{1,0:T(8,128)} %add_add_fusion.refs_0_.refs_3_.refs_4_, ...), custom_call_target="tpu_custom_call" | custom-call | tf_op jit(solution)/shard_map/attention_forward/pallas_call | solution.py:584
  94.5 10.9 %collective-permute-done.14.refs_2_.refs_10_ = bf16[192,1024]{1,0:T(8,128)(2,1)S(1)} collective-permute-done((bf16[192,1024]{1,0:T(8,128)(2,1)S(1)}, bf16[192,1024]{1,0:T(8,128)(2,1)S(1)}, u32[]{:S(2)}, u32[]{:S(2)}) %collective-permute-start.14) | collective-permute-done | bytes 393248 | tf_op jit(solution)/shard_map/ppermute | solution.py:324
  107.6 12.9 %attention_forward.3 = (f32[1536,256]{1,0:T(8,128)}, bf16[8,192,128]{2,1,0:T(8,128)(2,1)}) custom-call(bf16[1536,128]{1,0:T(8,128)(2,1)} %get-tuple-element.104.refs_0_.refs_2_, f32[1536,1]{1,0:T(8,128)} %get-tuple-element.105.refs_1_.refs_3_, s32[6144,1]{1,0:T(8,128)} %ids.1.refs_2_.refs_5_, ...), custom_call_target="tpu_custom_call", output_to_operand_aliasing={{0}: (6, {})} | custom-call | tf_op jit(solution)/shard_map/attention_forward/pallas_call | solution.py:584
  120.5 4.2 %collective-permute-done.13.refs_1_.refs_9_ = bf16[192,1024]{1,0:T(8,128)(2,1)S(1)} collective-permute-done((bf16[192,1024]{1,0:T(8,128)(2,1)S(1)}, bf16[192,1024]{1,0:T(8,128)(2,1)S(1)}, u32[]{:S(2)}, u32[]{:S(2)}) %collective-permute-start.13) | collective-permute-done | bytes 393248 | tf_op jit(solution)/shard_map/ppermute | solution.py:324
  125.2 5.0 %all-to-all-start.1 = ((bf16[8,192,128]{2,1,0:T(8,128)(2,1)}), bf16[8,192,128]{2,1,0:T(8,128)(2,1)S(1)}, u32[]{:S(2)}, u32[]{:S(2)}) async-start(bf16[8,192,128]{2,1,0:T(8,128)(2,1)} %get-tuple-element.111), calls=%async_computation.1 | async-start | bytes 786432 | tf_op jit(solution)/shard_map/all_to_all | solution.py:953
  135.7 8.9 %collective-permute-done.20.refs_5_ = bf16[4,16,2048]{2,1,0:T(8,128)(2,1)} collective-permute-done((bf16[4,16,2048]{2,1,0:T(8,128)(2,1)S(1)}, bf16[4,16,2048]{2,1,0:T(8,128)(2,1)}, u32[]{:S(2)}, u32[]{:S(2)}) %collective-permute-start.20) | collective-permute-done | bytes 262176 | tf_op jit(solution)/shard_map/ppermute | solution.py:324
  145.1 4.9 %collective-permute-done.22.refs_7_ = bf16[4,16,2048]{2,1,0:T(8,128)(2,1)} collective-permute-done((bf16[4,16,2048]{2,1,0:T(8,128)(2,1)S(1)}, bf16[4,16,2048]{2,1,0:T(8,128)(2,1)}, u32[]{:S(2)}, u32[]{:S(2)}) %collective-permute-start.22) | collective-permute-done | bytes 262176 | tf_op jit(solution)/shard_map/ppermute | solution.py:324
  150.8 7.3 %hidden_back.1.refs_8_ = f32[1536,512]{1,0:T(8,128)} custom-call(bf16[192,1024]{1,0:T(8,128)(2,1)} %refs_2_.6, bf16[192,1024]{1,0:T(8,128)(2,1)} %copy-done.6, bf16[192,1024]{1,0:T(8,128)(2,1)} %copy-done.2, bf16[192,1024]{1,0:T(8,128)(2,1)} %copy-done.4, bf16[192,1024]{1,0:T(8,128)(2,1)} %copy-done.12, bf16[192,1024]{1,0:T(8,128)(2,1)} %copy-done.10, ...), custom_call_target="tpu_custom_call" | custom-call | tf_op jit(solution)/shard_map/hidden_back/pallas_call | solution.py:370
  158.9 5.8 %project_out.1 = (bf16[192,1024]{1,0:T(8,128)(2,1)}, f32[192,1024]{1,0:T(8,128)}, bf16[192,1024]{1,0:T(8,128)(2,1)}, bf16[1024,1024]{1,0:T(8,128)(2,1)}) custom-call(s32[2]{0:T(128)} %pad_add_fusion.refs_0_.refs_7_, bf16[8,192,128]{2,1,0:T(8,128)(2,1)} %copy-done.23, bf16[192,1024]{1,0:T(8,128)(2,1)} %refs_2_.5, ...), custom_call_target="tpu_custom_call" | custom-call | tf_op jit(solution)/shard_map/project_out/pallas_call | solution.py:370
  168.3 13.5 %collective-permute-done.27.refs_1_ = bf16[192,1024]{1,0:T(8,128)(2,1)S(1)} collective-permute-done((bf16[192,1024]{1,0:T(8,128)(2,1)}, bf16[192,1024]{1,0:T(8,128)(2,1)S(1)}, u32[]{:S(2)}, u32[]{:S(2)}) %collective-permute-start.27) | collective-permute-done | bytes 393248 | tf_op jit(solution)/shard_map/ppermute | solution.py:324
  183.6 9.8 %collective-permute-done.29.refs_3_ = bf16[192,1024]{1,0:T(8,128)(2,1)S(1)} collective-permute-done((bf16[192,1024]{1,0:T(8,128)(2,1)}, bf16[192,1024]{1,0:T(8,128)(2,1)S(1)}, u32[]{:S(2)}, u32[]{:S(2)}) %collective-permute-start.29) | collective-permute-done | bytes 393248 | tf_op jit(solution)/shard_map/ppermute | solution.py:324
  196.3 9.3 %feed_forward.1 = (bf16[192,1024]{1,0:T(8,128)(2,1)S(1)}, bf16[192,1024]{1,0:T(8,128)(2,1)S(1)}, bf16[192,1024]{1,0:T(8,128)(2,1)S(1)}, bf16[192,1024]{1,0:T(8,1...) custom-call(bf16[192,1024]{1,0:T(8,128)(2,1)S(1)} %copy-done.14, ...), custom_call_target="tpu_custom_call" | custom-call | tf_op jit(solution)/shard_map/feed_forward/pallas_call | solution.py:370
  212.7 11.8 %feed_forward_rest.1 = (bf16[4,192,1024]{2,1,0:T(8,128)(2,1)}, bf16[4,192,1024]{2,1,0:T(8,128)(2,1)}, bf16[512,2048]{1,0:T(8,128)(2,1)}) custom-call(bf16[192,1024]{1,0:T(8,128)(2,1)S(1)} %copy-done.15, bf16[192,1024]{1,0:T(8,128)(2,1)S(1)} %collective-permute-done.27.refs_1_, bf16[192,1024]{1,0:T(8,128)(2,1)S(1)} %collective-permute-done.28.refs_2_, ...), custom_call_target="tpu_custom_call" | custom-call | tf_op jit(solution)/shard_map/feed_forward_rest/pallas_call | solution.py:370
  224.5 4.4 %collective-permute-done.38.refs_3_ = bf16[192,1024]{1,0:T(8,128)(2,1)S(1)} collective-permute-done((bf16[192,1024]{1,0:T(8,128)(2,1)S(1)}, bf16[192,1024]{1,0:T(8,128)(2,1)S(1)}, u32[]{:S(2)}, u32[]{:S(2)}) %collective-permute-start.38) | collective-permute-done | bytes 393248 | tf_op jit(solution)/shard_map/ppermute | solution.py:324
  229.8 5.9 %mid.1 = (bf16[192,1024]{1,0:T(8,128)(2,1)}, bf16[8,192,128]{2,1,0:T(8,128)(2,1)}, f32[8,1024]{1,0:T(8,128)}) custom-call(bf16[192,1024]{1,0:T(8,128)(2,1)} %copy-done.18, bf16[192,1024]{1,0:T(8,128)(2,1)} %copy-done.38, bf16[192,1024]{1,0:T(8,128)(2,1)} %copy-done.43, bf16[192,1024]{1,0:T(8,128)(2,1)} %copy-done.42, bf16[192,1024]{1,0:T(8,128)(2,1)} %copy-done.40, ...), custom_call_target="tpu_custom_call" | custom-call | tf_op jit(solution)/shard_map/mid/pallas_call | solution.py:370
  235.8 4.6 %grad_out.1 = (bf16[512,1152]{1,0:T(8,128)(2,1)}, bf16[512,1152]{1,0:T(8,128)(2,1)}) custom-call(s32[2]{0:T(128)} %pad_add_fusion.refs_0_.refs_7_, bf16[8,192,128]{2,1,0:T(8,128)(2,1)} %copy-done.23, bf16[192,1024]{1,0:T(8,128)(2,1)} %get-tuple-element.93.refs_2_, f32[8,1024]{1,0:T(8,128)} %get-tuple-element.143.refs_3_), custom_call_target="tpu_custom_call" | custom-call | flops 99999997952 | bytes 1 | tf_op jit(solution)/shard_map/grad_out/pallas_call | solution.py:370
  240.5 4.8 %all-to-all-start.2 = ((bf16[8,192,128]{2,1,0:T(8,128)(2,1)}), bf16[8,192,128]{2,1,0:T(8,128)(2,1)S(1)}, u32[]{:S(2)}, u32[]{:S(2)}) async-start(bf16[8,192,128]{2,1,0:T(8,128)(2,1)} %get-tuple-element.141), calls=%async_computation.2 | async-start | bytes 786432 | tf_op jit(solution)/shard_map/all_to_all | solution.py:1004
  246.3 4.4 %halve.4 = (bf16[256,1152]{1,0:T(8,128)(2,1)}, bf16[256,1152]{1,0:T(8,128)(2,1)}) custom-call(s32[2]{0:T(128)} %pad_add_fusion.refs_0_.refs_7_, bf16[512,1152]{1,0:T(8,128)(2,1)} %get-tuple-element.144.refs_1_, bf16[512,1152]{1,0:T(8,128)(2,1)} %copy-done.49), custom_call_target="tpu_custom_call" | custom-call | flops 99999997952 | bytes 1 | tf_op jit(solution)/shard_map/halve/pallas_call | solution.py:370
  251.9 15.6 %all-to-all-done.2.refs_1_ = bf16[8,192,128]{2,1,0:T(8,128)(2,1)S(1)} async-done(((bf16[8,192,128]{2,1,0:T(8,128)(2,1)}), bf16[8,192,128]{2,1,0:T(8,128)(2,1)S(1)}, u32[]{:S(2)}, u32[]{:S(2)}) %all-to-all-start.2) | async-done | bytes 393248 | tf_op jit(solution)/shard_map/all_to_all | solution.py:1004
  272.1 17.4 %attention_backward.2 = (f32[1536,256]{1,0:T(8,128)}, bf16[1536,256]{1,0:T(8,128)(2,1)}, bf16[1536,256]{1,0:T(8,128)(2,1)}) custom-call(bf16[1536,128]{1,0:T(8,128)(2,1)} %get-tuple-element.104.refs_0_.refs_2_, bf16[1536,128]{1,0:T(8,128)(2,1)} %get-tuple-element.149.refs_1_, f32[8,1536]{1,0:T(8,128)} %get-tuple-element.150.refs_2_, ...), custom_call_target="tpu_custom_call" | custom-call | flops 99999997952 | bytes 1 | tf_op jit(solution)/shard_map/attention_backward/pallas_call | solution.py:647
  294.4 18.6 %attention_backward.3 = (f32[1536,256]{1,0:T(8,128)}, bf16[1536,256]{1,0:T(8,128)(2,1)}, bf16[1536,256]{1,0:T(8,128)(2,1)}) custom-call(bf16[1536,128]{1,0:T(8,128)(2,1)} %get-tuple-element.104.refs_0_.refs_2_, bf16[1536,128]{1,0:T(8,128)(2,1)} %get-tuple-element.149.refs_1_, f32[8,1536]{1,0:T(8,128)} %get-tuple-element.150.refs_2_, ...), custom_call_target="tpu_custom_call", output_to_operand_aliasing={{0}: (8, {})} | custom-call | flops 99999997952 | bytes 1 | tf_op jit(solution)/shard_map/attention_backward/pallas_call | solution.py:647
  318.1 6.0 %gather_grads.1 = (bf16[8,192,256]{2,1,0:T(8,128)(2,1)}, bf16[1536,256]{1,0:T(8,128)(2,1)}) custom-call(s32[2]{0:T(128)} %pad_add_fusion.refs_0_.refs_7_, f32[1536,256]{1,0:T(8,128)} %get-tuple-element.161.refs_1_, bf16[1536,128]{1,0:T(8,128)(2,1)} %get-tuple-element.104.refs_0_.refs_2_, f32[1536,1]{1,0:T(8,128)} %get-tuple-element.105.refs_1_.refs_3_, ...), custom_call_target="tpu_custom_call" | custom-call | flops 99999997952 | bytes 1 | tf_op jit(solution)/shard_map/gather_grads/pallas_call | solution.py:370
  324.1 4.6 %project_back.1 = (bf16[8,32,256]{2,1,0:T(8,128)(2,1)}, bf16[8,32,256]{2,1,0:T(8,128)(2,1)}, bf16[8,32,256]{2,1,0:T(8,128)(2,1)}, bf16[8,32,256]{2,1,0:T(8,128)(2,1)}) custom-call(s32[2]{0:T(128)} %pad_add_fusion.refs_0_.refs_7_, bf16[1536,1024]{1,0:T(8,128)(2,1)} %get-tuple-element.126.refs_1_, bf16[1536,256]{1,0:T(8,128)(2,1)} %get-tuple-element.165.refs_2_), custom_call_target="tpu_custom_call" | custom-call | flops 99999997952 | bytes 1 | tf_op jit(solution)/shard_map/project_back/pallas_call | solution.py:370
  339.6 3.9 convert_add_fusion
  346.0 6.9 %all-to-all-done.3.refs_0_ = bf16[8,192,256]{2,1,0:T(8,128)(2,1)S(1)} async-done(((bf16[8,192,256]{2,1,0:T(8,128)(2,1)}), bf16[8,192,256]{2,1,0:T(8,128)(2,1)S(1)}, u32[]{:S(2)}, u32[]{:S(2)}) %all-to-all-start.3) | async-done | bytes 786464 | tf_op jit(solution)/shard_map/all_to_all | solution.py:1068
  356.1 4.2 %all-to-all-start.4 = ((bf16[8,32,256]{2,1,0:T(8,128)(2,1)}), bf16[8,32,256]{2,1,0:T(8,128)(2,1)}, u32[]{:S(2)}, u32[]{:S(2)}) async-start(bf16[8,32,256]{2,1,0:T(8,128)(2,1)} %sum_rows.1), calls=%async_computation.5 | async-start | bytes 262144 | tf_op jit(solution)/shard_map/all_to_all | solution.py:1087
  373.4 6.1 %last.1 = bf16[192,1024]{1,0:T(8,128)(2,1)} custom-call(bf16[8,192,256]{2,1,0:T(8,128)(2,1)} %copy-done.31, bf16[192,1024]{1,0:T(8,128)(2,1)} %refs_1_.6, bf16[192,1024]{1,0:T(8,128)(2,1)} %refs_2_.6, f32[8,1024]{1,0:T(8,128)} %get-tuple-element.119.refs_3_.refs_7_, bf16[1024,2048]{1,0:T(8,128)(2,1)} %all-gather.4.cloned.1.call-done.refs_4_), custom_call_target="tpu_custom_call" | custom-call | flops 99999997952 | bytes 1 | tf_op jit(solution)/shard_map/last/pallas_call | solution.py:370
  (275 shorter events, 120.9 us)
Async XLA Ops:
  7.2 23.0 %collective-permute-start.3 = (bf16[192,1024]{1,0:T(8,128)(2,1)}, bf16[192,1024]{1,0:T(8,128)(2,1)S(1)}, u32[]{:S(2)}, u32[]{:S(2)}) collective-permute-start(bf16[192,1024]{1,0:T(8,128)(2,1)} %refs_1_.6), channel_id=1, source_target_pairs={{0,4},{1,5},{2,6},{3,7},{4,0},{5,1},{6,2},{7,3},{8,12},{9,13},{10,... | collective-permute-start | bytes 1179656 | tf_op jit(solution)/shard_map/ppermute | solution.py:324
  11.3 25.2 %collective-permute-start.1 = (bf16[192,1024]{1,0:T(8,128)(2,1)}, bf16[192,1024]{1,0:T(8,128)(2,1)S(1)}, u32[]{:S(2)}, u32[]{:S(2)}) collective-permute-start(bf16[192,1024]{1,0:T(8,128)(2,1)} %refs_1_.6), channel_id=1, source_target_pairs={{0,2},{1,3},{2,0},{3,1},{4,6},{5,7},{6,4},{7,5},{8,10},{9,11},{10,... | collective-permute-start | bytes 1179656 | tf_op jit(solution)/shard_map/ppermute | solution.py:324
  12.9 24.5 %collective-permute-start = (bf16[192,1024]{1,0:T(8,128)(2,1)}, bf16[192,1024]{1,0:T(8,128)(2,1)S(1)}, u32[]{:S(2)}, u32[]{:S(2)}) collective-permute-start(bf16[192,1024]{1,0:T(8,128)(2,1)} %refs_1_.6), channel_id=1, source_target_pairs={{0,1},{1,0},{2,3},{3,2},{4,5},{5,4},{6,7},{7,6},{8,9},{9,8},{10,11... | collective-permute-start | bytes 1179656 | tf_op jit(solution)/shard_map/ppermute | solution.py:324
  18.6 15.4 %all-to-all-start = ((bf16[8,32,384]{2,1,0:T(8,128)(2,1)}), bf16[8,32,384]{2,1,0:T(8,128)(2,1)S(1)}, u32[]{:S(2)}, u32[]{:S(2)}) async-start(bf16[8,32,384]{2,1,0:T(8,128)(2,1)} %get-tuple-element.102), calls=%async_computation | async-start | bytes 393216 | tf_op jit(solution)/shard_map/all_to_all | solution.py:899
  22.0 108.5 %all-gather.6.cloned.1.call-start = ((), (), s32[]{:S(2)}) async-start(), calls=%async_computation.8 | async-start | bytes 2949120 | tf_op jit(solution)/shard_map/all_gather | solution.py:900
  35.6 188.9 %all-gather.4.cloned.1.call-start = ((), (), s32[]{:S(2)}) async-start(), calls=%async_computation.6 | async-start | bytes 4325376 | tf_op jit(solution)/shard_map/all_gather | solution.py:952
  37.4 19.5 %collective-permute-start.2 = (bf16[192,1024]{1,0:T(8,128)(2,1)S(1)}, bf16[192,1024]{1,0:T(8,128)(2,1)S(1)}, u32[]{:S(2)}, u32[]{:S(2)}) collective-permute-start(bf16[192,1024]{1,0:T(8,128)(2,1)S(1)} %collective-permute-done.1.refs_3_), channel_id=1, source_target_pairs={{0,1},{1,0},{2,3},{3,2},{4,5},{5,4},{6,7},{7,6},{8,9},{9,8},{10,11... | collective-permute-start | bytes 1179656 | tf_op jit(solution)/shard_map/ppermute | solution.py:324
  40.9 24.0 %collective-permute-start.6 = (bf16[192,1024]{1,0:T(8,128)(2,1)S(1)}, bf16[192,1024]{1,0:T(8,128)(2,1)S(1)}, u32[]{:S(2)}, u32[]{:S(2)}) collective-permute-start(bf16[192,1024]{1,0:T(8,128)(2,1)S(1)} %collective-permute-done.5.refs_7_), channel_id=1, source_target_pairs={{0,1},{1,0},{2,3},{3,2},{4,5},{5,4},{6,7},{7,6},{8,9},{9,8},{10,11... | collective-permute-start | bytes 1179656 | tf_op jit(solution)/shard_map/ppermute | solution.py:324
  73.8 20.2 %collective-permute-start.10 = (bf16[1536,256]{1,0:T(8,128)(2,1)}, bf16[1536,256]{1,0:T(8,128)(2,1)S(1)}, u32[]{:S(2)}, u32[]{:S(2)}) collective-permute-start(bf16[1536,256]{1,0:T(8,128)(2,1)} %get-tuple-element.106.refs_4_.refs_6_), channel_id=1, source_target_pairs={{0,16},{1,17},{2,18},{3,19},{4,20},{5,21},{6,22},{7,23},{8,24},{9,... | collective-permute-start | bytes 2359304 | tf_op jit(solution)/shard_map/ppermute | solution.py:324
  106.3 18.3 %collective-permute-start.13 = (bf16[192,1024]{1,0:T(8,128)(2,1)S(1)}, bf16[192,1024]{1,0:T(8,128)(2,1)S(1)}, u32[]{:S(2)}, u32[]{:S(2)}) collective-permute-start(bf16[192,1024]{1,0:T(8,128)(2,1)S(1)} %copy-done), channel_id=1, source_target_pairs={{0,1},{1,0},{2,3},{3,2},{4,5},{5,4},{6,7},{7,6},{8,9},{9,8},{10,11... | collective-permute-start | bytes 1179656 | tf_op jit(solution)/shard_map/ppermute | solution.py:324
  125.2 32.9 %all-to-all-start.1 = ((bf16[8,192,128]{2,1,0:T(8,128)(2,1)}), bf16[8,192,128]{2,1,0:T(8,128)(2,1)S(1)}, u32[]{:S(2)}, u32[]{:S(2)}) async-start(bf16[8,192,128]{2,1,0:T(8,128)(2,1)} %get-tuple-element.111), calls=%async_computation.1 | async-start | bytes 786432 | tf_op jit(solution)/shard_map/all_to_all | solution.py:953
  130.2 185.2 %reduce-scatter.2.cloned.1.call-start = ((), (), s32[]{:S(2)}) async-start(), calls=%async_computation.7 | async-start | bytes 2621440 | tf_op jit(solution)/shard_map/reduce_scatter | solution.py:1046
  134.1 15.8 %collective-permute-start.22 = (bf16[4,16,2048]{2,1,0:T(8,128)(2,1)S(1)}, bf16[4,16,2048]{2,1,0:T(8,128)(2,1)}, u32[]{:S(2)}, u32[]{:S(2)}) collective-permute-start(bf16[4,16,2048]{2,1,0:T(8,128)(2,1)S(1)} %slice.78.refs_4_), channel_id=1, source_target_pairs={{0,17},{1,16},{2,19},{3,18},{4,21},{5,20},{6,23},{7,22},{8,25},{9,... | collective-permute-start | bytes 786440 | tf_op jit(solution)/shard_map/ppermute | solution.py:324
  135.2 23.0 %collective-permute-start.23 = (bf16[4,16,2048]{2,1,0:T(8,128)(2,1)S(1)}, bf16[4,16,2048]{2,1,0:T(8,128)(2,1)}, u32[]{:S(2)}, u32[]{:S(2)}) collective-permute-start(bf16[4,16,2048]{2,1,0:T(8,128)(2,1)S(1)} %slice.78.refs_4_), channel_id=1, source_target_pairs={{0,8},{1,9},{2,10},{3,11},{4,12},{5,13},{6,14},{7,15},{8,0},{9,1},... | collective-permute-start | bytes 786440 | tf_op jit(solution)/shard_map/ppermute | solution.py:324
  164.7 17.1 %collective-permute-start.27 = (bf16[192,1024]{1,0:T(8,128)(2,1)}, bf16[192,1024]{1,0:T(8,128)(2,1)S(1)}, u32[]{:S(2)}, u32[]{:S(2)}) collective-permute-start(bf16[192,1024]{1,0:T(8,128)(2,1)} %get-tuple-element.122.refs_0_), channel_id=1, source_target_pairs={{0,1},{1,0},{2,3},{3,2},{4,5},{5,4},{6,7},{7,6},{8,9},{9,8},{10,11... | collective-permute-start | bytes 1179656 | tf_op jit(solution)/shard_map/ppermute | solution.py:324
  165.6 18.0 %collective-permute-start.28 = (bf16[192,1024]{1,0:T(8,128)(2,1)}, bf16[192,1024]{1,0:T(8,128)(2,1)S(1)}, u32[]{:S(2)}, u32[]{:S(2)}) collective-permute-start(bf16[192,1024]{1,0:T(8,128)(2,1)} %get-tuple-element.122.refs_0_), channel_id=1, source_target_pairs={{0,16},{1,17},{2,18},{3,19},{4,20},{5,21},{6,22},{7,23},{8,24},{9,... | collective-permute-start | bytes 1179656 | tf_op jit(solution)/shard_map/ppermute | solution.py:324
  166.7 26.7 %collective-permute-start.29 = (bf16[192,1024]{1,0:T(8,128)(2,1)}, bf16[192,1024]{1,0:T(8,128)(2,1)S(1)}, u32[]{:S(2)}, u32[]{:S(2)}) collective-permute-start(bf16[192,1024]{1,0:T(8,128)(2,1)} %get-tuple-element.122.refs_0_), channel_id=1, source_target_pairs={{0,17},{1,16},{2,19},{3,18},{4,21},{5,20},{6,23},{7,22},{8,25},{9,... | collective-permute-start | bytes 1179656 | tf_op jit(solution)/shard_map/ppermute | solution.py:324
  168.3 25.1 %collective-permute-start.30 = (bf16[192,1024]{1,0:T(8,128)(2,1)}, bf16[192,1024]{1,0:T(8,128)(2,1)S(1)}, u32[]{:S(2)}, u32[]{:S(2)}) collective-permute-start(bf16[192,1024]{1,0:T(8,128)(2,1)} %get-tuple-element.122.refs_0_), channel_id=1, source_target_pairs={{0,8},{1,9},{2,10},{3,11},{4,12},{5,13},{6,14},{7,15},{8,0},{9,1},... | collective-permute-start | bytes 1179656 | tf_op jit(solution)/shard_map/ppermute | solution.py:324
  207.4 17.1 %collective-permute-start.34 = (bf16[192,1024]{1,0:T(8,128)(2,1)S(1)}, bf16[192,1024]{1,0:T(8,128)(2,1)S(1)}, u32[]{:S(2)}, u32[]{:S(2)}) collective-permute-start(bf16[192,1024]{1,0:T(8,128)(2,1)S(1)} %get-tuple-element.128), channel_id=1, source_target_pairs={{0,8},{1,9},{2,10},{3,11},{4,12},{5,13},{6,14},{7,15},{8,0},{9,1},... | collective-permute-start | bytes 1179656 | tf_op jit(solution)/shard_map/ppermute | solution.py:324
  208.7 15.9 %collective-permute-start.40 = (bf16[192,1024]{1,0:T(8,128)(2,1)S(1)}, bf16[192,1024]{1,0:T(8,128)(2,1)S(1)}, u32[]{:S(2)}, u32[]{:S(2)}) collective-permute-start(bf16[192,1024]{1,0:T(8,128)(2,1)S(1)} %add_convert_fusion.1), channel_id=1, source_target_pairs={{0,17},{1,16},{2,19},{3,18},{4,21},{5,20},{6,23},{7,22},{8,25},{9,... | collective-permute-start | bytes 1179656 | tf_op jit(solution)/shard_map/ppermute | solution.py:324
  209.6 19.4 %collective-permute-start.38 = (bf16[192,1024]{1,0:T(8,128)(2,1)S(1)}, bf16[192,1024]{1,0:T(8,128)(2,1)S(1)}, u32[]{:S(2)}, u32[]{:S(2)}) collective-permute-start(bf16[192,1024]{1,0:T(8,128)(2,1)S(1)} %add_convert_fusion.2), channel_id=1, source_target_pairs={{0,16},{1,17},{2,18},{3,19},{4,20},{5,21},{6,22},{7,23},{8,24},{9,... | collective-permute-start | bytes 1179656 | tf_op jit(solution)/shard_map/ppermute | solution.py:324
  210.9 18.1 %collective-permute-start.36 = (bf16[192,1024]{1,0:T(8,128)(2,1)S(1)}, bf16[192,1024]{1,0:T(8,128)(2,1)S(1)}, u32[]{:S(2)}, u32[]{:S(2)}) collective-permute-start(bf16[192,1024]{1,0:T(8,128)(2,1)S(1)} %add_convert_fusion.3), channel_id=1, source_target_pairs={{0,1},{1,0},{2,3},{3,2},{4,5},{5,4},{6,7},{7,6},{8,9},{9,8},{10,11... | collective-permute-start | bytes 1179656 | tf_op jit(solution)/shard_map/ppermute | solution.py:324
  240.5 27.0 %all-to-all-start.2 = ((bf16[8,192,128]{2,1,0:T(8,128)(2,1)}), bf16[8,192,128]{2,1,0:T(8,128)(2,1)S(1)}, u32[]{:S(2)}, u32[]{:S(2)}) async-start(bf16[8,192,128]{2,1,0:T(8,128)(2,1)} %get-tuple-element.141), calls=%async_computation.2 | async-start | bytes 786432 | tf_op jit(solution)/shard_map/all_to_all | solution.py:1004
  250.7 38.9 %collective-permute-start.43 = (bf16[256,1152]{1,0:T(8,128)(2,1)}, bf16[256,1152]{1,0:T(8,128)(2,1)}, u32[]{:S(2)}, u32[]{:S(2)}) collective-permute-start(bf16[256,1152]{1,0:T(8,128)(2,1)} %get-tuple-element.146), channel_id=1, source_target_pairs={{0,16},{1,17},{2,18},{3,19},{4,20},{5,21},{6,22},{7,23},{8,24},{9,... | collective-permute-start | bytes 1769480 | tf_op jit(solution)/shard_map/ppermute | solution.py:324
  293.5 20.0 %collective-permute-start.44 = (bf16[1536,256]{1,0:T(8,128)(2,1)S(1)}, bf16[1536,256]{1,0:T(8,128)(2,1)S(1)}, u32[]{:S(2)}, u32[]{:S(2)}) collective-permute-start(bf16[1536,256]{1,0:T(8,128)(2,1)S(1)} %add_convert_fusion), channel_id=1, source_target_pairs={{0,16},{1,17},{2,18},{3,19},{4,20},{5,21},{6,22},{7,23},{8,24},{9,... | collective-permute-start | bytes 2359304 | tf_op jit(solution)/shard_map/ppermute | solution.py:324
  313.5 26.1 %collective-permute-start.46 = (bf16[4,192,1024]{2,1,0:T(8,128)(2,1)}, bf16[4,192,1024]{2,1,0:T(8,128)(2,1)}, u32[]{:S(2)}, u32[]{:S(2)}) collective-permute-start(bf16[4,192,1024]{2,1,0:T(8,128)(2,1)} %get-tuple-element.169), channel_id=1, source_target_pairs={{0,8},{1,9},{2,10},{3,11},{4,12},{5,13},{6,14},{7,15},{8,0},{9,1},... | collective-permute-start | bytes 4718600 | tf_op jit(solution)/shard_map/ppermute | solution.py:324
  328.7 24.2 %all-to-all-start.3 = ((bf16[8,192,256]{2,1,0:T(8,128)(2,1)}), bf16[8,192,256]{2,1,0:T(8,128)(2,1)S(1)}, u32[]{:S(2)}, u32[]{:S(2)}) async-start(bf16[8,192,256]{2,1,0:T(8,128)(2,1)} %get-tuple-element.170), calls=%async_computation.4 | async-start | bytes 1572864 | tf_op jit(solution)/shard_map/all_to_all | solution.py:1068
  335.8 24.5 %collective-permute-start.53 = (bf16[64,1152]{1,0:T(8,128)(2,1)}, bf16[64,1152]{1,0:T(8,128)(2,1)S(1)}, u32[]{:S(2)}, u32[]{:S(2)}) collective-permute-start(bf16[64,1152]{1,0:T(8,128)(2,1)} %get-tuple-element.187), channel_id=1, source_target_pairs={{0,2},{1,3},{2,0},{3,1},{4,6},{5,7},{6,4},{7,5},{8,10},{9,11},{10,... | collective-permute-start | bytes 442376 | tf_op jit(solution)/shard_map/ppermute | solution.py:324
  337.8 15.2 %collective-permute-start.49 = (bf16[8,32,256]{2,1,0:T(8,128)(2,1)S(1)}, bf16[8,32,256]{2,1,0:T(8,128)(2,1)S(1)}, u32[]{:S(2)}, u32[]{:S(2)}) collective-permute-start(bf16[8,32,256]{2,1,0:T(8,128)(2,1)S(1)} %copy-done.54), channel_id=1, source_target_pairs={{0,16},{1,17},{2,18},{3,19},{4,20},{5,21},{6,22},{7,23},{8,24},{9,... | collective-permute-start | bytes 393224 | tf_op jit(solution)/shard_map/ppermute | solution.py:324
  344.5 24.8 %collective-permute-start.47 = (bf16[2,192,1024]{2,1,0:T(8,128)(2,1)}, bf16[2,192,1024]{2,1,0:T(8,128)(2,1)}, u32[]{:S(2)}, u32[]{:S(2)}) collective-permute-start(bf16[2,192,1024]{2,1,0:T(8,128)(2,1)} %slice.80), channel_id=1, source_target_pairs={{0,1},{1,0},{2,3},{3,2},{4,5},{5,4},{6,7},{7,6},{8,9},{9,8},{10,11... | collective-permute-start | bytes 2359304 | tf_op jit(solution)/shard_map/ppermute | solution.py:324
  356.1 25.7 %all-to-all-start.4 = ((bf16[8,32,256]{2,1,0:T(8,128)(2,1)}), bf16[8,32,256]{2,1,0:T(8,128)(2,1)}, u32[]{:S(2)}, u32[]{:S(2)}) async-start(bf16[8,32,256]{2,1,0:T(8,128)(2,1)} %sum_rows.1), calls=%async_computation.5 | async-start | bytes 262144 | tf_op jit(solution)/shard_map/all_to_all | solution.py:1087
  364.1 15.4 %collective-permute-start.54 = (bf16[32,1152]{1,0:T(8,128)(2,1)}, bf16[32,1152]{1,0:T(8,128)(2,1)}, u32[]{:S(2)}, u32[]{:S(2)}) collective-permute-start(bf16[32,1152]{1,0:T(8,128)(2,1)} %get-tuple-element.190), channel_id=1, source_target_pairs={{0,4},{1,5},{2,6},{3,7},{4,0},{5,1},{6,2},{7,3},{8,12},{9,13},{10,... | collective-permute-start | bytes 221192 | tf_op jit(solution)/shard_map/ppermute | solution.py:324
  (90 other events, 712.7 us)
Sparse Core Ops, SparseCore 0:
  35.7 49.9 all-gather.5
  124.8 71.1 all-gather.3
  240.6 49.4 reduce-scatter.1

commit v3 on v2

--- a/solution.py
+++ b/solution.py
@@ -517,14 +517,14 @@
     return counts.astype(F32)
 
 
-def forward_kernel(*refs, tile, own, last):
+def forward_kernel(*refs, tile, parts, own, last):
     q_ref, n_ref, qid_ref, kid_ref = refs[:4]
-    kv_refs = refs[4:6]
-    acc_in = None if own else refs[6]
-    place_ref = refs[6 + (not own)] if last else None
+    kv_refs = refs[4 : 4 + parts]
+    acc_in = None if own else refs[4 + parts]
+    place_ref = refs[5 + parts] if last else None
     acc_ref = refs[-2] if last else refs[-1]
     step = pl.program_id(0)
-    steps = pl.num_programs(0) // 2
+    steps = pl.num_programs(0) // parts
 
     @pl.when(step == 0)
     def _():
@@ -542,36 +542,36 @@
             counts = pair_count(qid_ref[rows, :], kid_ref[0:1, :], kid_ref[2:3, :], diagonal)
             acc_ref[rows, :] += dot((powers * counts).astype(BF16), values)
 
-    @pl.when(step < steps)
-    def _():
-        part(kv_refs[0], step if own else None)
-
-    @pl.when(step >= steps)
-    def _():
-        part(kv_refs[1], None)
+    for number, kv_ref in enumerate(kv_refs):
+
+        @pl.when(step // steps == number)
+        def _(kv_ref=kv_ref, diagonal_at=step if own and number == 0 else None):
+            part(kv_ref, diagonal_at)
 
     if last:
         send_ref = refs[-1]
         rows = send_ref.shape[1]
 
-        @pl.when(step == 2 * steps - 1)
+        @pl.when(step == parts * steps - 1)
         def _():
             for j in range(NH):
                 block = acc_ref[j * rows : (j + 1) * rows, :]
                 send_ref[place_ref[1] ^ j] = (block[:, :DH] / block[:, DH:]).astype(BF16)
 
 
-def forward_call(queries, norms, ids, kv_pair, part, acc, place=None, tk=768, tile=256):
-    nq, nk = queries.shape[0], kv_pair[0].shape[0]
+def forward_call(queries, norms, ids, kvs, part, acc, place=None, tk=768, tile=256):
+    nq, nk = queries.shape[0], kvs[0].shape[0]
     steps = nk // tk
     column = pl.BlockSpec((nq, 1), lambda j: (0, 0))
     full = pl.BlockSpec((nq, DH), lambda j: (0, 0))
-    first = pl.BlockSpec((tk, 2 * DH), lambda j: (jnp.minimum(j, steps - 1), 0))
-    second = pl.BlockSpec((tk, 2 * DH), lambda j: (jnp.maximum(j - steps, 0), 0))
+    keyed = [
+        pl.BlockSpec((tk, 2 * DH), lambda j, n=n: (jnp.clip(j - n * steps, 0, steps - 1), 0))
+        for n in range(len(kvs))
+    ]
     wide = pl.BlockSpec((nq, 2 * DH), lambda j: (0, 0))
     listed = pl.BlockSpec((8, tk), lambda j: (0, part * steps + j))
-    inputs = [queries, norms, ids[0], ids[1], *kv_pair]
-    specs = [full, column, column, listed, first, second]
+    inputs = [queries, norms, ids[0], ids[1], *kvs]
+    specs = [full, column, column, listed, *keyed]
     out_shape, out_specs = [shaped(nq, 2 * DH, dtype=F32)], [wide]
     if acc is not None:
         inputs.append(acc)
@@ -582,12 +582,14 @@
         out_shape.append(shaped(NH, nq // NH, DH))
         out_specs.append(pl.BlockSpec((NH, nq // NH, DH), lambda j: (0, 0, 0)))
     return pl.pallas_call(
-        functools.partial(forward_kernel, tile=tile, own=acc is None, last=place is not None),
-        grid=(2 * steps,),
+        functools.partial(
+            forward_kernel, tile=tile, parts=len(kvs), own=acc is None, last=place is not None
+        ),
+        grid=(len(kvs) * steps,),
         in_specs=specs,
         out_specs=out_specs,
         out_shape=out_shape,
-        input_output_aliases={} if acc is None else {6: 0},
+        input_output_aliases={} if acc is None else {4 + len(kvs): 0},
         compiler_params=pltpu.CompilerParams(vmem_limit_bytes=56 * 2**20),
         name="attention_forward",
     )(*inputs)
@@ -922,7 +924,7 @@
     )[0]
     ids_both = (ids_column, ids_rows)
 
-    columns[0] = after(columns[0], *ids_both)
+    columns[0] = after(columns[0], *ids_both, cotangent_y)
     normed, queries, kv, norms, norm_row, gain_rows = call(
         project_kernel,
         [Far(blocks[0]), *blocks[1:], *columns],
@@ -941,15 +943,17 @@
         scratch=[pltpu.VMEM((width, 3 * DH), BF16)],
     )
     kv_parts = shares(kv)
+    near, near_y = after(grad_second, kv), after(cotangent_y, kv)
+    cotangents = [near, swap(near, X), near_y, swap(near_y, X)]
     acc, = forward_call(queries, norms, ids_both, kv_parts[:2], 0, None)
-    kv_parts[3] = swap(after(kv_parts[2], acc), CORE)
-    near, near_y = after(grad_second, kv_parts[3]), after(cotangent_y, kv_parts[3])
-    cotangents = [near, swap(near, X), near_y, swap(near_y, X)]
-    acc, attn_send = forward_call(queries, norms, ids_both, kv_parts[2:], 2, acc, place)
-    attn_send = after(attn_send, *cotangents)
-    out_parts = gather_xy(after(weights, attn_send)[:, own_units:])
+    kv_parts[2] = after(kv_parts[2], acc, *cotangents)
+    kv_parts[3] = swap(kv_parts[2], CORE)
+    qv_full = lax.all_gather(after(qv_rows, kv_parts[2]), BITS, axis=0, tiled=True)
+    acc, = forward_call(queries, norms, ids_both, kv_parts[2:3], 2, acc)
+    out_near = near_xy(after(weights, acc)[:, own_units:])
+    acc, attn_send = forward_call(queries, norms, ids_both, kv_parts[3:], 3, acc, place)
+    out_parts = with_cores([after(a, attn_send) for a in out_near])
     cotangents = with_cores([after(a, attn_send) for a in cotangents])
-    qv_full = lax.all_gather(after(qv_rows, attn_send), BITS, axis=0, tiled=True)
     attn_tok = lax.all_to_all(attn_send, HEAD_AXES, 0, 0, tiled=True)
     units = own_units * 4
     hidden_back = call(
@@ -1025,11 +1029,14 @@
             scalars=[place],
         )
 
+    ffn_far = swap(after(ffn_far, grad_mid), CORE)
     keep, move = halve(keep, swap(move, CORE), 4, 1)
     came = swap(move, Y)
+    ffn_sum = ffn_near.astype(F32) + ffn_far.astype(F32)
+    ffn_move = ffn_sum[1::2].astype(BF16)
     grads, term_row = call(
         turn_kernel,
-        [after(grad_attn, move), Far(acc)],
+        [after(grad_attn, move, ffn_move), Far(acc)],
         [shaped(wide_rows, DH), shaped(8, wide_rows, dtype=F32)],
         "turn",
         far_out=(0, 1),
@@ -1042,7 +1049,6 @@
             queries, grads, norm_row, term_row, ids_both, kv_parts[part : part + 2], part, acc
         )
 
-    ffn_far = swap(after(ffn_far, grads), CORE)
     grad_ffn = lax.psum_scatter(
         grad_ffn, ("z_hi", "z_lo"), scatter_dimension=0, tiled=True
     )
@@ -1050,7 +1056,8 @@
     far = swap(far, CORE)
     keep, move = halve(keep, after(came, direct), 0, 4)
     over_y = (over_y.astype(F32) + after(far, move).astype(F32)).astype(BF16)
-    direct = after(direct, over_y)
+    ffn_move = swap(ffn_move, X)
+    direct = after(direct, over_y, ffn_move)
     over_y = swap(over_y, Y)
     came = swap(move, X)
     direct, grad_kv, over_core = backward(0, direct)
@@ -1078,13 +1085,21 @@
     rows_parts = grad_rows
     grad_rows = call(
         sum_kernel,
-        [after(part, arrived) for part in sum_shares(grad_rows)],
+        sum_shares(grad_rows),
         [shaped(NH, own_rows, 2 * DH)],
         "sum_rows",
         scalars=[place],
     )
     rows_send = grad_rows[0]
-    grad_rows = lax.all_to_all(rows_send, HEAD_AXES, 0, 0, tiled=True)
+    grad_up, grad_down = call(
+        unpack_kernel,
+        [Far(after(grad_ffn, rows_send))],
+        [shaped(width, own_units, dtype=F32), shaped(own_units, width, dtype=F32)],
+        "unpack",
+        far_out=(0, 1),
+    )
+    arrived = after(arrived, rows_send, grad_up)
+    grad_rows = lax.all_to_all(after(rows_send, arrived), HEAD_AXES, 0, 0, tiled=True)
     grad_second_half = call(
         last_kernel,
         [arrived, *map(Far, (second_half, grad_second, gain_rows, qv_full))],
@@ -1093,21 +1108,12 @@
         far_out=(0,),
     )[0]
 
-    keep, move = halve(keep, after(came, rows_parts[0]), 1, 2)
-    keep, move = halve(keep, after(swap(move, Z_LO), rows_send), 2, 1)
+    keep, move = halve(keep, after(came, rows_send), 1, 2)
+    keep, move = halve(keep, after(swap(move, Z_LO), arrived), 2, 1)
     grad_out = keep.astype(F32) + swap(move, Z_HI).astype(F32)
-    ffn_sum = after(ffn_near, rows_parts[0]).astype(F32) + ffn_far.astype(F32)
-    ffn_move = swap(ffn_sum[1::2].astype(BF16), X)
     ffn_sum = ffn_sum[0::2] + after(ffn_move, rows_send).astype(F32)
-    ffn_sum = ffn_sum[0] + swap(ffn_sum[1].astype(BF16), Y).astype(F32)
+    ffn_sum = ffn_sum[0] + after(swap(ffn_sum[1].astype(BF16), Y), arrived).astype(F32)
     second_out = second_half.astype(F32) + ffn_sum
-    grad_up, grad_down = call(
-        unpack_kernel,
-        [Far(after(grad_ffn, arrived))],
-        [shaped(width, own_units, dtype=F32), shaped(own_units, width, dtype=F32)],
-        "unpack",
-        far_out=(0, 1),
-    )
     grad_qk, grad_value, grad_attn_gain = call(
         own_rows_kernel,
         [after(grad_rows, grad_second_half, grad_up), Far(qk_weight), Far(value_weight), Far(gains)],

time: 403 us -> 373 us (0.926)
  waiting for transfers between devices: 118 us -> 89.9 us
  other arithmetic: 13.1 us -> 8.23 us
    ppermute x55, waiting for transfers between devices: 92.8 us -> 69 us  [swap(): return lax.ppermute(value, BITS, [(i, i ^ mask) for i in range(32)])]
    pallas_call x2 -> x3, Pallas kernels: 26.2 us -> 29.2 us  [forward_call(): pl.pallas_call(functools.partial(forward_kernel, tile=tile, parts=len(kvs...]
    unnamed x118 -> x120, local copies, waits for them, and re-layouts: 12.2 us -> 14.7 us
  transfers between devices with their start and end apart: 63 -> 63, of which waited for: 23 -> 22; matrix products, arithmetic and copies ran while one was open for 5% -> 4% of each run, Pallas kernels for 39% -> 39%
where the time goes in v3:
time: 373 us; the launch traced here: 366 us
  Pallas kernels  167 us (45%)
  waiting for transfers between devices  89.9 us (24%)
  starting transfers between devices  64.3 us (17%)
  local copies, waits for them, and re-layouts  22 us (6%)
  between operations  15 us (4%)
  other arithmetic  8.23 us (2%)
    pallas_call x20, Pallas kernels, call(): pl.pallas_call(body, in_specs=[SMEM] * len(scalars) + [far if i in far_in...  102 us
    ppermute x55, waiting for transfers between devices, swap(): return lax.ppermute(value, BITS, [(i, i ^ mask) for i in range(32)])  69 us
    ppermute x55, starting transfers between devices, swap(): return lax.ppermute(value, BITS, [(i, i ^ mask) for i in range(32)])  41.1 us
    pallas_call x2, Pallas kernels, backward_call(): pl.pallas_call(functools.partial(backward_kernel, tile=tile, own=acc is n...  35.7 us
    pallas_call x3, Pallas kernels, forward_call(): pl.pallas_call(functools.partial(forward_kernel, tile=tile, parts=len(kvs...  29.2 us
    unnamed x120, local copies, waits for them, and re-layouts  14.7 us
    all_to_all x1, waiting for transfers between devices, cube_plan(): grad_attn = lax.all_to_all(grad_attn, HEAD_AXES, 0, 0, tiled=True)  12.1 us
  transfers between devices with their start and end apart: 63, of which 22 were waited for; matrix products, arithmetic and copies ran while one was open for 4% of the time, Pallas kernels for 39%

profile of v3, /device:TPU:0, one launch (start us, length us, event | category | flops | bytes accessed | tf_op | source)
XLA Modules:
  0.0 366.2 jit_solution(1798349957049371504)
XLA Ops:
  7.2 4.1 %collective-permute-start.3 = (bf16[192,1024]{1,0:T(8,128)(2,1)}, bf16[192,1024]{1,0:T(8,128)(2,1)S(1)}, u32[]{:S(2)}, u32[]{:S(2)}) collective-permute-start(bf16[192,1024]{1,0:T(8,128)(2,1)} %refs_1_.6), channel_id=1, source_target_pairs={{0,4},{1,5},{2,6},{3,7},{4,0},{5,1},{6,2},{7,3},{8,12},{9,13},{10,... | collective-permute-start | bytes 1179656 | tf_op jit(solution)/shard_map/ppermute | solution.py:324
  26.3 3.9 %collective-permute-done.3.refs_5_ = bf16[192,1024]{1,0:T(8,128)(2,1)S(1)} collective-permute-done((bf16[192,1024]{1,0:T(8,128)(2,1)}, bf16[192,1024]{1,0:T(8,128)(2,1)S(1)}, u32[]{:S(2)}, u32[]{:S(2)}) %collective-permute-start.3) | collective-permute-done | bytes 393248 | tf_op jit(solution)/shard_map/ppermute | solution.py:324
  47.8 8.4 %collective-permute-done.2.refs_4_ = bf16[192,1024]{1,0:T(8,128)(2,1)S(1)} collective-permute-done((bf16[192,1024]{1,0:T(8,128)(2,1)S(1)}, bf16[192,1024]{1,0:T(8,128)(2,1)S(1)}, u32[]{:S(2)}, u32[]{:S(2)}) %collective-permute-start.2) | collective-permute-done | bytes 393248 | tf_op jit(solution)/shard_map/ppermute | solution.py:324
  56.3 8.1 %collective-permute-done.6.refs_8_ = bf16[192,1024]{1,0:T(8,128)(2,1)} collective-permute-done((bf16[192,1024]{1,0:T(8,128)(2,1)S(1)}, bf16[192,1024]{1,0:T(8,128)(2,1)}, u32[]{:S(2)}, u32[]{:S(2)}) %collective-permute-start.6) | collective-permute-done | bytes 393248 | tf_op jit(solution)/shard_map/ppermute | solution.py:324
  64.3 8.0 %project.1 = (bf16[1536,1024]{1,0:T(8,128)(2,1)}, bf16[1536,128]{1,0:T(8,128)(2,1)}, bf16[1536,256]{1,0:T(8,128)(2,1)}, f32[1536,1]{1,0:T(8,128)}, f32[8,1536]{1,0:T(8,128)}, /*index=5*/f32[8,1024]{1,0:T(8,128)}) custom-call(s32[2]{0:T(128)} %pad_add_fusion.refs_0_.refs_6_, bf16[192,1024]{1,0:T(8,128)(2,1)} %refs_1_.6, bf16[192,1024]{1,0:T(8,128)(2,1)} %copy-done.34, ...), custom_call_target="tpu_custom_call" | custom-call | tf_op jit(solution)/shard_map/project/pallas_call | solution.py:370
  76.0 13.3 %attention_forward.3.refs_5_ = f32[1536,256]{1,0:T(8,128)} custom-call(bf16[1536,128]{1,0:T(8,128)(2,1)} %get-tuple-element.105.refs_0_.refs_2_, f32[1536,1]{1,0:T(8,128)} %get-tuple-element.106.refs_1_.refs_3_, s32[6144,1]{1,0:T(8,128)} %ids.1.refs_2_.refs_5_, s32[8,6144]{1,0:T(8,128)} %add_add_fusion.refs_0_.refs_3_.refs_4_, ...), custom_call_target="tpu_custom_call" | custom-call | tf_op jit(solution)/shard_map/attention_forward/pallas_call | solution.py:584
  93.7 7.8 %attention_forward.4.refs_5_ = f32[1536,256]{1,0:T(8,128)} custom-call(bf16[1536,128]{1,0:T(8,128)(2,1)} %get-tuple-element.105.refs_0_.refs_2_, f32[1536,1]{1,0:T(8,128)} %get-tuple-element.106.refs_1_.refs_3_, s32[6144,1]{1,0:T(8,128)} %ids.1.refs_2_.refs_5_, s32[8,6144]{1,0:T(8,128)} %add_add_fusion.refs_0_.refs_3_.refs_4_, ...), custom_call_target="tpu_custom_call", output_to_operand_aliasing={{}: (5, {})} | custom-call | tf_op jit(solution)/shard_map/attention_forward/pallas_call | solution.py:584
  105.2 8.0 %attention_forward.5 = (f32[1536,256]{1,0:T(8,128)}, bf16[8,192,128]{2,1,0:T(8,128)(2,1)}) custom-call(bf16[1536,128]{1,0:T(8,128)(2,1)} %get-tuple-element.105.refs_0_.refs_2_, f32[1536,1]{1,0:T(8,128)} %get-tuple-element.106.refs_1_.refs_3_, s32[6144,1]{1,0:T(8,128)} %ids.1.refs_2_.refs_5_, ...), custom_call_target="tpu_custom_call", output_to_operand_aliasing={{0}: (5, {})} | custom-call | tf_op jit(solution)/shard_map/attention_forward/pallas_call | solution.py:584
  113.3 4.8 %all-to-all-start.1 = ((bf16[8,192,128]{2,1,0:T(8,128)(2,1)}), bf16[8,192,128]{2,1,0:T(8,128)(2,1)S(1)}, u32[]{:S(2)}, u32[]{:S(2)}) async-start(bf16[8,192,128]{2,1,0:T(8,128)(2,1)} %get-tuple-element.111), calls=%async_computation.1 | async-start | bytes 786432 | tf_op jit(solution)/shard_map/all_to_all | solution.py:957
  121.4 6.1 %collective-permute-done.21.refs_6_ = bf16[4,16,2048]{2,1,0:T(8,128)(2,1)S(1)} collective-permute-done((bf16[4,16,2048]{2,1,0:T(8,128)(2,1)S(1)}, bf16[4,16,2048]{2,1,0:T(8,128)(2,1)S(1)}, u32[]{:S(2)}, u32[]{:S(2)}) %collective-permute-start.21) | collective-permute-done | bytes 262176 | tf_op jit(solution)/shard_map/ppermute | solution.py:324
  127.5 6.8 %collective-permute-done.20.refs_5_ = bf16[4,16,2048]{2,1,0:T(8,128)(2,1)S(1)} collective-permute-done((bf16[4,16,2048]{2,1,0:T(8,128)(2,1)S(1)}, bf16[4,16,2048]{2,1,0:T(8,128)(2,1)S(1)}, u32[]{:S(2)}, u32[]{:S(2)}) %collective-permute-start.20) | collective-permute-done | bytes 262176 | tf_op jit(solution)/shard_map/ppermute | solution.py:324
  136.5 7.2 %hidden_back.1.refs_8_ = f32[1536,512]{1,0:T(8,128)} custom-call(bf16[192,1024]{1,0:T(8,128)(2,1)} %refs_2_.6, bf16[192,1024]{1,0:T(8,128)(2,1)} %copy-done.6, bf16[192,1024]{1,0:T(8,128)(2,1)} %copy-done.2, bf16[192,1024]{1,0:T(8,128)(2,1)} %copy-done.4, bf16[192,1024]{1,0:T(8,128)(2,1)} %copy-done.12, bf16[192,1024]{1,0:T(8,128)(2,1)} %copy-done.10, ...), custom_call_target="tpu_custom_call" | custom-call | tf_op jit(solution)/shard_map/hidden_back/pallas_call | solution.py:370
  144.9 5.9 %project_out.1 = (bf16[192,1024]{1,0:T(8,128)(2,1)}, f32[192,1024]{1,0:T(8,128)}, bf16[192,1024]{1,0:T(8,128)(2,1)}, bf16[1024,1024]{1,0:T(8,128)(2,1)}) custom-call(s32[2]{0:T(128)} %pad_add_fusion.refs_0_.refs_6_, bf16[8,192,128]{2,1,0:T(8,128)(2,1)} %copy-done.23, bf16[192,1024]{1,0:T(8,128)(2,1)} %refs_2_.5, ...), custom_call_target="tpu_custom_call" | custom-call | tf_op jit(solution)/shard_map/project_out/pallas_call | solution.py:370
  154.3 8.6 %collective-permute-done.27.refs_1_ = bf16[192,1024]{1,0:T(8,128)(2,1)S(1)} collective-permute-done((bf16[192,1024]{1,0:T(8,128)(2,1)}, bf16[192,1024]{1,0:T(8,128)(2,1)S(1)}, u32[]{:S(2)}, u32[]{:S(2)}) %collective-permute-start.27) | collective-permute-done | bytes 393248 | tf_op jit(solution)/shard_map/ppermute | solution.py:324
  163.5 7.7 %collective-permute-done.29.refs_3_ = bf16[192,1024]{1,0:T(8,128)(2,1)S(1)} collective-permute-done((bf16[192,1024]{1,0:T(8,128)(2,1)}, bf16[192,1024]{1,0:T(8,128)(2,1)S(1)}, u32[]{:S(2)}, u32[]{:S(2)}) %collective-permute-start.29) | collective-permute-done | bytes 393248 | tf_op jit(solution)/shard_map/ppermute | solution.py:324
  173.9 9.3 %feed_forward.1 = (bf16[192,1024]{1,0:T(8,128)(2,1)S(1)}, bf16[192,1024]{1,0:T(8,128)(2,1)S(1)}, bf16[192,1024]{1,0:T(8,128)(2,1)S(1)}, bf16[192,1024]{1,0:T(8,1...) custom-call(bf16[192,1024]{1,0:T(8,128)(2,1)S(1)} %copy-done.14, ...), custom_call_target="tpu_custom_call" | custom-call | tf_op jit(solution)/shard_map/feed_forward/pallas_call | solution.py:370
  190.4 11.7 %feed_forward_rest.1 = (bf16[4,192,1024]{2,1,0:T(8,128)(2,1)}, bf16[4,192,1024]{2,1,0:T(8,128)(2,1)}, bf16[512,2048]{1,0:T(8,128)(2,1)}) custom-call(bf16[192,1024]{1,0:T(8,128)(2,1)S(1)} %copy-done.15, bf16[192,1024]{1,0:T(8,128)(2,1)S(1)} %collective-permute-done.27.refs_1_, bf16[192,1024]{1,0:T(8,128)(2,1)S(1)} %collective-permute-done.28.refs_2_, ...), custom_call_target="tpu_custom_call" | custom-call | tf_op jit(solution)/shard_map/feed_forward_rest/pallas_call | solution.py:370
  202.2 4.7 %collective-permute-done.38.refs_3_ = bf16[192,1024]{1,0:T(8,128)(2,1)S(1)} collective-permute-done((bf16[192,1024]{1,0:T(8,128)(2,1)S(1)}, bf16[192,1024]{1,0:T(8,128)(2,1)S(1)}, u32[]{:S(2)}, u32[]{:S(2)}) %collective-permute-start.38) | collective-permute-done | bytes 393248 | tf_op jit(solution)/shard_map/ppermute | solution.py:324
  207.7 6.0 %mid.1 = (bf16[192,1024]{1,0:T(8,128)(2,1)}, bf16[8,192,128]{2,1,0:T(8,128)(2,1)}, f32[8,1024]{1,0:T(8,128)}) custom-call(bf16[192,1024]{1,0:T(8,128)(2,1)} %copy-done.18, bf16[192,1024]{1,0:T(8,128)(2,1)} %copy-done.37, bf16[192,1024]{1,0:T(8,128)(2,1)} %copy-done.41, bf16[192,1024]{1,0:T(8,128)(2,1)} %copy-done.40, bf16[192,1024]{1,0:T(8,128)(2,1)} %copy-done.39, ...), custom_call_target="tpu_custom_call" | custom-call | tf_op jit(solution)/shard_map/mid/pallas_call | solution.py:370
  213.7 4.6 %grad_out.1 = (bf16[512,1152]{1,0:T(8,128)(2,1)}, bf16[512,1152]{1,0:T(8,128)(2,1)}) custom-call(s32[2]{0:T(128)} %pad_add_fusion.refs_0_.refs_6_, bf16[8,192,128]{2,1,0:T(8,128)(2,1)} %copy-done.23, bf16[192,1024]{1,0:T(8,128)(2,1)} %get-tuple-element.94.refs_2_, f32[8,1024]{1,0:T(8,128)} %get-tuple-element.149.refs_3_), custom_call_target="tpu_custom_call" | custom-call | flops 99999997952 | bytes 1 | tf_op jit(solution)/shard_map/grad_out/pallas_call | solution.py:370
  219.7 5.8 %all-to-all-start.2 = ((bf16[8,192,128]{2,1,0:T(8,128)(2,1)}), bf16[8,192,128]{2,1,0:T(8,128)(2,1)S(1)}, u32[]{:S(2)}, u32[]{:S(2)}) async-start(bf16[8,192,128]{2,1,0:T(8,128)(2,1)} %get-tuple-element.148), calls=%async_computation.2 | async-start | bytes 786432 | tf_op jit(solution)/shard_map/all_to_all | solution.py:1008
  225.5 4.5 %halve.4 = (bf16[256,1152]{1,0:T(8,128)(2,1)}, bf16[256,1152]{1,0:T(8,128)(2,1)}) custom-call(s32[2]{0:T(128)} %pad_add_fusion.refs_0_.refs_6_, bf16[512,1152]{1,0:T(8,128)(2,1)} %get-tuple-element.150.refs_1_, bf16[512,1152]{1,0:T(8,128)(2,1)} %collective-permute-done.43.refs_2_), custom_call_target="tpu_custom_call" | custom-call | flops 99999997952 | bytes 1 | tf_op jit(solution)/shard_map/halve/pallas_call | solution.py:370
  236.3 12.1 %all-to-all-done.2.refs_1_ = bf16[8,192,128]{2,1,0:T(8,128)(2,1)S(1)} async-done(((bf16[8,192,128]{2,1,0:T(8,128)(2,1)}), bf16[8,192,128]{2,1,0:T(8,128)(2,1)S(1)}, u32[]{:S(2)}, u32[]{:S(2)}) %all-to-all-start.2) | async-done | bytes 393248 | tf_op jit(solution)/shard_map/all_to_all | solution.py:1008
  249.1 3.8 %turn.1 = (bf16[1536,128]{1,0:T(8,128)(2,1)}, f32[8,1536]{1,0:T(8,128)}) custom-call(s32[2]{0:T(128)} %pad_add_fusion.refs_0_.refs_6_, bf16[8,192,128]{2,1,0:T(8,128)(2,1)} %copy-done.42, f32[1536,256]{1,0:T(8,128)} %get-tuple-element.154.refs_2_), custom_call_target="tpu_custom_call" | custom-call | flops 99999997952 | bytes 1 | tf_op jit(solution)/shard_map/turn/pallas_call | solution.py:370
  253.0 17.4 %attention_backward.2 = (f32[1536,256]{1,0:T(8,128)}, bf16[1536,256]{1,0:T(8,128)(2,1)}, bf16[1536,256]{1,0:T(8,128)(2,1)}) custom-call(bf16[1536,128]{1,0:T(8,128)(2,1)} %get-tuple-element.105.refs_0_.refs_2_, bf16[1536,128]{1,0:T(8,128)(2,1)} %get-tuple-element.155.refs_1_, f32[8,1536]{1,0:T(8,128)} %get-tuple-element.156.refs_2_, ...), custom_call_target="tpu_custom_call" | custom-call | flops 99999997952 | bytes 1 | tf_op jit(solution)/shard_map/attention_backward/pallas_call | solution.py:649
  275.6 18.3 %attention_backward.3 = (f32[1536,256]{1,0:T(8,128)}, bf16[1536,256]{1,0:T(8,128)(2,1)}, bf16[1536,256]{1,0:T(8,128)(2,1)}) custom-call(bf16[1536,128]{1,0:T(8,128)(2,1)} %get-tuple-element.105.refs_0_.refs_2_, bf16[1536,128]{1,0:T(8,128)(2,1)} %get-tuple-element.155.refs_1_, f32[8,1536]{1,0:T(8,128)} %get-tuple-element.156.refs_2_, ...), custom_call_target="tpu_custom_call", output_to_operand_aliasing={{0}: (8, {})} | custom-call | flops 99999997952 | bytes 1 | tf_op jit(solution)/shard_map/attention_backward/pallas_call | solution.py:649
  297.7 6.0 %gather_grads.1 = (bf16[8,192,256]{2,1,0:T(8,128)(2,1)}, bf16[1536,256]{1,0:T(8,128)(2,1)}) custom-call(s32[2]{0:T(128)} %pad_add_fusion.refs_0_.refs_6_, f32[1536,256]{1,0:T(8,128)} %get-tuple-element.167.refs_1_, bf16[1536,128]{1,0:T(8,128)(2,1)} %get-tuple-element.105.refs_0_.refs_2_, f32[1536,1]{1,0:T(8,128)} %get-tuple-element.106.refs_1_.refs_3_, ...), custom_call_target="tpu_custom_call" | custom-call | flops 99999997952 | bytes 1 | tf_op jit(solution)/shard_map/gather_grads/pallas_call | solution.py:370
  303.7 4.7 %project_back.1 = (bf16[8,32,256]{2,1,0:T(8,128)(2,1)}, bf16[8,32,256]{2,1,0:T(8,128)(2,1)}, bf16[8,32,256]{2,1,0:T(8,128)(2,1)}, bf16[8,32,256]{2,1,0:T(8,128)(2,1)}) custom-call(s32[2]{0:T(128)} %pad_add_fusion.refs_0_.refs_6_, bf16[1536,1024]{1,0:T(8,128)(2,1)} %get-tuple-element.147.refs_1_, bf16[1536,256]{1,0:T(8,128)(2,1)} %get-tuple-element.171.refs_2_), custom_call_target="tpu_custom_call" | custom-call | flops 99999997952 | bytes 1 | tf_op jit(solution)/shard_map/project_back/pallas_call | solution.py:370
  311.8 4.2 %all-to-all-start.3 = ((bf16[8,192,256]{2,1,0:T(8,128)(2,1)}), bf16[8,192,256]{2,1,0:T(8,128)(2,1)}, u32[]{:S(2)}, u32[]{:S(2)}) async-start(bf16[8,192,256]{2,1,0:T(8,128)(2,1)} %get-tuple-element.177), calls=%async_computation.4 | async-start | bytes 1572864 | tf_op jit(solution)/shard_map/all_to_all | solution.py:1075
  331.4 5.4 %all-to-all-done.3.refs_0_ = bf16[8,192,256]{2,1,0:T(8,128)(2,1)} async-done(((bf16[8,192,256]{2,1,0:T(8,128)(2,1)}), bf16[8,192,256]{2,1,0:T(8,128)(2,1)}, u32[]{:S(2)}, u32[]{:S(2)}) %all-to-all-start.3) | async-done | bytes 786464 | tf_op jit(solution)/shard_map/all_to_all | solution.py:1075
  341.0 4.7 %all-to-all-start.4 = ((bf16[8,32,256]{2,1,0:T(8,128)(2,1)}), bf16[8,32,256]{2,1,0:T(8,128)(2,1)S(1)}, u32[]{:S(2)}, u32[]{:S(2)}) async-start(bf16[8,32,256]{2,1,0:T(8,128)(2,1)} %sum_rows.1), calls=%async_computation.5 | async-start | bytes 262144 | tf_op jit(solution)/shard_map/all_to_all | solution.py:1102
  345.7 6.3 %last.1 = bf16[192,1024]{1,0:T(8,128)(2,1)} custom-call(bf16[8,192,256]{2,1,0:T(8,128)(2,1)} %all-to-all-done.3.refs_0_, bf16[192,1024]{1,0:T(8,128)(2,1)} %refs_1_.6, bf16[192,1024]{1,0:T(8,128)(2,1)} %refs_2_.6, f32[8,1024]{1,0:T(8,128)} %get-tuple-element.119.refs_3_.refs_7_, bf16[1024,2048]{1,0:T(8,128)(2,1)} %all-gather.4.cloned.1.call-done.refs_4_), custom_call_target="tpu_custom_call" | custom-call | flops 99999997952 | bytes 1 | tf_op jit(solution)/shard_map/last/pallas_call | solution.py:370
  (278 shorter events, 113.0 us)
Async XLA Ops:
  7.2 23.0 %collective-permute-start.3 = (bf16[192,1024]{1,0:T(8,128)(2,1)}, bf16[192,1024]{1,0:T(8,128)(2,1)S(1)}, u32[]{:S(2)}, u32[]{:S(2)}) collective-permute-start(bf16[192,1024]{1,0:T(8,128)(2,1)} %refs_1_.6), channel_id=1, source_target_pairs={{0,4},{1,5},{2,6},{3,7},{4,0},{5,1},{6,2},{7,3},{8,12},{9,13},{10,... | collective-permute-start | bytes 1179656 | tf_op jit(solution)/shard_map/ppermute | solution.py:324
  11.3 24.6 %collective-permute-start.1 = (bf16[192,1024]{1,0:T(8,128)(2,1)}, bf16[192,1024]{1,0:T(8,128)(2,1)S(1)}, u32[]{:S(2)}, u32[]{:S(2)}) collective-permute-start(bf16[192,1024]{1,0:T(8,128)(2,1)} %refs_1_.6), channel_id=1, source_target_pairs={{0,2},{1,3},{2,0},{3,1},{4,6},{5,7},{6,4},{7,5},{8,10},{9,11},{10,... | collective-permute-start | bytes 1179656 | tf_op jit(solution)/shard_map/ppermute | solution.py:324
  12.9 23.9 %collective-permute-start = (bf16[192,1024]{1,0:T(8,128)(2,1)}, bf16[192,1024]{1,0:T(8,128)(2,1)S(1)}, u32[]{:S(2)}, u32[]{:S(2)}) collective-permute-start(bf16[192,1024]{1,0:T(8,128)(2,1)} %refs_1_.6), channel_id=1, source_target_pairs={{0,1},{1,0},{2,3},{3,2},{4,5},{5,4},{6,7},{7,6},{8,9},{9,8},{10,11... | collective-permute-start | bytes 1179656 | tf_op jit(solution)/shard_map/ppermute | solution.py:324
  18.7 15.4 %all-to-all-start = ((bf16[8,32,384]{2,1,0:T(8,128)(2,1)}), bf16[8,32,384]{2,1,0:T(8,128)(2,1)S(1)}, u32[]{:S(2)}, u32[]{:S(2)}) async-start(bf16[8,32,384]{2,1,0:T(8,128)(2,1)} %get-tuple-element.103), calls=%async_computation | async-start | bytes 393216 | tf_op jit(solution)/shard_map/all_to_all | solution.py:901
  22.1 79.4 %all-gather.6.cloned.1.call-start = ((), (), s32[]{:S(2)}) async-start(), calls=%async_computation.8 | async-start | bytes 2949120 | tf_op jit(solution)/shard_map/all_gather | solution.py:902
  22.1 13.7 %collective-permute-start.7 = (bf16[192,1024]{1,0:T(8,128)(2,1)}, bf16[192,1024]{1,0:T(8,128)(2,1)S(1)}, u32[]{:S(2)}, u32[]{:S(2)}) collective-permute-start(bf16[192,1024]{1,0:T(8,128)(2,1)} %refs_2_.6), channel_id=1, source_target_pairs={{0,16},{1,17},{2,18},{3,19},{4,20},{5,21},{6,22},{7,23},{8,24},{9,... | collective-permute-start | bytes 1179656 | tf_op jit(solution)/shard_map/ppermute | solution.py:324
  30.2 171.9 %all-gather.4.cloned.1.call-start = ((), (), s32[]{:S(2)}) async-start(), calls=%async_computation.6 | async-start | bytes 4325376 | tf_op jit(solution)/shard_map/all_gather | solution.py:951
  36.7 19.5 %collective-permute-start.2 = (bf16[192,1024]{1,0:T(8,128)(2,1)S(1)}, bf16[192,1024]{1,0:T(8,128)(2,1)S(1)}, u32[]{:S(2)}, u32[]{:S(2)}) collective-permute-start(bf16[192,1024]{1,0:T(8,128)(2,1)S(1)} %collective-permute-done.1.refs_3_), channel_id=1, source_target_pairs={{0,1},{1,0},{2,3},{3,2},{4,5},{5,4},{6,7},{7,6},{8,9},{9,8},{10,11... | collective-permute-start | bytes 1179656 | tf_op jit(solution)/shard_map/ppermute | solution.py:324
  40.9 23.4 %collective-permute-start.6 = (bf16[192,1024]{1,0:T(8,128)(2,1)S(1)}, bf16[192,1024]{1,0:T(8,128)(2,1)}, u32[]{:S(2)}, u32[]{:S(2)}) collective-permute-start(bf16[192,1024]{1,0:T(8,128)(2,1)S(1)} %collective-permute-done.5.refs_7_), channel_id=1, source_target_pairs={{0,1},{1,0},{2,3},{3,2},{4,5},{5,4},{6,7},{7,6},{8,9},{9,8},{10,11... | collective-permute-start | bytes 1179656 | tf_op jit(solution)/shard_map/ppermute | solution.py:324
  72.5 20.2 %collective-permute-start.11 = (bf16[1536,256]{1,0:T(8,128)(2,1)}, bf16[1536,256]{1,0:T(8,128)(2,1)S(1)}, u32[]{:S(2)}, u32[]{:S(2)}) collective-permute-start(bf16[1536,256]{1,0:T(8,128)(2,1)} %get-tuple-element.107.refs_4_.refs_6_), channel_id=1, source_target_pairs={{0,16},{1,17},{2,18},{3,19},{4,20},{5,21},{6,22},{7,23},{8,24},{9,... | collective-permute-start | bytes 2359304 | tf_op jit(solution)/shard_map/ppermute | solution.py:324
  73.1 16.2 %collective-permute-start.14 = (bf16[192,1024]{1,0:T(8,128)(2,1)S(1)}, bf16[192,1024]{1,0:T(8,128)(2,1)S(1)}, u32[]{:S(2)}, u32[]{:S(2)}) collective-permute-start(bf16[192,1024]{1,0:T(8,128)(2,1)S(1)} %collective-permute-done.7.refs_2_.refs_10_), channel_id=1, source_target_pairs={{0,1},{1,0},{2,3},{3,2},{4,5},{5,4},{6,7},{7,6},{8,9},{9,8},{10,11... | collective-permute-start | bytes 1179656 | tf_op jit(solution)/shard_map/ppermute | solution.py:324
  73.9 18.8 %collective-permute-start.13 = (bf16[192,1024]{1,0:T(8,128)(2,1)S(1)}, bf16[192,1024]{1,0:T(8,128)(2,1)S(1)}, u32[]{:S(2)}, u32[]{:S(2)}) collective-permute-start(bf16[192,1024]{1,0:T(8,128)(2,1)S(1)} %copy-done), channel_id=1, source_target_pairs={{0,1},{1,0},{2,3},{3,2},{4,5},{5,4},{6,7},{7,6},{8,9},{9,8},{10,11... | collective-permute-start | bytes 1179656 | tf_op jit(solution)/shard_map/ppermute | solution.py:324
  102.5 16.9 %collective-permute-start.22 = (bf16[4,16,2048]{2,1,0:T(8,128)(2,1)S(1)}, bf16[4,16,2048]{2,1,0:T(8,128)(2,1)}, u32[]{:S(2)}, u32[]{:S(2)}) collective-permute-start(bf16[4,16,2048]{2,1,0:T(8,128)(2,1)S(1)} %slice.78.refs_4_), channel_id=1, source_target_pairs={{0,17},{1,16},{2,19},{3,18},{4,21},{5,20},{6,23},{7,22},{8,25},{9,... | collective-permute-start | bytes 786440 | tf_op jit(solution)/shard_map/ppermute | solution.py:324
  113.3 30.5 %all-to-all-start.1 = ((bf16[8,192,128]{2,1,0:T(8,128)(2,1)}), bf16[8,192,128]{2,1,0:T(8,128)(2,1)S(1)}, u32[]{:S(2)}, u32[]{:S(2)}) async-start(bf16[8,192,128]{2,1,0:T(8,128)(2,1)} %get-tuple-element.111), calls=%async_computation.1 | async-start | bytes 786432 | tf_op jit(solution)/shard_map/all_to_all | solution.py:957
  118.1 176.2 %reduce-scatter.2.cloned.1.call-start = ((), (), s32[]{:S(2)}) async-start(), calls=%async_computation.7 | async-start | bytes 2621440 | tf_op jit(solution)/shard_map/reduce_scatter | solution.py:1052
  118.9 15.5 %collective-permute-start.19 = (bf16[192,1024]{1,0:T(8,128)(2,1)S(1)}, bf16[192,1024]{1,0:T(8,128)(2,1)S(1)}, u32[]{:S(2)}, u32[]{:S(2)}) collective-permute-start(bf16[192,1024]{1,0:T(8,128)(2,1)S(1)} %collective-permute-done.14.refs_3_.refs_11_), channel_id=1, source_target_pairs={{0,8},{1,9},{2,10},{3,11},{4,12},{5,13},{6,14},{7,15},{8,0},{9,1},... | collective-permute-start | bytes 1179656 | tf_op jit(solution)/shard_map/ppermute | solution.py:324
  118.9 16.0 %collective-permute-start.18 = (bf16[192,1024]{1,0:T(8,128)(2,1)S(1)}, bf16[192,1024]{1,0:T(8,128)(2,1)S(1)}, u32[]{:S(2)}, u32[]{:S(2)}) collective-permute-start(bf16[192,1024]{1,0:T(8,128)(2,1)S(1)} %collective-permute-done.7.refs_2_.refs_10_), channel_id=1, source_target_pairs={{0,8},{1,9},{2,10},{3,11},{4,12},{5,13},{6,14},{7,15},{8,0},{9,1},... | collective-permute-start | bytes 1179656 | tf_op jit(solution)/shard_map/ppermute | solution.py:324
  119.4 15.6 %collective-permute-start.17 = (bf16[192,1024]{1,0:T(8,128)(2,1)S(1)}, bf16[192,1024]{1,0:T(8,128)(2,1)S(1)}, u32[]{:S(2)}, u32[]{:S(2)}) collective-permute-start(bf16[192,1024]{1,0:T(8,128)(2,1)S(1)} %collective-permute-done.13.refs_1_.refs_9_), channel_id=1, source_target_pairs={{0,8},{1,9},{2,10},{3,11},{4,12},{5,13},{6,14},{7,15},{8,0},{9,1},... | collective-permute-start | bytes 1179656 | tf_op jit(solution)/shard_map/ppermute | solution.py:324
  119.4 14.9 %collective-permute-start.20 = (bf16[4,16,2048]{2,1,0:T(8,128)(2,1)S(1)}, bf16[4,16,2048]{2,1,0:T(8,128)(2,1)S(1)}, u32[]{:S(2)}, u32[]{:S(2)}) collective-permute-start(bf16[4,16,2048]{2,1,0:T(8,128)(2,1)S(1)} %slice.78.refs_4_), channel_id=1, source_target_pairs={{0,1},{1,0},{2,3},{3,2},{4,5},{5,4},{6,7},{7,6},{8,9},{9,8},{10,11... | collective-permute-start | bytes 786440 | tf_op jit(solution)/shard_map/ppermute | solution.py:324
  152.2 18.9 %collective-permute-start.29 = (bf16[192,1024]{1,0:T(8,128)(2,1)}, bf16[192,1024]{1,0:T(8,128)(2,1)S(1)}, u32[]{:S(2)}, u32[]{:S(2)}) collective-permute-start(bf16[192,1024]{1,0:T(8,128)(2,1)} %get-tuple-element.126.refs_0_), channel_id=1, source_target_pairs={{0,17},{1,16},{2,19},{3,18},{4,21},{5,20},{6,23},{7,22},{8,25},{9,... | collective-permute-start | bytes 1179656 | tf_op jit(solution)/shard_map/ppermute | solution.py:324
  154.3 16.8 %collective-permute-start.30 = (bf16[192,1024]{1,0:T(8,128)(2,1)}, bf16[192,1024]{1,0:T(8,128)(2,1)S(1)}, u32[]{:S(2)}, u32[]{:S(2)}) collective-permute-start(bf16[192,1024]{1,0:T(8,128)(2,1)} %get-tuple-element.126.refs_0_), channel_id=1, source_target_pairs={{0,8},{1,9},{2,10},{3,11},{4,12},{5,13},{6,14},{7,15},{8,0},{9,1},... | collective-permute-start | bytes 1179656 | tf_op jit(solution)/shard_map/ppermute | solution.py:324
  185.0 17.1 %collective-permute-start.34 = (bf16[192,1024]{1,0:T(8,128)(2,1)S(1)}, bf16[192,1024]{1,0:T(8,128)(2,1)S(1)}, u32[]{:S(2)}, u32[]{:S(2)}) collective-permute-start(bf16[192,1024]{1,0:T(8,128)(2,1)S(1)} %get-tuple-element.132), channel_id=1, source_target_pairs={{0,8},{1,9},{2,10},{3,11},{4,12},{5,13},{6,14},{7,15},{8,0},{9,1},... | collective-permute-start | bytes 1179656 | tf_op jit(solution)/shard_map/ppermute | solution.py:324
  186.3 15.9 %collective-permute-start.40 = (bf16[192,1024]{1,0:T(8,128)(2,1)S(1)}, bf16[192,1024]{1,0:T(8,128)(2,1)S(1)}, u32[]{:S(2)}, u32[]{:S(2)}) collective-permute-start(bf16[192,1024]{1,0:T(8,128)(2,1)S(1)} %add_convert_fusion.1), channel_id=1, source_target_pairs={{0,17},{1,16},{2,19},{3,18},{4,21},{5,20},{6,23},{7,22},{8,25},{9,... | collective-permute-start | bytes 1179656 | tf_op jit(solution)/shard_map/ppermute | solution.py:324
  188.8 18.0 %collective-permute-start.38 = (bf16[192,1024]{1,0:T(8,128)(2,1)S(1)}, bf16[192,1024]{1,0:T(8,128)(2,1)S(1)}, u32[]{:S(2)}, u32[]{:S(2)}) collective-permute-start(bf16[192,1024]{1,0:T(8,128)(2,1)S(1)} %add_convert_fusion.2), channel_id=1, source_target_pairs={{0,16},{1,17},{2,18},{3,19},{4,20},{5,21},{6,22},{7,23},{8,24},{9,... | collective-permute-start | bytes 1179656 | tf_op jit(solution)/shard_map/ppermute | solution.py:324
  190.3 16.6 %collective-permute-start.36 = (bf16[192,1024]{1,0:T(8,128)(2,1)S(1)}, bf16[192,1024]{1,0:T(8,128)(2,1)S(1)}, u32[]{:S(2)}, u32[]{:S(2)}) collective-permute-start(bf16[192,1024]{1,0:T(8,128)(2,1)S(1)} %add_convert_fusion.3), channel_id=1, source_target_pairs={{0,1},{1,0},{2,3},{3,2},{4,5},{5,4},{6,7},{7,6},{8,9},{9,8},{10,11... | collective-permute-start | bytes 1179656 | tf_op jit(solution)/shard_map/ppermute | solution.py:324
  219.7 28.6 %all-to-all-start.2 = ((bf16[8,192,128]{2,1,0:T(8,128)(2,1)}), bf16[8,192,128]{2,1,0:T(8,128)(2,1)S(1)}, u32[]{:S(2)}, u32[]{:S(2)}) async-start(bf16[8,192,128]{2,1,0:T(8,128)(2,1)} %get-tuple-element.148), calls=%async_computation.2 | async-start | bytes 786432 | tf_op jit(solution)/shard_map/all_to_all | solution.py:1008
  230.0 40.3 %collective-permute-start.45 = (bf16[256,1152]{1,0:T(8,128)(2,1)}, bf16[256,1152]{1,0:T(8,128)(2,1)}, u32[]{:S(2)}, u32[]{:S(2)}) collective-permute-start(bf16[256,1152]{1,0:T(8,128)(2,1)} %get-tuple-element.152), channel_id=1, source_target_pairs={{0,16},{1,17},{2,18},{3,19},{4,20},{5,21},{6,22},{7,23},{8,24},{9,... | collective-permute-start | bytes 1769480 | tf_op jit(solution)/shard_map/ppermute | solution.py:324
  234.3 41.3 %collective-permute-start.42 = (bf16[2,192,1024]{2,1,0:T(8,128)(2,1)}, bf16[2,192,1024]{2,1,0:T(8,128)(2,1)}, u32[]{:S(2)}, u32[]{:S(2)}) collective-permute-start(bf16[2,192,1024]{2,1,0:T(8,128)(2,1)} %slice.80), channel_id=1, source_target_pairs={{0,1},{1,0},{2,3},{3,2},{4,5},{5,4},{6,7},{7,6},{8,9},{9,8},{10,11... | collective-permute-start | bytes 2359304 | tf_op jit(solution)/shard_map/ppermute | solution.py:324
  274.3 20.0 %collective-permute-start.46 = (bf16[1536,256]{1,0:T(8,128)(2,1)S(1)}, bf16[1536,256]{1,0:T(8,128)(2,1)S(1)}, u32[]{:S(2)}, u32[]{:S(2)}) collective-permute-start(bf16[1536,256]{1,0:T(8,128)(2,1)S(1)} %add_convert_fusion), channel_id=1, source_target_pairs={{0,16},{1,17},{2,18},{3,19},{4,20},{5,21},{6,22},{7,23},{8,24},{9,... | collective-permute-start | bytes 2359304 | tf_op jit(solution)/shard_map/ppermute | solution.py:324
  311.8 25.0 %all-to-all-start.3 = ((bf16[8,192,256]{2,1,0:T(8,128)(2,1)}), bf16[8,192,256]{2,1,0:T(8,128)(2,1)}, u32[]{:S(2)}, u32[]{:S(2)}) async-start(bf16[8,192,256]{2,1,0:T(8,128)(2,1)} %get-tuple-element.177), calls=%async_computation.4 | async-start | bytes 1572864 | tf_op jit(solution)/shard_map/all_to_all | solution.py:1075
  330.1 15.6 %collective-permute-start.51 = (bf16[192,1024]{1,0:T(8,128)(2,1)S(1)}, bf16[192,1024]{1,0:T(8,128)(2,1)S(1)}, u32[]{:S(2)}, u32[]{:S(2)}) collective-permute-start(bf16[192,1024]{1,0:T(8,128)(2,1)S(1)} %fusion.3), channel_id=1, source_target_pairs={{0,16},{1,17},{2,18},{3,19},{4,20},{5,21},{6,22},{7,23},{8,24},{9,... | collective-permute-start | bytes 1179656 | tf_op jit(solution)/shard_map/ppermute | solution.py:324
  341.0 13.3 %all-to-all-start.4 = ((bf16[8,32,256]{2,1,0:T(8,128)(2,1)}), bf16[8,32,256]{2,1,0:T(8,128)(2,1)S(1)}, u32[]{:S(2)}, u32[]{:S(2)}) async-start(bf16[8,32,256]{2,1,0:T(8,128)(2,1)} %sum_rows.1), calls=%async_computation.5 | async-start | bytes 262144 | tf_op jit(solution)/shard_map/all_to_all | solution.py:1102
  (91 other events, 666.8 us)
Sparse Core Ops, SparseCore 0:
  30.3 51.4 all-gather.5
  92.8 68.3 all-gather.3
  218.5 50.3 reduce-scatter.1

commit v4 on v3

--- a/solution.py
+++ b/solution.py
@@ -337,7 +337,7 @@
         self.value = value
 
 
-def call(kernel, inputs, out_shape, name, far_out=(), mib=56, scalars=(), scratch=(), cost=LONG):
+def call(kernel, inputs, out_shape, name, far_out=(), mib=62, scalars=(), scratch=(), cost=LONG):
     far_in = [i for i, a in enumerate(inputs) if isinstance(a, Far)]
     arrays = [a.value if isinstance(a, Far) else a for a in inputs]
     first_in, first_out = len(scalars), len(scalars) + len(arrays)
@@ -397,8 +397,11 @@
 
 def gather_zx(value):
     low, high = swap(value, Z_LO), swap(value, Z_HI)
-    line = [value, low, high, swap(high, Z_LO)]
-    return [block for part in line for block in (part, swap(part, X))]
+    both = swap(high, Z_LO)
+    beside_low = swap(low, X)
+    beside_high = swap(after(high, beside_low), X)
+    beside_both = swap(after(both, beside_high), X)
+    return [value, swap(value, X), low, beside_low, high, beside_high, both, beside_both]
 
 
 def scatter_xy(blocks):
@@ -590,7 +593,7 @@
         out_specs=out_specs,
         out_shape=out_shape,
         input_output_aliases={} if acc is None else {4 + len(kvs): 0},
-        compiler_params=pltpu.CompilerParams(vmem_limit_bytes=56 * 2**20),
+        compiler_params=pltpu.CompilerParams(vmem_limit_bytes=62 * 2**20),
         name="attention_forward",
     )(*inputs)
 
@@ -653,7 +656,7 @@
         out_specs=[wide, first, second],
         out_shape=[shaped(nq, 2 * DH, dtype=F32), *[shaped(nk, 2 * DH)] * 2],
         input_output_aliases={8: 0} if more else {},
-        compiler_params=pltpu.CompilerParams(vmem_limit_bytes=56 * 2**20),
+        compiler_params=pltpu.CompilerParams(vmem_limit_bytes=62 * 2**20),
         cost_estimate=LONG,
         name="attention_backward",
     )(queries, grads, norms, terms, ids[1], ids[0], *kv_pair, *more)
@@ -726,21 +729,33 @@
     sum_ref[:, width:] = dot(hidden_ref[...], cotangents, TN).astype(BF16)
 
 
-def mid_kernel(*refs):
-    parts, rest, outs = refs[:5], refs[5:9], refs[9:]
-    out_ref, first_ref, gain_ref, weight_ref = rest
-    mid_ref, send_ref, gain_sum_ref = outs
+def mid_kernel(place_ref, *refs):
+    parts, rest, outs = refs[:5], refs[5:10], refs[10:]
+    out_ref, first_ref, gain_ref, weight_ref, attn_ref = rest
+    mid_ref, send_ref, keep_ref, move_ref = outs
     xhat, rstd = normalised(out_ref[...])
     grads = sum(part[...].astype(F32) for part in parts)
-    gain_sum_ref[...] = jnp.broadcast_to(
-        jnp.sum(grads * xhat, axis=0, keepdims=True), gain_sum_ref.shape
-    )
+    gain_sum = jnp.sum(grads * xhat, axis=0, keepdims=True)
     mid = first_ref[...].astype(F32) + norm_back(grads * gain_ref[1:2, :], xhat, rstd)
     mid = mid.astype(BF16)
     mid_ref[...] = mid
     grad_attn = dot(mid, weight_ref[...], NT).astype(BF16)
     for h in range(NH):
         send_ref[h] = grad_attn[:, h * DH : (h + 1) * DH]
+    width = mid_ref.shape[1]
+    heads = NH // 4
+    core = (place_ref[0] >> 3) & 1
+    gains = [
+        jnp.broadcast_to(gain_sum[:, h * DH : (h + 1) * DH], (DH, DH)).T for h in range(NH)
+    ]
+    for ref, bit in ((keep_ref, core), (move_ref, 1 - core)):
+        for i in range(NH // 2):
+            first, k = divmod(i, heads)
+            rows = slice(i * DH, (i + 1) * DH)
+            attn = attn_ref[(2 * first + bit) * heads + k]
+            ref[rows, :width] = dot(attn, mid, TN).astype(BF16)
+            low, high = (gains[(2 * first + b) * heads + k] for b in range(2))
+            ref[rows, width:] = jnp.where(bit == 0, low, high).astype(BF16)
 
 
 def turn_kernel(place_ref, arrived_ref, acc_ref, grads_ref, row_ref, column_ref):
@@ -758,23 +773,6 @@
     to_row(column_ref, row_ref)
 
 
-def grad_out_kernel(place_ref, attn_ref, mid_ref, gain_ref, keep_ref, send_ref):
-    width = mid_ref.shape[1]
-    heads = NH // 4
-    core = (place_ref[0] >> 3) & 1
-    gains = [
-        jnp.broadcast_to(gain_ref[0:1, h * DH : (h + 1) * DH], (DH, DH)).T for h in range(NH)
-    ]
-    for ref, bit in ((keep_ref, core), (send_ref, 1 - core)):
-        for i in range(NH // 2):
-            first, k = divmod(i, heads)
-            rows = slice(i * DH, (i + 1) * DH)
-            attn = attn_ref[(2 * first + bit) * heads + k]
-            ref[rows, :width] = dot(attn, mid_ref[...], TN).astype(BF16)
-            low, high = (gains[(2 * first + b) * heads + k] for b in range(2))
-            ref[rows, width:] = jnp.where(bit == 0, low, high).astype(BF16)
-
-
 def halve_kernel(place_ref, kept_ref, came_ref, keep_ref, send_ref, *, shift, blocks):
     rows = kept_ref.shape[0] // (2 * blocks)
     bit = (place_ref[0] >> shift) & 1
@@ -786,8 +784,16 @@
             ref[out, :] = total.astype(BF16)
 
 
-def gather_grads_kernel(place_ref, direct_ref, q_ref, n_ref, *refs):
-    kv_refs, (send_ref, both_ref) = refs[:3], refs[3:]
+def quarter_kernel(place_ref, kept_ref, came_ref, *outs):
+    rows = outs[0].shape[0]
+    for p, out in enumerate(outs):
+        start = pl.ds(pl.multiple_of((((place_ref[0] >> 1) & 3) ^ p) * rows, rows), rows)
+        total = kept_ref[start, :].astype(F32) + came_ref[start, :].astype(F32)
+        out[...] = total.astype(BF16)
+
+
+def gather_grads_kernel(place_ref, direct_ref, q_ref, n_ref, normed_ref, *refs):
+    kv_refs, (send_ref, *outs), (both_ref, sum_ref) = refs[:3], refs[3:8], refs[8:]
     rows = send_ref.shape[1]
     for j in range(NH):
         place = slice(j * rows, (j + 1) * rows)
@@ -805,10 +811,6 @@
         both = jnp.concatenate([grad_queries.astype(BF16), grad_values.astype(BF16)], axis=1)
         both_ref[place, :] = both
         send_ref[place_ref[1] ^ j] = both
-
-
-def project_back_kernel(place_ref, normed_ref, both_ref, *refs):
-    outs, sum_ref = refs[:4], refs[4]
     sum_ref[...] = dot(normed_ref[...], both_ref[...], TN)
     rows = outs[0].shape[1]
     for out, mask in zip(outs, PARTS, strict=True):
@@ -952,7 +954,6 @@
     acc, = forward_call(queries, norms, ids_both, kv_parts[2:3], 2, acc)
     out_near = near_xy(after(weights, acc)[:, own_units:])
     acc, attn_send = forward_call(queries, norms, ids_both, kv_parts[3:], 3, acc, place)
-    out_parts = with_cores([after(a, attn_send) for a in out_near])
     cotangents = with_cores([after(a, attn_send) for a in cotangents])
     attn_tok = lax.all_to_all(attn_send, HEAD_AXES, 0, 0, tiled=True)
     units = own_units * 4
@@ -964,7 +965,7 @@
         cost=None,
         far_out=(0,),
     )[0]
-    attn_tok = after(attn_tok, hidden_back)
+    out_parts = with_cores([after(a, hidden_back) for a in out_near])
     y_first, first_out, normed_ffn, out_full = call(
         out_kernel,
         [attn_tok, Far(first_half), Far(gain_rows), *out_parts],
@@ -977,46 +978,40 @@
     ffn_in = gather_xy(normed_ffn)
     *grad_blocks, hidden, grad_pre = call(
         ffn_kernel,
-        [*ffn_in, Far(hidden_back), Far(weights)],
+        [Far(ffn_in[0]), *ffn_in[1:], Far(hidden_back), Far(weights)],
         [row_block] * 8 + [shaped(wide_rows, units)] * 2,
         "feed_forward",
         cost=None,
         mib=44,
+        far_out=(8, 9),
     )
     grad_parts = scatter_xy(grad_blocks)
     ffn_near, ffn_far, grad_ffn = call(
         ffn_rest_kernel,
-        [*ffn_in, *map(Far, cotangents), hidden, grad_pre, Far(weights)],
+        [Far(ffn_in[0]), *ffn_in[1:], *map(Far, (*cotangents, hidden, grad_pre, weights))],
         [shaped(4, rows, width)] * 2 + [shaped(units, 2 * width)],
         "feed_forward_rest",
         cost=None,
         far_out=range(3),
         mib=48,
     )
-    grad_mid, grad_attn, gain_sum = call(
+    out_width = width + DH
+    half = shaped(width // 2, out_width)
+    grad_mid, grad_attn, keep, move = call(
         mid_kernel,
         [
             *grad_parts,
             *map(Far, (after(first_out, grad_ffn, qv_full), grad_first, gain_rows, out_full)),
+            Far(attn_tok),
         ],
-        [row_block, shaped(NH, rows, DH), shaped(8, width, dtype=F32)],
+        [row_block, shaped(NH, rows, DH), half, half],
         "mid",
         cost=None,
-        far_out=(0,),
+        far_out=(0, 2),
+        scalars=[place],
     )
 
     grad_attn = lax.all_to_all(grad_attn, HEAD_AXES, 0, 0, tiled=True)
-
-    out_width = width + DH
-    half = shaped(width // 2, out_width)
-    keep, move = call(
-        grad_out_kernel,
-        [Far(attn_tok), Far(grad_mid), Far(gain_sum)],
-        [half, half],
-        "grad_out",
-        far_out=(0,),
-        scalars=[place],
-    )
 
     def halve(keep, came, shift, blocks):
         half = shaped(keep.shape[0] // 2, out_width)
@@ -1029,8 +1024,8 @@
             scalars=[place],
         )
 
-    ffn_far = swap(after(ffn_far, grad_mid), CORE)
     keep, move = halve(keep, swap(move, CORE), 4, 1)
+    ffn_far = swap(after(ffn_far, move), CORE)
     came = swap(move, Y)
     ffn_sum = ffn_near.astype(F32) + ffn_far.astype(F32)
     ffn_move = ffn_sum[1::2].astype(BF16)
@@ -1064,25 +1059,15 @@
     direct = after(direct, grad_ffn)
     over_core = swap(after(over_core, over_y), CORE)
 
-    send, grad_both = call(
+    send, *grad_rows = call(
         gather_grads_kernel,
-        [*map(Far, (direct, queries, norms, grad_kv)), over_core, over_y],
-        [shaped(NH, rows, 2 * DH), shaped(wide_rows, 2 * DH)],
+        [*map(Far, (direct, queries, norms, normed, grad_kv)), over_core, over_y],
+        [shaped(NH, rows, 2 * DH)] + [shaped(NH, own_rows, 2 * DH)] * 4,
         "gather_grads",
-        far_out=(1,),
         scalars=[place],
+        scratch=[pltpu.VMEM((wide_rows, 2 * DH), BF16), pltpu.VMEM((width, 2 * DH), F32)],
     )
     arrived = lax.all_to_all(send, HEAD_AXES, 0, 0, tiled=True)
-
-    grad_rows = call(
-        project_back_kernel,
-        [Far(normed), Far(grad_both)],
-        [shaped(NH, own_rows, 2 * DH)] * 4,
-        "project_back",
-        scalars=[place],
-        scratch=[pltpu.VMEM((width, 2 * DH), F32)],
-    )
-    rows_parts = grad_rows
     grad_rows = call(
         sum_kernel,
         sum_shares(grad_rows),
@@ -1108,9 +1093,17 @@
         far_out=(0,),
     )[0]
 
-    keep, move = halve(keep, after(came, rows_send), 1, 2)
-    keep, move = halve(keep, after(swap(move, Z_LO), arrived), 2, 1)
-    grad_out = keep.astype(F32) + swap(move, Z_HI).astype(F32)
+    grad_out = call(
+        quarter_kernel,
+        [keep, after(came, rows_send)],
+        [shaped(own_rows, out_width)] * 4,
+        "quarter",
+        scalars=[place],
+    )
+    grad_out = sum(
+        after(swap(part, p * Z_LO) if p else part, arrived).astype(F32)
+        for p, part in enumerate(grad_out)
+    )
     ffn_sum = ffn_sum[0::2] + after(ffn_move, rows_send).astype(F32)
     ffn_sum = ffn_sum[0] + after(swap(ffn_sum[1].astype(BF16), Y), arrived).astype(F32)
     second_out = second_half.astype(F32) + ffn_sum

time: 373 us -> 357 us (0.957)
  Pallas kernels: 167 us -> 156 us
  waiting for transfers between devices: 89.9 us -> 81.5 us
  starting transfers between devices: 64.3 us -> 70 us
  local copies, waits for them, and re-layouts: 22 us -> 16.7 us
    pallas_call x20 -> x17, Pallas kernels: 102 us -> 90.2 us  [call(): pl.pallas_call(body, in_specs=[SMEM] * len(scalars) + [far if i in far_in...]
    ppermute x55 -> x56, starting transfers between devices: 41.1 us -> 49.2 us  [swap(): return lax.ppermute(value, BITS, [(i, i ^ mask) for i in range(32)])]
    all_to_all x1, waiting for transfers between devices: 12.1 us -> 4.58 us  [cube_plan(): grad_attn = lax.all_to_all(grad_attn, HEAD_AXES, 0, 0, tiled=True)]
    unnamed x120 -> x94, local copies, waits for them, and re-layouts: 14.7 us -> 8.73 us
    ppermute x55 -> x56, waiting for transfers between devices: 69 us -> 68.7 us  [swap(): return lax.ppermute(value, BITS, [(i, i ^ mask) for i in range(32)])]
  transfers between devices with their start and end apart: 63 -> 64, of which waited for: 22 -> 23; matrix products, arithmetic and copies ran while one was open for 4% -> 5% of each run, Pallas kernels for 39% -> 38%
where the time goes in v4:
time: 357 us; the launch traced here: 350 us
  Pallas kernels  156 us (44%)
  waiting for transfers between devices  81.5 us (23%)
  starting transfers between devices  70 us (20%)
  local copies, waits for them, and re-layouts  16.7 us (5%)
  between operations  14.8 us (4%)
  other arithmetic  11 us (3%)
    pallas_call x17, Pallas kernels, call(): pl.pallas_call(body, in_specs=[SMEM] * len(scalars) + [far if i in far_in...  90.2 us
    ppermute x56, waiting for transfers between devices, swap(): return lax.ppermute(value, BITS, [(i, i ^ mask) for i in range(32)])  68.7 us
    ppermute x56, starting transfers between devices, swap(): return lax.ppermute(value, BITS, [(i, i ^ mask) for i in range(32)])  49.2 us
    pallas_call x2, Pallas kernels, backward_call(): pl.pallas_call(functools.partial(backward_kernel, tile=tile, own=acc is n...  36.2 us
    pallas_call x3, Pallas kernels, forward_call(): pl.pallas_call(functools.partial(forward_kernel, tile=tile, parts=len(kvs...  29.4 us
    unnamed x94, local copies, waits for them, and re-layouts  8.73 us
    all_to_all x1, waiting for transfers between devices, cube_plan(): arrived = lax.all_to_all(send, HEAD_AXES, 0, 0, tiled=True)  7.48 us
  transfers between devices with their start and end apart: 64, of which 23 were waited for; matrix products, arithmetic and copies ran while one was open for 5% of the time, Pallas kernels for 38%

profile of v4, /device:TPU:0, one launch (start us, length us, event | category | flops | bytes accessed | tf_op | source)
XLA Modules:
  0.0 349.8 jit_solution(6200697709603545944)
XLA Ops:
  7.2 4.1 %collective-permute-start.3 = (bf16[192,1024]{1,0:T(8,128)(2,1)}, bf16[192,1024]{1,0:T(8,128)(2,1)S(1)}, u32[]{:S(2)}, u32[]{:S(2)}) collective-permute-start(bf16[192,1024]{1,0:T(8,128)(2,1)} %refs_1_.6), channel_id=1, source_target_pairs={{0,4},{1,5},{2,6},{3,7},{4,0},{5,1},{6,2},{7,3},{8,12},{9,13},{10,... | collective-permute-start | bytes 1179656 | tf_op jit(solution)/shard_map/ppermute | solution.py:324
  33.7 6.1 %collective-permute-done.2.refs_4_ = bf16[192,1024]{1,0:T(8,128)(2,1)S(1)} collective-permute-done((bf16[192,1024]{1,0:T(8,128)(2,1)S(1)}, bf16[192,1024]{1,0:T(8,128)(2,1)S(1)}, u32[]{:S(2)}, u32[]{:S(2)}) %collective-permute-start.2) | collective-permute-done | bytes 393248 | tf_op jit(solution)/shard_map/ppermute | solution.py:324
  42.7 3.9 %collective-permute-done.9.refs_11_ = bf16[8,32,384]{2,1,0:T(8,128)(2,1)S(1)} collective-permute-done((bf16[8,32,384]{2,1,0:T(8,128)(2,1)S(1)}, bf16[8,32,384]{2,1,0:T(8,128)(2,1)S(1)}, u32[]{:S(2)}, u32[]{:S(2)}) %collective-permute-start.9) | collective-permute-done | bytes 196640 | tf_op jit(solution)/shard_map/ppermute | solution.py:324
  55.2 4.1 %collective-permute-done.6.refs_8_ = bf16[192,1024]{1,0:T(8,128)(2,1)} collective-permute-done((bf16[192,1024]{1,0:T(8,128)(2,1)}, bf16[192,1024]{1,0:T(8,128)(2,1)}, u32[]{:S(2)}, u32[]{:S(2)}) %collective-permute-start.6) | collective-permute-done | bytes 393248 | tf_op jit(solution)/shard_map/ppermute | solution.py:324
  59.3 8.1 %project.1 = (bf16[1536,1024]{1,0:T(8,128)(2,1)}, bf16[1536,128]{1,0:T(8,128)(2,1)}, bf16[1536,256]{1,0:T(8,128)(2,1)}, f32[1536,1]{1,0:T(8,128)}, f32[8,1536]{1,0:T(8,128)}, /*index=5*/f32[8,1024]{1,0:T(8,128)}) custom-call(s32[2]{0:T(128)} %pad_add_fusion.refs_0_.refs_6_, bf16[192,1024]{1,0:T(8,128)(2,1)} %refs_1_.6, ...), custom_call_target="tpu_custom_call" | custom-call | tf_op jit(solution)/shard_map/project/pallas_call | solution.py:370
  71.1 13.3 %attention_forward.3.refs_5_ = f32[1536,256]{1,0:T(8,128)} custom-call(bf16[1536,128]{1,0:T(8,128)(2,1)} %get-tuple-element.109.refs_0_.refs_2_, f32[1536,1]{1,0:T(8,128)} %get-tuple-element.110.refs_1_.refs_3_, s32[6144,1]{1,0:T(8,128)} %ids.1.refs_2_.refs_5_, s32[8,6144]{1,0:T(8,128)} %add_add_fusion.refs_0_.refs_3_.refs_4_, ...), custom_call_target="tpu_custom_call" | custom-call | tf_op jit(solution)/shard_map/attention_forward/pallas_call | solution.py:587
  84.5 4.2 %collective-permute-done.13.refs_1_.refs_9_ = bf16[192,1024]{1,0:T(8,128)(2,1)S(1)} collective-permute-done((bf16[192,1024]{1,0:T(8,128)(2,1)S(1)}, bf16[192,1024]{1,0:T(8,128)(2,1)S(1)}, u32[]{:S(2)}, u32[]{:S(2)}) %collective-permute-start.13) | collective-permute-done | bytes 393248 | tf_op jit(solution)/shard_map/ppermute | solution.py:324
  88.8 7.9 %attention_forward.4.refs_5_ = f32[1536,256]{1,0:T(8,128)} custom-call(bf16[1536,128]{1,0:T(8,128)(2,1)} %get-tuple-element.109.refs_0_.refs_2_, f32[1536,1]{1,0:T(8,128)} %get-tuple-element.110.refs_1_.refs_3_, s32[6144,1]{1,0:T(8,128)} %ids.1.refs_2_.refs_5_, s32[8,6144]{1,0:T(8,128)} %add_add_fusion.refs_0_.refs_3_.refs_4_, ...), custom_call_target="tpu_custom_call", output_to_operand_aliasing={{}: (5, {})} | custom-call | tf_op jit(solution)/shard_map/attention_forward/pallas_call | solution.py:587
  96.8 8.1 %attention_forward.5 = (f32[1536,256]{1,0:T(8,128)}, bf16[8,192,128]{2,1,0:T(8,128)(2,1)}) custom-call(bf16[1536,128]{1,0:T(8,128)(2,1)} %get-tuple-element.109.refs_0_.refs_2_, f32[1536,1]{1,0:T(8,128)} %get-tuple-element.110.refs_1_.refs_3_, s32[6144,1]{1,0:T(8,128)} %ids.1.refs_2_.refs_5_, ...), custom_call_target="tpu_custom_call", output_to_operand_aliasing={{0}: (5, {})} | custom-call | tf_op jit(solution)/shard_map/attention_forward/pallas_call | solution.py:587
  105.4 4.3 %all-to-all-start.1 = ((bf16[8,192,128]{2,1,0:T(8,128)(2,1)}), bf16[8,192,128]{2,1,0:T(8,128)(2,1)}, u32[]{:S(2)}, u32[]{:S(2)}) async-start(bf16[8,192,128]{2,1,0:T(8,128)(2,1)} %get-tuple-element.115), calls=%async_computation.1 | async-start | bytes 786432 | tf_op jit(solution)/shard_map/all_to_all | solution.py:958
  116.3 7.2 %hidden_back.1.refs_8_ = f32[1536,512]{1,0:T(8,128)} custom-call(bf16[192,1024]{1,0:T(8,128)(2,1)} %refs_2_.6, bf16[192,1024]{1,0:T(8,128)(2,1)} %copy-done.6, bf16[192,1024]{1,0:T(8,128)(2,1)} %copy-done.2, bf16[192,1024]{1,0:T(8,128)(2,1)} %copy-done.4, bf16[192,1024]{1,0:T(8,128)(2,1)} %collective-permute-done.16.refs_4_.refs_12_, ...), custom_call_target="tpu_custom_call" | custom-call | tf_op jit(solution)/shard_map/hidden_back/pallas_call | solution.py:370
  123.6 3.7 %collective-permute-done.22.refs_7_ = bf16[4,16,2048]{2,1,0:T(8,128)(2,1)} collective-permute-done((bf16[4,16,2048]{2,1,0:T(8,128)(2,1)}, bf16[4,16,2048]{2,1,0:T(8,128)(2,1)}, u32[]{:S(2)}, u32[]{:S(2)}) %collective-permute-start.22) | collective-permute-done | bytes 262176 | tf_op jit(solution)/shard_map/ppermute | solution.py:324
  127.9 4.7 %collective-permute-done.20.refs_5_ = bf16[4,16,2048]{2,1,0:T(8,128)(2,1)S(1)} collective-permute-done((bf16[4,16,2048]{2,1,0:T(8,128)(2,1)}, bf16[4,16,2048]{2,1,0:T(8,128)(2,1)S(1)}, u32[]{:S(2)}, u32[]{:S(2)}) %collective-permute-start.20) | collective-permute-done | bytes 262176 | tf_op jit(solution)/shard_map/ppermute | solution.py:324
  135.4 5.9 %project_out.1 = (bf16[192,1024]{1,0:T(8,128)(2,1)}, f32[192,1024]{1,0:T(8,128)}, bf16[192,1024]{1,0:T(8,128)(2,1)}, bf16[1024,1024]{1,0:T(8,128)(2,1)}) custom-call(s32[2]{0:T(128)} %pad_add_fusion.refs_0_.refs_6_, bf16[8,192,128]{2,1,0:T(8,128)(2,1)} %all-to-all-done.1.refs_1_.refs_10_, bf16[192,1024]{1,0:T(8,128)(2,1)} %refs_2_.5, ...), custom_call_target="tpu_custom_call" | custom-call | tf_op jit(solution)/shard_map/project_out/pallas_call | solution.py:370
  144.9 8.8 %collective-permute-done.27.refs_1_ = bf16[192,1024]{1,0:T(8,128)(2,1)S(1)} collective-permute-done((bf16[192,1024]{1,0:T(8,128)(2,1)}, bf16[192,1024]{1,0:T(8,128)(2,1)S(1)}, u32[]{:S(2)}, u32[]{:S(2)}) %collective-permute-start.27) | collective-permute-done | bytes 393248 | tf_op jit(solution)/shard_map/ppermute | solution.py:324
  154.2 8.5 %collective-permute-done.29.refs_3_ = bf16[192,1024]{1,0:T(8,128)(2,1)S(1)} collective-permute-done((bf16[192,1024]{1,0:T(8,128)(2,1)}, bf16[192,1024]{1,0:T(8,128)(2,1)S(1)}, u32[]{:S(2)}, u32[]{:S(2)}) %collective-permute-start.29) | collective-permute-done | bytes 393248 | tf_op jit(solution)/shard_map/ppermute | solution.py:324
  165.5 9.8 %feed_forward.1 = (bf16[192,1024]{1,0:T(8,128)(2,1)S(1)}, bf16[192,1024]{1,0:T(8,128)(2,1)S(1)}, bf16[192,1024]{1,0:T(8,128)(2,1)S(1)}, bf16[192,1024]{1,0:T(8,1...) custom-call(bf16[192,1024]{1,0:T(8,128)(2,1)S(1)} %copy-done.12, ...), custom_call_target="tpu_custom_call" | custom-call | tf_op jit(solution)/shard_map/feed_forward/pallas_call | solution.py:370
  182.4 10.8 %feed_forward_rest.1 = (bf16[4,192,1024]{2,1,0:T(8,128)(2,1)}, bf16[4,192,1024]{2,1,0:T(8,128)(2,1)}, bf16[512,2048]{1,0:T(8,128)(2,1)}) custom-call(bf16[192,1024]{1,0:T(8,128)(2,1)S(1)} %copy-done.13, bf16[192,1024]{1,0:T(8,128)(2,1)S(1)} %collective-permute-done.27.refs_1_, bf16[192,1024]{1,0:T(8,128)(2,1)S(1)} %collective-permute-done.28.refs_2_, ...), custom_call_target="tpu_custom_call" | custom-call | tf_op jit(solution)/shard_map/feed_forward_rest/pallas_call | solution.py:370
  193.3 5.6 %collective-permute-done.38.refs_4_ = bf16[192,1024]{1,0:T(8,128)(2,1)S(1)} collective-permute-done((bf16[192,1024]{1,0:T(8,128)(2,1)S(1)}, bf16[192,1024]{1,0:T(8,128)(2,1)S(1)}, u32[]{:S(2)}, u32[]{:S(2)}) %collective-permute-start.38) | collective-permute-done | bytes 393248 | tf_op jit(solution)/shard_map/ppermute | solution.py:324
  199.8 7.8 %mid.1 = (bf16[192,1024]{1,0:T(8,128)(2,1)}, bf16[8,192,128]{2,1,0:T(8,128)(2,1)}, bf16[512,1152]{1,0:T(8,128)(2,1)}, bf16[512,1152]{1,0:T(8,128)(2,1)}) custom-call(s32[2]{0:T(128)} %pad_add_fusion.refs_0_.refs_6_, bf16[192,1024]{1,0:T(8,128)(2,1)} %copy-done.16, bf16[192,1024]{1,0:T(8,128)(2,1)} %copy-done.26, bf16[192,1024]{1,0:T(8,128)(2,1)} %copy-done.29, ...), custom_call_target="tpu_custom_call" | custom-call | tf_op jit(solution)/shard_map/mid/pallas_call | solution.py:370
  211.7 4.4 %halve.2 = (bf16[256,1152]{1,0:T(8,128)(2,1)}, bf16[256,1152]{1,0:T(8,128)(2,1)}) custom-call(s32[2]{0:T(128)} %pad_add_fusion.refs_0_.refs_6_, bf16[512,1152]{1,0:T(8,128)(2,1)} %get-tuple-element.148.refs_1_, bf16[512,1152]{1,0:T(8,128)(2,1)} %copy-done.39), custom_call_target="tpu_custom_call" | custom-call | flops 99999997952 | bytes 1 | tf_op jit(solution)/shard_map/halve/pallas_call | solution.py:370
  216.3 4.8 %all-to-all-start.2 = ((bf16[8,192,128]{2,1,0:T(8,128)(2,1)}), bf16[8,192,128]{2,1,0:T(8,128)(2,1)S(1)}, u32[]{:S(2)}, u32[]{:S(2)}) async-start(bf16[8,192,128]{2,1,0:T(8,128)(2,1)} %get-tuple-element.152), calls=%async_computation.2 | async-start | bytes 786432 | tf_op jit(solution)/shard_map/all_to_all | solution.py:1014
  228.7 4.6 %all-to-all-done.2.refs_1_ = bf16[8,192,128]{2,1,0:T(8,128)(2,1)S(1)} async-done(((bf16[8,192,128]{2,1,0:T(8,128)(2,1)}), bf16[8,192,128]{2,1,0:T(8,128)(2,1)S(1)}, u32[]{:S(2)}, u32[]{:S(2)}) %all-to-all-start.2) | async-done | bytes 393248 | tf_op jit(solution)/shard_map/all_to_all | solution.py:1014
  234.0 3.8 %turn.1 = (bf16[1536,128]{1,0:T(8,128)(2,1)}, f32[8,1536]{1,0:T(8,128)}) custom-call(s32[2]{0:T(128)} %pad_add_fusion.refs_0_.refs_6_, bf16[8,192,128]{2,1,0:T(8,128)(2,1)} %copy-done.30, f32[1536,256]{1,0:T(8,128)} %get-tuple-element.154.refs_2_), custom_call_target="tpu_custom_call" | custom-call | flops 99999997952 | bytes 1 | tf_op jit(solution)/shard_map/turn/pallas_call | solution.py:370
  237.8 17.8 %attention_backward.2 = (f32[1536,256]{1,0:T(8,128)}, bf16[1536,256]{1,0:T(8,128)(2,1)}, bf16[1536,256]{1,0:T(8,128)(2,1)}) custom-call(bf16[1536,128]{1,0:T(8,128)(2,1)} %get-tuple-element.109.refs_0_.refs_2_, bf16[1536,128]{1,0:T(8,128)(2,1)} %get-tuple-element.155.refs_1_, f32[8,1536]{1,0:T(8,128)} %get-tuple-element.156.refs_2_, ...), custom_call_target="tpu_custom_call" | custom-call | flops 99999997952 | bytes 1 | tf_op jit(solution)/shard_map/attention_backward/pallas_call | solution.py:652
  255.7 3.7 %halve.3 = (bf16[128,1152]{1,0:T(8,128)(2,1)}, bf16[128,1152]{1,0:T(8,128)(2,1)}) custom-call(s32[2]{0:T(128)} %pad_add_fusion.refs_0_.refs_6_, bf16[256,1152]{1,0:T(8,128)(2,1)} %get-tuple-element.161.refs_1_, bf16[256,1152]{1,0:T(8,128)(2,1)} %collective-permute-done.45.refs_2_), custom_call_target="tpu_custom_call" | custom-call | flops 99999997952 | bytes 1 | tf_op jit(solution)/shard_map/halve/pallas_call | solution.py:370
  262.3 18.4 %attention_backward.3 = (f32[1536,256]{1,0:T(8,128)}, bf16[1536,256]{1,0:T(8,128)(2,1)}, bf16[1536,256]{1,0:T(8,128)(2,1)}) custom-call(bf16[1536,128]{1,0:T(8,128)(2,1)} %get-tuple-element.109.refs_0_.refs_2_, bf16[1536,128]{1,0:T(8,128)(2,1)} %get-tuple-element.155.refs_1_, f32[8,1536]{1,0:T(8,128)} %get-tuple-element.156.refs_2_, ...), custom_call_target="tpu_custom_call", output_to_operand_aliasing={{0}: (8, {})} | custom-call | flops 99999997952 | bytes 1 | tf_op jit(solution)/shard_map/attention_backward/pallas_call | solution.py:652
  284.2 7.1 %gather_grads.1 = (bf16[8,192,256]{2,1,0:T(8,128)(2,1)}, bf16[8,32,256]{2,1,0:T(8,128)(2,1)}, bf16[8,32,256]{2,1,0:T(8,128)(2,1)}, bf16[8,32,256]{2,1,0:T(8,128)(2,1)}, bf16[8,32,256]{2,1,0:T(8,128)(2,1)}) custom-call(s32[2]{0:T(128)} %pad_add_fusion.refs_0_.refs_6_, f32[1536,256]{1,0:T(8,128)} %get-tuple-element.167.refs_1_, ...), custom_call_target="tpu_custom_call" | custom-call | flops 99999997952 | bytes 1 | tf_op jit(solution)/shard_map/gather_grads/pallas_call | solution.py:370
  294.7 4.2 %all-to-all-start.3 = ((bf16[8,192,256]{2,1,0:T(8,128)(2,1)}), bf16[8,192,256]{2,1,0:T(8,128)(2,1)}, u32[]{:S(2)}, u32[]{:S(2)}) async-start(bf16[8,192,256]{2,1,0:T(8,128)(2,1)} %get-tuple-element.177), calls=%async_computation.4 | async-start | bytes 1572864 | tf_op jit(solution)/shard_map/all_to_all | solution.py:1070
  316.2 7.5 %all-to-all-done.3.refs_0_ = bf16[8,192,256]{2,1,0:T(8,128)(2,1)} async-done(((bf16[8,192,256]{2,1,0:T(8,128)(2,1)}), bf16[8,192,256]{2,1,0:T(8,128)(2,1)}, u32[]{:S(2)}, u32[]{:S(2)}) %all-to-all-start.3) | async-done | bytes 786464 | tf_op jit(solution)/shard_map/all_to_all | solution.py:1070
  325.8 4.0 %all-to-all-start.4 = ((bf16[8,32,256]{2,1,0:T(8,128)(2,1)}), bf16[8,32,256]{2,1,0:T(8,128)(2,1)}, u32[]{:S(2)}, u32[]{:S(2)}) async-start(bf16[8,32,256]{2,1,0:T(8,128)(2,1)} %sum_rows.1), calls=%async_computation.5 | async-start | bytes 262144 | tf_op jit(solution)/shard_map/all_to_all | solution.py:1087
  330.5 6.2 %last.1 = bf16[192,1024]{1,0:T(8,128)(2,1)} custom-call(bf16[8,192,256]{2,1,0:T(8,128)(2,1)} %all-to-all-done.3.refs_0_, bf16[192,1024]{1,0:T(8,128)(2,1)} %refs_1_.6, bf16[192,1024]{1,0:T(8,128)(2,1)} %refs_2_.6, f32[8,1024]{1,0:T(8,128)} %get-tuple-element.116.refs_3_.refs_8_, bf16[1024,2048]{1,0:T(8,128)(2,1)} %all-gather.4.cloned.1.call-done.refs_4_), custom_call_target="tpu_custom_call" | custom-call | flops 99999997952 | bytes 1 | tf_op jit(solution)/shard_map/last/pallas_call | solution.py:370
  (251 shorter events, 111.5 us)
Async XLA Ops:
  7.2 23.9 %collective-permute-start.3 = (bf16[192,1024]{1,0:T(8,128)(2,1)}, bf16[192,1024]{1,0:T(8,128)(2,1)S(1)}, u32[]{:S(2)}, u32[]{:S(2)}) collective-permute-start(bf16[192,1024]{1,0:T(8,128)(2,1)} %refs_1_.6), channel_id=1, source_target_pairs={{0,4},{1,5},{2,6},{3,7},{4,0},{5,1},{6,2},{7,3},{8,12},{9,13},{10,... | collective-permute-start | bytes 1179656 | tf_op jit(solution)/shard_map/ppermute | solution.py:324
  11.3 18.3 %collective-permute-start.1 = (bf16[192,1024]{1,0:T(8,128)(2,1)}, bf16[192,1024]{1,0:T(8,128)(2,1)S(1)}, u32[]{:S(2)}, u32[]{:S(2)}) collective-permute-start(bf16[192,1024]{1,0:T(8,128)(2,1)} %refs_1_.6), channel_id=1, source_target_pairs={{0,2},{1,3},{2,0},{3,1},{4,6},{5,7},{6,4},{7,5},{8,10},{9,11},{10,... | collective-permute-start | bytes 1179656 | tf_op jit(solution)/shard_map/ppermute | solution.py:324
  12.9 42.3 %collective-permute-start = (bf16[192,1024]{1,0:T(8,128)(2,1)}, bf16[192,1024]{1,0:T(8,128)(2,1)}, u32[]{:S(2)}, u32[]{:S(2)}) collective-permute-start(bf16[192,1024]{1,0:T(8,128)(2,1)} %refs_1_.6), channel_id=1, source_target_pairs={{0,1},{1,0},{2,3},{3,2},{4,5},{5,4},{6,7},{7,6},{8,9},{9,8},{10,11... | collective-permute-start | bytes 1179656 | tf_op jit(solution)/shard_map/ppermute | solution.py:324
  18.6 22.3 %all-to-all-start = ((bf16[8,32,384]{2,1,0:T(8,128)(2,1)}), bf16[8,32,384]{2,1,0:T(8,128)(2,1)S(1)}, u32[]{:S(2)}, u32[]{:S(2)}) async-start(bf16[8,32,384]{2,1,0:T(8,128)(2,1)} %get-tuple-element.107), calls=%async_computation | async-start | bytes 393216 | tf_op jit(solution)/shard_map/all_to_all | solution.py:903
  22.1 74.7 %all-gather.6.cloned.1.call-start = ((), (), s32[]{:S(2)}) async-start(), calls=%async_computation.8 | async-start | bytes 2949120 | tf_op jit(solution)/shard_map/all_gather | solution.py:904
  22.1 33.1 %collective-permute-start.7 = (bf16[192,1024]{1,0:T(8,128)(2,1)}, bf16[192,1024]{1,0:T(8,128)(2,1)S(1)}, u32[]{:S(2)}, u32[]{:S(2)}) collective-permute-start(bf16[192,1024]{1,0:T(8,128)(2,1)} %refs_2_.6), channel_id=1, source_target_pairs={{0,16},{1,17},{2,18},{3,19},{4,20},{5,21},{6,22},{7,23},{8,24},{9,... | collective-permute-start | bytes 1179656 | tf_op jit(solution)/shard_map/ppermute | solution.py:324
  31.2 162.1 %all-gather.4.cloned.1.call-start = ((), (), s32[]{:S(2)}) async-start(), calls=%async_computation.6 | async-start | bytes 4325376 | tf_op jit(solution)/shard_map/all_gather | solution.py:953
  31.2 15.5 %collective-permute-start.5 = (bf16[192,1024]{1,0:T(8,128)(2,1)S(1)}, bf16[192,1024]{1,0:T(8,128)(2,1)}, u32[]{:S(2)}, u32[]{:S(2)}) collective-permute-start(bf16[192,1024]{1,0:T(8,128)(2,1)S(1)} %collective-permute-done.3.refs_5_), channel_id=1, source_target_pairs={{0,2},{1,3},{2,0},{3,1},{4,6},{5,7},{6,4},{7,5},{8,10},{9,11},{10,... | collective-permute-start | bytes 1179656 | tf_op jit(solution)/shard_map/ppermute | solution.py:324
  67.5 21.2 %collective-permute-start.11 = (bf16[1536,256]{1,0:T(8,128)(2,1)}, bf16[1536,256]{1,0:T(8,128)(2,1)}, u32[]{:S(2)}, u32[]{:S(2)}) collective-permute-start(bf16[1536,256]{1,0:T(8,128)(2,1)} %get-tuple-element.111.refs_4_.refs_6_), channel_id=1, source_target_pairs={{0,16},{1,17},{2,18},{3,19},{4,20},{5,21},{6,22},{7,23},{8,24},{9,... | collective-permute-start | bytes 2359304 | tf_op jit(solution)/shard_map/ppermute | solution.py:324
  69.1 15.4 %collective-permute-start.14 = (bf16[192,1024]{1,0:T(8,128)(2,1)S(1)}, bf16[192,1024]{1,0:T(8,128)(2,1)S(1)}, u32[]{:S(2)}, u32[]{:S(2)}) collective-permute-start(bf16[192,1024]{1,0:T(8,128)(2,1)S(1)} %collective-permute-done.7.refs_2_.refs_10_), channel_id=1, source_target_pairs={{0,1},{1,0},{2,3},{3,2},{4,5},{5,4},{6,7},{7,6},{8,9},{9,8},{10,11... | collective-permute-start | bytes 1179656 | tf_op jit(solution)/shard_map/ppermute | solution.py:324
  70.1 18.6 %collective-permute-start.13 = (bf16[192,1024]{1,0:T(8,128)(2,1)S(1)}, bf16[192,1024]{1,0:T(8,128)(2,1)S(1)}, u32[]{:S(2)}, u32[]{:S(2)}) collective-permute-start(bf16[192,1024]{1,0:T(8,128)(2,1)S(1)} %copy-done), channel_id=1, source_target_pairs={{0,1},{1,0},{2,3},{3,2},{4,5},{5,4},{6,7},{7,6},{8,9},{9,8},{10,11... | collective-permute-start | bytes 1179656 | tf_op jit(solution)/shard_map/ppermute | solution.py:324
  105.4 29.3 %all-to-all-start.1 = ((bf16[8,192,128]{2,1,0:T(8,128)(2,1)}), bf16[8,192,128]{2,1,0:T(8,128)(2,1)}, u32[]{:S(2)}, u32[]{:S(2)}) async-start(bf16[8,192,128]{2,1,0:T(8,128)(2,1)} %get-tuple-element.115), calls=%async_computation.1 | async-start | bytes 786432 | tf_op jit(solution)/shard_map/all_to_all | solution.py:958
  112.0 15.3 %collective-permute-start.22 = (bf16[4,16,2048]{2,1,0:T(8,128)(2,1)}, bf16[4,16,2048]{2,1,0:T(8,128)(2,1)}, u32[]{:S(2)}, u32[]{:S(2)}) collective-permute-start(bf16[4,16,2048]{2,1,0:T(8,128)(2,1)} %slice.78.refs_4_), channel_id=1, source_target_pairs={{0,17},{1,16},{2,19},{3,18},{4,21},{5,20},{6,23},{7,22},{8,25},{9,... | collective-permute-start | bytes 786440 | tf_op jit(solution)/shard_map/ppermute | solution.py:324
  114.0 13.9 %collective-permute-start.21 = (bf16[4,16,2048]{2,1,0:T(8,128)(2,1)}, bf16[4,16,2048]{2,1,0:T(8,128)(2,1)S(1)}, u32[]{:S(2)}, u32[]{:S(2)}) collective-permute-start(bf16[4,16,2048]{2,1,0:T(8,128)(2,1)} %slice.78.refs_4_), channel_id=1, source_target_pairs={{0,16},{1,17},{2,18},{3,19},{4,20},{5,21},{6,22},{7,23},{8,24},{9,... | collective-permute-start | bytes 786440 | tf_op jit(solution)/shard_map/ppermute | solution.py:324
  115.5 17.2 %collective-permute-start.20 = (bf16[4,16,2048]{2,1,0:T(8,128)(2,1)}, bf16[4,16,2048]{2,1,0:T(8,128)(2,1)S(1)}, u32[]{:S(2)}, u32[]{:S(2)}) collective-permute-start(bf16[4,16,2048]{2,1,0:T(8,128)(2,1)} %slice.78.refs_4_), channel_id=1, source_target_pairs={{0,1},{1,0},{2,3},{3,2},{4,5},{5,4},{6,7},{7,6},{8,9},{9,8},{10,11... | collective-permute-start | bytes 786440 | tf_op jit(solution)/shard_map/ppermute | solution.py:324
  142.8 20.0 %collective-permute-start.29 = (bf16[192,1024]{1,0:T(8,128)(2,1)}, bf16[192,1024]{1,0:T(8,128)(2,1)S(1)}, u32[]{:S(2)}, u32[]{:S(2)}) collective-permute-start(bf16[192,1024]{1,0:T(8,128)(2,1)} %get-tuple-element.129.refs_0_), channel_id=1, source_target_pairs={{0,17},{1,16},{2,19},{3,18},{4,21},{5,20},{6,23},{7,22},{8,25},{9,... | collective-permute-start | bytes 1179656 | tf_op jit(solution)/shard_map/ppermute | solution.py:324
  144.9 17.9 %collective-permute-start.30 = (bf16[192,1024]{1,0:T(8,128)(2,1)}, bf16[192,1024]{1,0:T(8,128)(2,1)S(1)}, u32[]{:S(2)}, u32[]{:S(2)}) collective-permute-start(bf16[192,1024]{1,0:T(8,128)(2,1)} %get-tuple-element.129.refs_0_), channel_id=1, source_target_pairs={{0,8},{1,9},{2,10},{3,11},{4,12},{5,13},{6,14},{7,15},{8,0},{9,1},... | collective-permute-start | bytes 1179656 | tf_op jit(solution)/shard_map/ppermute | solution.py:324
  177.1 16.2 %collective-permute-start.34 = (bf16[192,1024]{1,0:T(8,128)(2,1)S(1)}, bf16[192,1024]{1,0:T(8,128)(2,1)S(1)}, u32[]{:S(2)}, u32[]{:S(2)}) collective-permute-start(bf16[192,1024]{1,0:T(8,128)(2,1)S(1)} %get-tuple-element.135), channel_id=1, source_target_pairs={{0,8},{1,9},{2,10},{3,11},{4,12},{5,13},{6,14},{7,15},{8,0},{9,1},... | collective-permute-start | bytes 1179656 | tf_op jit(solution)/shard_map/ppermute | solution.py:324
  178.4 14.9 %collective-permute-start.40 = (bf16[192,1024]{1,0:T(8,128)(2,1)S(1)}, bf16[192,1024]{1,0:T(8,128)(2,1)S(1)}, u32[]{:S(2)}, u32[]{:S(2)}) collective-permute-start(bf16[192,1024]{1,0:T(8,128)(2,1)S(1)} %add_convert_fusion.1), channel_id=1, source_target_pairs={{0,17},{1,16},{2,19},{3,18},{4,21},{5,20},{6,23},{7,22},{8,25},{9,... | collective-permute-start | bytes 1179656 | tf_op jit(solution)/shard_map/ppermute | solution.py:324
  179.8 19.1 %collective-permute-start.38 = (bf16[192,1024]{1,0:T(8,128)(2,1)S(1)}, bf16[192,1024]{1,0:T(8,128)(2,1)S(1)}, u32[]{:S(2)}, u32[]{:S(2)}) collective-permute-start(bf16[192,1024]{1,0:T(8,128)(2,1)S(1)} %add_convert_fusion.2), channel_id=1, source_target_pairs={{0,16},{1,17},{2,18},{3,19},{4,20},{5,21},{6,22},{7,23},{8,24},{9,... | collective-permute-start | bytes 1179656 | tf_op jit(solution)/shard_map/ppermute | solution.py:324
  180.8 18.1 %collective-permute-start.36 = (bf16[192,1024]{1,0:T(8,128)(2,1)S(1)}, bf16[192,1024]{1,0:T(8,128)(2,1)S(1)}, u32[]{:S(2)}, u32[]{:S(2)}) collective-permute-start(bf16[192,1024]{1,0:T(8,128)(2,1)S(1)} %add_convert_fusion.3), channel_id=1, source_target_pairs={{0,1},{1,0},{2,3},{3,2},{4,5},{5,4},{6,7},{7,6},{8,9},{9,8},{10,11... | collective-permute-start | bytes 1179656 | tf_op jit(solution)/shard_map/ppermute | solution.py:324
  216.3 17.0 %all-to-all-start.2 = ((bf16[8,192,128]{2,1,0:T(8,128)(2,1)}), bf16[8,192,128]{2,1,0:T(8,128)(2,1)S(1)}, u32[]{:S(2)}, u32[]{:S(2)}) async-start(bf16[8,192,128]{2,1,0:T(8,128)(2,1)} %get-tuple-element.152), calls=%async_computation.2 | async-start | bytes 786432 | tf_op jit(solution)/shard_map/all_to_all | solution.py:1014
  221.0 60.0 %reduce-scatter.2.cloned.1.call-start = ((), (), s32[]{:S(2)}) async-start(), calls=%async_computation.7 | async-start | bytes 2621440 | tf_op jit(solution)/shard_map/reduce_scatter | solution.py:1047
  221.8 33.8 %collective-permute-start.45 = (bf16[256,1152]{1,0:T(8,128)(2,1)}, bf16[256,1152]{1,0:T(8,128)(2,1)}, u32[]{:S(2)}, u32[]{:S(2)}) collective-permute-start(bf16[256,1152]{1,0:T(8,128)(2,1)} %get-tuple-element.150), channel_id=1, source_target_pairs={{0,16},{1,17},{2,18},{3,19},{4,20},{5,21},{6,22},{7,23},{8,24},{9,... | collective-permute-start | bytes 1769480 | tf_op jit(solution)/shard_map/ppermute | solution.py:324
  226.7 35.7 %collective-permute-start.43 = (bf16[2,192,1024]{2,1,0:T(8,128)(2,1)}, bf16[2,192,1024]{2,1,0:T(8,128)(2,1)}, u32[]{:S(2)}, u32[]{:S(2)}) collective-permute-start(bf16[2,192,1024]{2,1,0:T(8,128)(2,1)} %slice.80), channel_id=1, source_target_pairs={{0,1},{1,0},{2,3},{3,2},{4,5},{5,4},{6,7},{7,6},{8,9},{9,8},{10,11... | collective-permute-start | bytes 2359304 | tf_op jit(solution)/shard_map/ppermute | solution.py:324
  260.8 20.0 %collective-permute-start.46 = (bf16[1536,256]{1,0:T(8,128)(2,1)S(1)}, bf16[1536,256]{1,0:T(8,128)(2,1)S(1)}, u32[]{:S(2)}, u32[]{:S(2)}) collective-permute-start(bf16[1536,256]{1,0:T(8,128)(2,1)S(1)} %add_convert_fusion), channel_id=1, source_target_pairs={{0,16},{1,17},{2,18},{3,19},{4,20},{5,21},{6,22},{7,23},{8,24},{9,... | collective-permute-start | bytes 2359304 | tf_op jit(solution)/shard_map/ppermute | solution.py:324
  294.7 28.9 %all-to-all-start.3 = ((bf16[8,192,256]{2,1,0:T(8,128)(2,1)}), bf16[8,192,256]{2,1,0:T(8,128)(2,1)}, u32[]{:S(2)}, u32[]{:S(2)}) async-start(bf16[8,192,256]{2,1,0:T(8,128)(2,1)} %get-tuple-element.177), calls=%async_computation.4 | async-start | bytes 1572864 | tf_op jit(solution)/shard_map/all_to_all | solution.py:1070
  308.1 15.5 %collective-permute-start.53 = (bf16[32,1152]{1,0:T(8,128)(2,1)}, bf16[32,1152]{1,0:T(8,128)(2,1)S(1)}, u32[]{:S(2)}, u32[]{:S(2)}) collective-permute-start(bf16[32,1152]{1,0:T(8,128)(2,1)} %get-tuple-element.191), channel_id=1, source_target_pairs={{0,2},{1,3},{2,0},{3,1},{4,6},{5,7},{6,4},{7,5},{8,10},{9,11},{10,... | collective-permute-start | bytes 221192 | tf_op jit(solution)/shard_map/ppermute | solution.py:324
  308.2 16.9 %collective-permute-start.54 = (bf16[32,1152]{1,0:T(8,128)(2,1)}, bf16[32,1152]{1,0:T(8,128)(2,1)S(1)}, u32[]{:S(2)}, u32[]{:S(2)}) collective-permute-start(bf16[32,1152]{1,0:T(8,128)(2,1)} %get-tuple-element.193), channel_id=1, source_target_pairs={{0,4},{1,5},{2,6},{3,7},{4,0},{5,1},{6,2},{7,3},{8,12},{9,13},{10,... | collective-permute-start | bytes 221192 | tf_op jit(solution)/shard_map/ppermute | solution.py:324
  310.0 15.1 %collective-permute-start.55 = (bf16[32,1152]{1,0:T(8,128)(2,1)}, bf16[32,1152]{1,0:T(8,128)(2,1)S(1)}, u32[]{:S(2)}, u32[]{:S(2)}) collective-permute-start(bf16[32,1152]{1,0:T(8,128)(2,1)} %get-tuple-element.195), channel_id=1, source_target_pairs={{0,6},{1,7},{2,4},{3,5},{4,2},{5,3},{6,0},{7,1},{8,14},{9,15},{10,... | collective-permute-start | bytes 221192 | tf_op jit(solution)/shard_map/ppermute | solution.py:324
  314.7 15.8 %collective-permute-start.51 = (bf16[192,1024]{1,0:T(8,128)(2,1)S(1)}, bf16[192,1024]{1,0:T(8,128)(2,1)}, u32[]{:S(2)}, u32[]{:S(2)}) collective-permute-start(bf16[192,1024]{1,0:T(8,128)(2,1)S(1)} %fusion.3), channel_id=1, source_target_pairs={{0,16},{1,17},{2,18},{3,19},{4,20},{5,21},{6,22},{7,23},{8,24},{9,... | collective-permute-start | bytes 1179656 | tf_op jit(solution)/shard_map/ppermute | solution.py:324
  325.8 12.7 %all-to-all-start.4 = ((bf16[8,32,256]{2,1,0:T(8,128)(2,1)}), bf16[8,32,256]{2,1,0:T(8,128)(2,1)}, u32[]{:S(2)}, u32[]{:S(2)}) async-start(bf16[8,32,256]{2,1,0:T(8,128)(2,1)} %sum_rows.1), calls=%async_computation.5 | async-start | bytes 262144 | tf_op jit(solution)/shard_map/all_to_all | solution.py:1087
  (79 other events, 526.4 us)
Sparse Core Ops, SparseCore 0:
  31.3 50.4 all-gather.5
  88.8 65.4 all-gather.3
  224.2 45.2 reduce-scatter.1

commit v5 on v4

--- a/solution.py
+++ b/solution.py
@@ -337,8 +337,22 @@
         self.value = value
 
 
-def call(kernel, inputs, out_shape, name, far_out=(), mib=62, scalars=(), scratch=(), cost=LONG):
-    far_in = [i for i, a in enumerate(inputs) if isinstance(a, Far)]
+class Fetched:
+    def __init__(self, ref, copy):
+        self.ref, self.copy, self.shape = ref, copy, ref.shape
+
+    def wait(self):
+        if self.copy is not None:
+            self.copy.wait()
+            self.copy = None
+
+    def __getitem__(self, place):
+        self.wait()
+        return self.ref[place]
+
+
+def call(kernel, inputs, out_shape, name, far_out=(), mib=62, scalars=(), scratch=(), cost=LONG, lazy=False):
+    far_in = [i for i, a in enumerate(inputs) if lazy or isinstance(a, Far)]
     arrays = [a.value if isinstance(a, Far) else a for a in inputs]
     first_in, first_out = len(scalars), len(scalars) + len(arrays)
     first_scratch = first_out + len(out_shape)
@@ -348,19 +362,22 @@
         refs, sems = list(refs[:-1]), refs[-1]
         own = refs[first_scratch : first_scratch + len(scratch)]
         stages = refs[first_scratch + len(scratch) :]
-        copies = []
+        fetched = []
         for k, i in enumerate(far_in):
-            copies.append(pltpu.make_async_copy(refs[first_in + i], stages[k], sems.at[k]))
-            refs[first_in + i] = stages[k]
-        for copy in copies:
+            copy = pltpu.make_async_copy(refs[first_in + i], stages[k], sems.at[k])
             copy.start()
-        for copy in copies:
-            copy.wait()
+            fetched.append(Fetched(stages[k], copy))
+            refs[first_in + i] = fetched[-1]
+        if not lazy:
+            for operand in fetched:
+                operand.wait()
         copies = []
         for k, i in enumerate(far_out, len(far_in)):
             copies.append(pltpu.make_async_copy(stages[k], refs[first_out + i], sems.at[k]))
             refs[first_out + i] = stages[k]
         kernel(*refs[:first_scratch], *own)
+        for operand in fetched:
+            operand.wait()
         for copy in copies:
             copy.start()
         for copy in copies:
@@ -1006,6 +1023,7 @@
         ],
         [row_block, shaped(NH, rows, DH), half, half],
         "mid",
+        lazy=True,
         cost=None,
         far_out=(0, 2),
         scalars=[place],
@@ -1020,6 +1038,7 @@
             [Far(keep), came],
             [half, half],
             "halve",
+            lazy=True,
             far_out=(0,),
             scalars=[place],
         )
@@ -1034,6 +1053,7 @@
         [after(grad_attn, move, ffn_move), Far(acc)],
         [shaped(wide_rows, DH), shaped(8, wide_rows, dtype=F32)],
         "turn",
+        lazy=True,
         far_out=(0, 1),
         scalars=[place],
         scratch=[pltpu.VMEM((wide_rows, 1), F32)],
@@ -1090,6 +1110,7 @@
         [arrived, *map(Far, (second_half, grad_second, gain_rows, qv_full))],
         [row_block],
         "last",
+        lazy=True,
         far_out=(0,),
     )[0]
 
@@ -1112,6 +1133,7 @@
         [after(grad_rows, grad_second_half, grad_up), Far(qk_weight), Far(value_weight), Far(gains)],
         [shaped(own_rows, width, dtype=F32)] * 2 + [shaped(own_rows, 128, dtype=F32)],
         "own_rows",
+        lazy=True,
         far_out=(0, 1),
     )
 

time: 357 us -> 355 us (level)
  no operation moved by 1% of the time
where the time goes in v5:
time: 355 us; the launch traced here: 348 us
  Pallas kernels  153 us (43%)
  waiting for transfers between devices  81.7 us (23%)
  starting transfers between devices  70.4 us (20%)
  local copies, waits for them, and re-layouts  16.7 us (5%)
  between operations  15 us (4%)
  other arithmetic  11 us (3%)
    pallas_call x17, Pallas kernels, call(): pl.pallas_call(body, in_specs=[SMEM] * len(scalars) + [far if i in far_in...  88 us
    ppermute x56, waiting for transfers between devices, swap(): return lax.ppermute(value, BITS, [(i, i ^ mask) for i in range(32)])  68.9 us
    ppermute x56, starting transfers between devices, swap(): return lax.ppermute(value, BITS, [(i, i ^ mask) for i in range(32)])  49.4 us
    pallas_call x2, Pallas kernels, backward_call(): pl.pallas_call(functools.partial(backward_kernel, tile=tile, own=acc is n...  36.1 us
    pallas_call x3, Pallas kernels, forward_call(): pl.pallas_call(functools.partial(forward_kernel, tile=tile, parts=len(kvs...  29.1 us
    unnamed x94, local copies, waits for them, and re-layouts  8.73 us
    all_to_all x1, waiting for transfers between devices, cube_plan(): arrived = lax.all_to_all(send, HEAD_AXES, 0, 0, tiled=True)  7.55 us
  transfers between devices with their start and end apart: 64, of which 23 were waited for; matrix products, arithmetic and copies ran while one was open for 5% of the time, Pallas kernels for 38%

profile of v5, /device:TPU:0, one launch (start us, length us, event | category | flops | bytes accessed | tf_op | source)
XLA Modules:
  0.0 348.1 jit_solution(14725294476285037196)
XLA Ops:
  7.2 4.1 %collective-permute-start.3 = (bf16[192,1024]{1,0:T(8,128)(2,1)}, bf16[192,1024]{1,0:T(8,128)(2,1)S(1)}, u32[]{:S(2)}, u32[]{:S(2)}) collective-permute-start(bf16[192,1024]{1,0:T(8,128)(2,1)} %refs_1_.6), channel_id=1, source_target_pairs={{0,4},{1,5},{2,6},{3,7},{4,0},{5,1},{6,2},{7,3},{8,12},{9,13},{10,... | collective-permute-start | bytes 1179656 | tf_op jit(solution)/shard_map/ppermute | solution.py:324
  33.7 6.1 %collective-permute-done.2.refs_4_ = bf16[192,1024]{1,0:T(8,128)(2,1)S(1)} collective-permute-done((bf16[192,1024]{1,0:T(8,128)(2,1)S(1)}, bf16[192,1024]{1,0:T(8,128)(2,1)S(1)}, u32[]{:S(2)}, u32[]{:S(2)}) %collective-permute-start.2) | collective-permute-done | bytes 393248 | tf_op jit(solution)/shard_map/ppermute | solution.py:324
  42.7 3.9 %collective-permute-done.9.refs_11_ = bf16[8,32,384]{2,1,0:T(8,128)(2,1)S(1)} collective-permute-done((bf16[8,32,384]{2,1,0:T(8,128)(2,1)S(1)}, bf16[8,32,384]{2,1,0:T(8,128)(2,1)S(1)}, u32[]{:S(2)}, u32[]{:S(2)}) %collective-permute-start.9) | collective-permute-done | bytes 196640 | tf_op jit(solution)/shard_map/ppermute | solution.py:324
  55.2 4.1 %collective-permute-done.6.refs_8_ = bf16[192,1024]{1,0:T(8,128)(2,1)} collective-permute-done((bf16[192,1024]{1,0:T(8,128)(2,1)}, bf16[192,1024]{1,0:T(8,128)(2,1)}, u32[]{:S(2)}, u32[]{:S(2)}) %collective-permute-start.6) | collective-permute-done | bytes 393248 | tf_op jit(solution)/shard_map/ppermute | solution.py:324
  59.3 8.1 %project.1 = (bf16[1536,1024]{1,0:T(8,128)(2,1)}, bf16[1536,128]{1,0:T(8,128)(2,1)}, bf16[1536,256]{1,0:T(8,128)(2,1)}, f32[1536,1]{1,0:T(8,128)}, f32[8,1536]{1,0:T(8,128)}, /*index=5*/f32[8,1024]{1,0:T(8,128)}) custom-call(s32[2]{0:T(128)} %pad_add_fusion.refs_0_.refs_6_, bf16[192,1024]{1,0:T(8,128)(2,1)} %refs_1_.6, ...), custom_call_target="tpu_custom_call" | custom-call | tf_op jit(solution)/shard_map/project/pallas_call | solution.py:387
  71.1 13.1 %attention_forward.3.refs_5_ = f32[1536,256]{1,0:T(8,128)} custom-call(bf16[1536,128]{1,0:T(8,128)(2,1)} %get-tuple-element.109.refs_0_.refs_2_, f32[1536,1]{1,0:T(8,128)} %get-tuple-element.110.refs_1_.refs_3_, s32[6144,1]{1,0:T(8,128)} %ids.1.refs_2_.refs_5_, s32[8,6144]{1,0:T(8,128)} %add_add_fusion.refs_0_.refs_3_.refs_4_, ...), custom_call_target="tpu_custom_call" | custom-call | tf_op jit(solution)/shard_map/attention_forward/pallas_call | solution.py:604
  84.2 4.5 %collective-permute-done.13.refs_1_.refs_9_ = bf16[192,1024]{1,0:T(8,128)(2,1)S(1)} collective-permute-done((bf16[192,1024]{1,0:T(8,128)(2,1)S(1)}, bf16[192,1024]{1,0:T(8,128)(2,1)S(1)}, u32[]{:S(2)}, u32[]{:S(2)}) %collective-permute-start.13) | collective-permute-done | bytes 393248 | tf_op jit(solution)/shard_map/ppermute | solution.py:324
  88.8 7.9 %attention_forward.4.refs_5_ = f32[1536,256]{1,0:T(8,128)} custom-call(bf16[1536,128]{1,0:T(8,128)(2,1)} %get-tuple-element.109.refs_0_.refs_2_, f32[1536,1]{1,0:T(8,128)} %get-tuple-element.110.refs_1_.refs_3_, s32[6144,1]{1,0:T(8,128)} %ids.1.refs_2_.refs_5_, s32[8,6144]{1,0:T(8,128)} %add_add_fusion.refs_0_.refs_3_.refs_4_, ...), custom_call_target="tpu_custom_call", output_to_operand_aliasing={{}: (5, {})} | custom-call | tf_op jit(solution)/shard_map/attention_forward/pallas_call | solution.py:604
  96.8 8.1 %attention_forward.5 = (f32[1536,256]{1,0:T(8,128)}, bf16[8,192,128]{2,1,0:T(8,128)(2,1)}) custom-call(bf16[1536,128]{1,0:T(8,128)(2,1)} %get-tuple-element.109.refs_0_.refs_2_, f32[1536,1]{1,0:T(8,128)} %get-tuple-element.110.refs_1_.refs_3_, s32[6144,1]{1,0:T(8,128)} %ids.1.refs_2_.refs_5_, ...), custom_call_target="tpu_custom_call", output_to_operand_aliasing={{0}: (5, {})} | custom-call | tf_op jit(solution)/shard_map/attention_forward/pallas_call | solution.py:604
  105.4 4.5 %all-to-all-start.1 = ((bf16[8,192,128]{2,1,0:T(8,128)(2,1)}), bf16[8,192,128]{2,1,0:T(8,128)(2,1)}, u32[]{:S(2)}, u32[]{:S(2)}) async-start(bf16[8,192,128]{2,1,0:T(8,128)(2,1)} %get-tuple-element.115), calls=%async_computation.1 | async-start | bytes 786432 | tf_op jit(solution)/shard_map/all_to_all | solution.py:975
  116.6 7.2 %hidden_back.1.refs_8_ = f32[1536,512]{1,0:T(8,128)} custom-call(bf16[192,1024]{1,0:T(8,128)(2,1)} %refs_2_.6, bf16[192,1024]{1,0:T(8,128)(2,1)} %copy-done.6, bf16[192,1024]{1,0:T(8,128)(2,1)} %copy-done.2, bf16[192,1024]{1,0:T(8,128)(2,1)} %copy-done.4, bf16[192,1024]{1,0:T(8,128)(2,1)} %collective-permute-done.16.refs_4_.refs_12_, ...), custom_call_target="tpu_custom_call" | custom-call | tf_op jit(solution)/shard_map/hidden_back/pallas_call | solution.py:387
  123.8 3.6 %collective-permute-done.22.refs_7_ = bf16[4,16,2048]{2,1,0:T(8,128)(2,1)} collective-permute-done((bf16[4,16,2048]{2,1,0:T(8,128)(2,1)}, bf16[4,16,2048]{2,1,0:T(8,128)(2,1)}, u32[]{:S(2)}, u32[]{:S(2)}) %collective-permute-start.22) | collective-permute-done | bytes 262176 | tf_op jit(solution)/shard_map/ppermute | solution.py:324
  128.1 4.7 %collective-permute-done.20.refs_5_ = bf16[4,16,2048]{2,1,0:T(8,128)(2,1)S(1)} collective-permute-done((bf16[4,16,2048]{2,1,0:T(8,128)(2,1)}, bf16[4,16,2048]{2,1,0:T(8,128)(2,1)S(1)}, u32[]{:S(2)}, u32[]{:S(2)}) %collective-permute-start.20) | collective-permute-done | bytes 262176 | tf_op jit(solution)/shard_map/ppermute | solution.py:324
  135.6 5.9 %project_out.1 = (bf16[192,1024]{1,0:T(8,128)(2,1)}, f32[192,1024]{1,0:T(8,128)}, bf16[192,1024]{1,0:T(8,128)(2,1)}, bf16[1024,1024]{1,0:T(8,128)(2,1)}) custom-call(s32[2]{0:T(128)} %pad_add_fusion.refs_0_.refs_6_, bf16[8,192,128]{2,1,0:T(8,128)(2,1)} %all-to-all-done.1.refs_1_.refs_10_, bf16[192,1024]{1,0:T(8,128)(2,1)} %refs_2_.5, ...), custom_call_target="tpu_custom_call" | custom-call | tf_op jit(solution)/shard_map/project_out/pallas_call | solution.py:387
  145.1 8.9 %collective-permute-done.27.refs_1_ = bf16[192,1024]{1,0:T(8,128)(2,1)S(1)} collective-permute-done((bf16[192,1024]{1,0:T(8,128)(2,1)}, bf16[192,1024]{1,0:T(8,128)(2,1)S(1)}, u32[]{:S(2)}, u32[]{:S(2)}) %collective-permute-start.27) | collective-permute-done | bytes 393248 | tf_op jit(solution)/shard_map/ppermute | solution.py:324
  154.4 8.5 %collective-permute-done.29.refs_3_ = bf16[192,1024]{1,0:T(8,128)(2,1)S(1)} collective-permute-done((bf16[192,1024]{1,0:T(8,128)(2,1)}, bf16[192,1024]{1,0:T(8,128)(2,1)S(1)}, u32[]{:S(2)}, u32[]{:S(2)}) %collective-permute-start.29) | collective-permute-done | bytes 393248 | tf_op jit(solution)/shard_map/ppermute | solution.py:324
  165.7 9.8 %feed_forward.1 = (bf16[192,1024]{1,0:T(8,128)(2,1)S(1)}, bf16[192,1024]{1,0:T(8,128)(2,1)S(1)}, bf16[192,1024]{1,0:T(8,128)(2,1)S(1)}, bf16[192,1024]{1,0:T(8,1...) custom-call(bf16[192,1024]{1,0:T(8,128)(2,1)S(1)} %copy-done.12, ...), custom_call_target="tpu_custom_call" | custom-call | tf_op jit(solution)/shard_map/feed_forward/pallas_call | solution.py:387
  182.6 10.8 %feed_forward_rest.1 = (bf16[4,192,1024]{2,1,0:T(8,128)(2,1)}, bf16[4,192,1024]{2,1,0:T(8,128)(2,1)}, bf16[512,2048]{1,0:T(8,128)(2,1)}) custom-call(bf16[192,1024]{1,0:T(8,128)(2,1)S(1)} %copy-done.13, bf16[192,1024]{1,0:T(8,128)(2,1)S(1)} %collective-permute-done.27.refs_1_, bf16[192,1024]{1,0:T(8,128)(2,1)S(1)} %collective-permute-done.28.refs_2_, ...), custom_call_target="tpu_custom_call" | custom-call | tf_op jit(solution)/shard_map/feed_forward_rest/pallas_call | solution.py:387
  193.4 5.6 %collective-permute-done.38.refs_4_ = bf16[192,1024]{1,0:T(8,128)(2,1)S(1)} collective-permute-done((bf16[192,1024]{1,0:T(8,128)(2,1)S(1)}, bf16[192,1024]{1,0:T(8,128)(2,1)S(1)}, u32[]{:S(2)}, u32[]{:S(2)}) %collective-permute-start.38) | collective-permute-done | bytes 393248 | tf_op jit(solution)/shard_map/ppermute | solution.py:324
  200.0 7.5 %mid.1 = (bf16[192,1024]{1,0:T(8,128)(2,1)}, bf16[8,192,128]{2,1,0:T(8,128)(2,1)}, bf16[512,1152]{1,0:T(8,128)(2,1)}, bf16[512,1152]{1,0:T(8,128)(2,1)}) custom-call(s32[2]{0:T(128)} %pad_add_fusion.refs_0_.refs_6_, bf16[192,1024]{1,0:T(8,128)(2,1)} %copy-done.16, bf16[192,1024]{1,0:T(8,128)(2,1)} %copy-done.26, bf16[192,1024]{1,0:T(8,128)(2,1)} %copy-done.29, ...), custom_call_target="tpu_custom_call" | custom-call | tf_op jit(solution)/shard_map/mid/pallas_call | solution.py:387
  211.6 4.1 %halve.2 = (bf16[256,1152]{1,0:T(8,128)(2,1)}, bf16[256,1152]{1,0:T(8,128)(2,1)}) custom-call(s32[2]{0:T(128)} %pad_add_fusion.refs_0_.refs_6_, bf16[512,1152]{1,0:T(8,128)(2,1)} %get-tuple-element.148.refs_1_, bf16[512,1152]{1,0:T(8,128)(2,1)} %copy-done.39), custom_call_target="tpu_custom_call" | custom-call | flops 99999997952 | bytes 1 | tf_op jit(solution)/shard_map/halve/pallas_call | solution.py:387
  215.9 4.8 %all-to-all-start.2 = ((bf16[8,192,128]{2,1,0:T(8,128)(2,1)}), bf16[8,192,128]{2,1,0:T(8,128)(2,1)S(1)}, u32[]{:S(2)}, u32[]{:S(2)}) async-start(bf16[8,192,128]{2,1,0:T(8,128)(2,1)} %get-tuple-element.152), calls=%async_computation.2 | async-start | bytes 786432 | tf_op jit(solution)/shard_map/all_to_all | solution.py:1032
  228.4 4.5 %all-to-all-done.2.refs_1_ = bf16[8,192,128]{2,1,0:T(8,128)(2,1)S(1)} async-done(((bf16[8,192,128]{2,1,0:T(8,128)(2,1)}), bf16[8,192,128]{2,1,0:T(8,128)(2,1)S(1)}, u32[]{:S(2)}, u32[]{:S(2)}) %all-to-all-start.2) | async-done | bytes 393248 | tf_op jit(solution)/shard_map/all_to_all | solution.py:1032
  233.7 3.6 %turn.1 = (bf16[1536,128]{1,0:T(8,128)(2,1)}, f32[8,1536]{1,0:T(8,128)}) custom-call(s32[2]{0:T(128)} %pad_add_fusion.refs_0_.refs_6_, bf16[8,192,128]{2,1,0:T(8,128)(2,1)} %copy-done.30, f32[1536,256]{1,0:T(8,128)} %get-tuple-element.154.refs_2_), custom_call_target="tpu_custom_call" | custom-call | flops 99999997952 | bytes 1 | tf_op jit(solution)/shard_map/turn/pallas_call | solution.py:387
  237.3 17.6 %attention_backward.2 = (f32[1536,256]{1,0:T(8,128)}, bf16[1536,256]{1,0:T(8,128)(2,1)}, bf16[1536,256]{1,0:T(8,128)(2,1)}) custom-call(bf16[1536,128]{1,0:T(8,128)(2,1)} %get-tuple-element.109.refs_0_.refs_2_, bf16[1536,128]{1,0:T(8,128)(2,1)} %get-tuple-element.155.refs_1_, f32[8,1536]{1,0:T(8,128)} %get-tuple-element.156.refs_2_, ...), custom_call_target="tpu_custom_call" | custom-call | flops 99999997952 | bytes 1 | tf_op jit(solution)/shard_map/attention_backward/pallas_call | solution.py:669
  255.0 3.6 %halve.3 = (bf16[128,1152]{1,0:T(8,128)(2,1)}, bf16[128,1152]{1,0:T(8,128)(2,1)}) custom-call(s32[2]{0:T(128)} %pad_add_fusion.refs_0_.refs_6_, bf16[256,1152]{1,0:T(8,128)(2,1)} %get-tuple-element.161.refs_1_, bf16[256,1152]{1,0:T(8,128)(2,1)} %collective-permute-done.45.refs_2_), custom_call_target="tpu_custom_call" | custom-call | flops 99999997952 | bytes 1 | tf_op jit(solution)/shard_map/halve/pallas_call | solution.py:387
  261.5 18.5 %attention_backward.3 = (f32[1536,256]{1,0:T(8,128)}, bf16[1536,256]{1,0:T(8,128)(2,1)}, bf16[1536,256]{1,0:T(8,128)(2,1)}) custom-call(bf16[1536,128]{1,0:T(8,128)(2,1)} %get-tuple-element.109.refs_0_.refs_2_, bf16[1536,128]{1,0:T(8,128)(2,1)} %get-tuple-element.155.refs_1_, f32[8,1536]{1,0:T(8,128)} %get-tuple-element.156.refs_2_, ...), custom_call_target="tpu_custom_call", output_to_operand_aliasing={{0}: (8, {})} | custom-call | flops 99999997952 | bytes 1 | tf_op jit(solution)/shard_map/attention_backward/pallas_call | solution.py:669
  283.5 7.1 %gather_grads.1 = (bf16[8,192,256]{2,1,0:T(8,128)(2,1)}, bf16[8,32,256]{2,1,0:T(8,128)(2,1)}, bf16[8,32,256]{2,1,0:T(8,128)(2,1)}, bf16[8,32,256]{2,1,0:T(8,128)(2,1)}, bf16[8,32,256]{2,1,0:T(8,128)(2,1)}) custom-call(s32[2]{0:T(128)} %pad_add_fusion.refs_0_.refs_6_, f32[1536,256]{1,0:T(8,128)} %get-tuple-element.167.refs_1_, ...), custom_call_target="tpu_custom_call" | custom-call | flops 99999997952 | bytes 1 | tf_op jit(solution)/shard_map/gather_grads/pallas_call | solution.py:387
  294.0 4.2 %all-to-all-start.3 = ((bf16[8,192,256]{2,1,0:T(8,128)(2,1)}), bf16[8,192,256]{2,1,0:T(8,128)(2,1)}, u32[]{:S(2)}, u32[]{:S(2)}) async-start(bf16[8,192,256]{2,1,0:T(8,128)(2,1)} %get-tuple-element.177), calls=%async_computation.4 | async-start | bytes 1572864 | tf_op jit(solution)/shard_map/all_to_all | solution.py:1090
  315.4 7.6 %all-to-all-done.3.refs_0_ = bf16[8,192,256]{2,1,0:T(8,128)(2,1)} async-done(((bf16[8,192,256]{2,1,0:T(8,128)(2,1)}), bf16[8,192,256]{2,1,0:T(8,128)(2,1)}, u32[]{:S(2)}, u32[]{:S(2)}) %all-to-all-start.3) | async-done | bytes 786464 | tf_op jit(solution)/shard_map/all_to_all | solution.py:1090
  325.1 4.0 %all-to-all-start.4 = ((bf16[8,32,256]{2,1,0:T(8,128)(2,1)}), bf16[8,32,256]{2,1,0:T(8,128)(2,1)}, u32[]{:S(2)}, u32[]{:S(2)}) async-start(bf16[8,32,256]{2,1,0:T(8,128)(2,1)} %sum_rows.1), calls=%async_computation.5 | async-start | bytes 262144 | tf_op jit(solution)/shard_map/all_to_all | solution.py:1107
  329.8 5.7 %last.1 = bf16[192,1024]{1,0:T(8,128)(2,1)} custom-call(bf16[8,192,256]{2,1,0:T(8,128)(2,1)} %all-to-all-done.3.refs_0_, bf16[192,1024]{1,0:T(8,128)(2,1)} %refs_1_.6, bf16[192,1024]{1,0:T(8,128)(2,1)} %refs_2_.6, f32[8,1024]{1,0:T(8,128)} %get-tuple-element.116.refs_3_.refs_8_, bf16[1024,2048]{1,0:T(8,128)(2,1)} %all-gather.4.cloned.1.call-done.refs_4_), custom_call_target="tpu_custom_call" | custom-call | flops 99999997952 | bytes 1 | tf_op jit(solution)/shard_map/last/pallas_call | solution.py:387
  (251 shorter events, 110.9 us)
Async XLA Ops:
  7.2 23.9 %collective-permute-start.3 = (bf16[192,1024]{1,0:T(8,128)(2,1)}, bf16[192,1024]{1,0:T(8,128)(2,1)S(1)}, u32[]{:S(2)}, u32[]{:S(2)}) collective-permute-start(bf16[192,1024]{1,0:T(8,128)(2,1)} %refs_1_.6), channel_id=1, source_target_pairs={{0,4},{1,5},{2,6},{3,7},{4,0},{5,1},{6,2},{7,3},{8,12},{9,13},{10,... | collective-permute-start | bytes 1179656 | tf_op jit(solution)/shard_map/ppermute | solution.py:324
  11.3 18.3 %collective-permute-start.1 = (bf16[192,1024]{1,0:T(8,128)(2,1)}, bf16[192,1024]{1,0:T(8,128)(2,1)S(1)}, u32[]{:S(2)}, u32[]{:S(2)}) collective-permute-start(bf16[192,1024]{1,0:T(8,128)(2,1)} %refs_1_.6), channel_id=1, source_target_pairs={{0,2},{1,3},{2,0},{3,1},{4,6},{5,7},{6,4},{7,5},{8,10},{9,11},{10,... | collective-permute-start | bytes 1179656 | tf_op jit(solution)/shard_map/ppermute | solution.py:324
  12.9 42.3 %collective-permute-start = (bf16[192,1024]{1,0:T(8,128)(2,1)}, bf16[192,1024]{1,0:T(8,128)(2,1)}, u32[]{:S(2)}, u32[]{:S(2)}) collective-permute-start(bf16[192,1024]{1,0:T(8,128)(2,1)} %refs_1_.6), channel_id=1, source_target_pairs={{0,1},{1,0},{2,3},{3,2},{4,5},{5,4},{6,7},{7,6},{8,9},{9,8},{10,11... | collective-permute-start | bytes 1179656 | tf_op jit(solution)/shard_map/ppermute | solution.py:324
  18.6 22.3 %all-to-all-start = ((bf16[8,32,384]{2,1,0:T(8,128)(2,1)}), bf16[8,32,384]{2,1,0:T(8,128)(2,1)S(1)}, u32[]{:S(2)}, u32[]{:S(2)}) async-start(bf16[8,32,384]{2,1,0:T(8,128)(2,1)} %get-tuple-element.107), calls=%async_computation | async-start | bytes 393216 | tf_op jit(solution)/shard_map/all_to_all | solution.py:920
  22.1 74.7 %all-gather.6.cloned.1.call-start = ((), (), s32[]{:S(2)}) async-start(), calls=%async_computation.8 | async-start | bytes 2949120 | tf_op jit(solution)/shard_map/all_gather | solution.py:921
  22.1 33.1 %collective-permute-start.7 = (bf16[192,1024]{1,0:T(8,128)(2,1)}, bf16[192,1024]{1,0:T(8,128)(2,1)S(1)}, u32[]{:S(2)}, u32[]{:S(2)}) collective-permute-start(bf16[192,1024]{1,0:T(8,128)(2,1)} %refs_2_.6), channel_id=1, source_target_pairs={{0,16},{1,17},{2,18},{3,19},{4,20},{5,21},{6,22},{7,23},{8,24},{9,... | collective-permute-start | bytes 1179656 | tf_op jit(solution)/shard_map/ppermute | solution.py:324
  31.2 162.2 %all-gather.4.cloned.1.call-start = ((), (), s32[]{:S(2)}) async-start(), calls=%async_computation.6 | async-start | bytes 4325376 | tf_op jit(solution)/shard_map/all_gather | solution.py:970
  31.2 15.5 %collective-permute-start.5 = (bf16[192,1024]{1,0:T(8,128)(2,1)S(1)}, bf16[192,1024]{1,0:T(8,128)(2,1)}, u32[]{:S(2)}, u32[]{:S(2)}) collective-permute-start(bf16[192,1024]{1,0:T(8,128)(2,1)S(1)} %collective-permute-done.3.refs_5_), channel_id=1, source_target_pairs={{0,2},{1,3},{2,0},{3,1},{4,6},{5,7},{6,4},{7,5},{8,10},{9,11},{10,... | collective-permute-start | bytes 1179656 | tf_op jit(solution)/shard_map/ppermute | solution.py:324
  67.5 21.2 %collective-permute-start.11 = (bf16[1536,256]{1,0:T(8,128)(2,1)}, bf16[1536,256]{1,0:T(8,128)(2,1)}, u32[]{:S(2)}, u32[]{:S(2)}) collective-permute-start(bf16[1536,256]{1,0:T(8,128)(2,1)} %get-tuple-element.111.refs_4_.refs_6_), channel_id=1, source_target_pairs={{0,16},{1,17},{2,18},{3,19},{4,20},{5,21},{6,22},{7,23},{8,24},{9,... | collective-permute-start | bytes 2359304 | tf_op jit(solution)/shard_map/ppermute | solution.py:324
  69.1 15.1 %collective-permute-start.14 = (bf16[192,1024]{1,0:T(8,128)(2,1)S(1)}, bf16[192,1024]{1,0:T(8,128)(2,1)S(1)}, u32[]{:S(2)}, u32[]{:S(2)}) collective-permute-start(bf16[192,1024]{1,0:T(8,128)(2,1)S(1)} %collective-permute-done.7.refs_2_.refs_10_), channel_id=1, source_target_pairs={{0,1},{1,0},{2,3},{3,2},{4,5},{5,4},{6,7},{7,6},{8,9},{9,8},{10,11... | collective-permute-start | bytes 1179656 | tf_op jit(solution)/shard_map/ppermute | solution.py:324
  70.1 18.6 %collective-permute-start.13 = (bf16[192,1024]{1,0:T(8,128)(2,1)S(1)}, bf16[192,1024]{1,0:T(8,128)(2,1)S(1)}, u32[]{:S(2)}, u32[]{:S(2)}) collective-permute-start(bf16[192,1024]{1,0:T(8,128)(2,1)S(1)} %copy-done), channel_id=1, source_target_pairs={{0,1},{1,0},{2,3},{3,2},{4,5},{5,4},{6,7},{7,6},{8,9},{9,8},{10,11... | collective-permute-start | bytes 1179656 | tf_op jit(solution)/shard_map/ppermute | solution.py:324
  105.4 29.5 %all-to-all-start.1 = ((bf16[8,192,128]{2,1,0:T(8,128)(2,1)}), bf16[8,192,128]{2,1,0:T(8,128)(2,1)}, u32[]{:S(2)}, u32[]{:S(2)}) async-start(bf16[8,192,128]{2,1,0:T(8,128)(2,1)} %get-tuple-element.115), calls=%async_computation.1 | async-start | bytes 786432 | tf_op jit(solution)/shard_map/all_to_all | solution.py:975
  112.2 15.3 %collective-permute-start.22 = (bf16[4,16,2048]{2,1,0:T(8,128)(2,1)}, bf16[4,16,2048]{2,1,0:T(8,128)(2,1)}, u32[]{:S(2)}, u32[]{:S(2)}) collective-permute-start(bf16[4,16,2048]{2,1,0:T(8,128)(2,1)} %slice.78.refs_4_), channel_id=1, source_target_pairs={{0,17},{1,16},{2,19},{3,18},{4,21},{5,20},{6,23},{7,22},{8,25},{9,... | collective-permute-start | bytes 786440 | tf_op jit(solution)/shard_map/ppermute | solution.py:324
  114.2 13.8 %collective-permute-start.21 = (bf16[4,16,2048]{2,1,0:T(8,128)(2,1)}, bf16[4,16,2048]{2,1,0:T(8,128)(2,1)S(1)}, u32[]{:S(2)}, u32[]{:S(2)}) collective-permute-start(bf16[4,16,2048]{2,1,0:T(8,128)(2,1)} %slice.78.refs_4_), channel_id=1, source_target_pairs={{0,16},{1,17},{2,18},{3,19},{4,20},{5,21},{6,22},{7,23},{8,24},{9,... | collective-permute-start | bytes 786440 | tf_op jit(solution)/shard_map/ppermute | solution.py:324
  115.7 17.1 %collective-permute-start.20 = (bf16[4,16,2048]{2,1,0:T(8,128)(2,1)}, bf16[4,16,2048]{2,1,0:T(8,128)(2,1)S(1)}, u32[]{:S(2)}, u32[]{:S(2)}) collective-permute-start(bf16[4,16,2048]{2,1,0:T(8,128)(2,1)} %slice.78.refs_4_), channel_id=1, source_target_pairs={{0,1},{1,0},{2,3},{3,2},{4,5},{5,4},{6,7},{7,6},{8,9},{9,8},{10,11... | collective-permute-start | bytes 786440 | tf_op jit(solution)/shard_map/ppermute | solution.py:324
  141.5 12.4 %collective-permute-start.27 = (bf16[192,1024]{1,0:T(8,128)(2,1)}, bf16[192,1024]{1,0:T(8,128)(2,1)S(1)}, u32[]{:S(2)}, u32[]{:S(2)}) collective-permute-start(bf16[192,1024]{1,0:T(8,128)(2,1)} %get-tuple-element.129.refs_0_), channel_id=1, source_target_pairs={{0,1},{1,0},{2,3},{3,2},{4,5},{5,4},{6,7},{7,6},{8,9},{9,8},{10,11... | collective-permute-start | bytes 1179656 | tf_op jit(solution)/shard_map/ppermute | solution.py:324
  142.8 20.2 %collective-permute-start.29 = (bf16[192,1024]{1,0:T(8,128)(2,1)}, bf16[192,1024]{1,0:T(8,128)(2,1)S(1)}, u32[]{:S(2)}, u32[]{:S(2)}) collective-permute-start(bf16[192,1024]{1,0:T(8,128)(2,1)} %get-tuple-element.129.refs_0_), channel_id=1, source_target_pairs={{0,17},{1,16},{2,19},{3,18},{4,21},{5,20},{6,23},{7,22},{8,25},{9,... | collective-permute-start | bytes 1179656 | tf_op jit(solution)/shard_map/ppermute | solution.py:324
  145.0 17.9 %collective-permute-start.30 = (bf16[192,1024]{1,0:T(8,128)(2,1)}, bf16[192,1024]{1,0:T(8,128)(2,1)S(1)}, u32[]{:S(2)}, u32[]{:S(2)}) collective-permute-start(bf16[192,1024]{1,0:T(8,128)(2,1)} %get-tuple-element.129.refs_0_), channel_id=1, source_target_pairs={{0,8},{1,9},{2,10},{3,11},{4,12},{5,13},{6,14},{7,15},{8,0},{9,1},... | collective-permute-start | bytes 1179656 | tf_op jit(solution)/shard_map/ppermute | solution.py:324
  177.3 16.1 %collective-permute-start.34 = (bf16[192,1024]{1,0:T(8,128)(2,1)S(1)}, bf16[192,1024]{1,0:T(8,128)(2,1)S(1)}, u32[]{:S(2)}, u32[]{:S(2)}) collective-permute-start(bf16[192,1024]{1,0:T(8,128)(2,1)S(1)} %get-tuple-element.135), channel_id=1, source_target_pairs={{0,8},{1,9},{2,10},{3,11},{4,12},{5,13},{6,14},{7,15},{8,0},{9,1},... | collective-permute-start | bytes 1179656 | tf_op jit(solution)/shard_map/ppermute | solution.py:324
  178.5 14.9 %collective-permute-start.40 = (bf16[192,1024]{1,0:T(8,128)(2,1)S(1)}, bf16[192,1024]{1,0:T(8,128)(2,1)S(1)}, u32[]{:S(2)}, u32[]{:S(2)}) collective-permute-start(bf16[192,1024]{1,0:T(8,128)(2,1)S(1)} %add_convert_fusion.1), channel_id=1, source_target_pairs={{0,17},{1,16},{2,19},{3,18},{4,21},{5,20},{6,23},{7,22},{8,25},{9,... | collective-permute-start | bytes 1179656 | tf_op jit(solution)/shard_map/ppermute | solution.py:324
  180.0 19.1 %collective-permute-start.38 = (bf16[192,1024]{1,0:T(8,128)(2,1)S(1)}, bf16[192,1024]{1,0:T(8,128)(2,1)S(1)}, u32[]{:S(2)}, u32[]{:S(2)}) collective-permute-start(bf16[192,1024]{1,0:T(8,128)(2,1)S(1)} %add_convert_fusion.2), channel_id=1, source_target_pairs={{0,16},{1,17},{2,18},{3,19},{4,20},{5,21},{6,22},{7,23},{8,24},{9,... | collective-permute-start | bytes 1179656 | tf_op jit(solution)/shard_map/ppermute | solution.py:324
  181.0 18.1 %collective-permute-start.36 = (bf16[192,1024]{1,0:T(8,128)(2,1)S(1)}, bf16[192,1024]{1,0:T(8,128)(2,1)S(1)}, u32[]{:S(2)}, u32[]{:S(2)}) collective-permute-start(bf16[192,1024]{1,0:T(8,128)(2,1)S(1)} %add_convert_fusion.3), channel_id=1, source_target_pairs={{0,1},{1,0},{2,3},{3,2},{4,5},{5,4},{6,7},{7,6},{8,9},{9,8},{10,11... | collective-permute-start | bytes 1179656 | tf_op jit(solution)/shard_map/ppermute | solution.py:324
  215.9 17.0 %all-to-all-start.2 = ((bf16[8,192,128]{2,1,0:T(8,128)(2,1)}), bf16[8,192,128]{2,1,0:T(8,128)(2,1)S(1)}, u32[]{:S(2)}, u32[]{:S(2)}) async-start(bf16[8,192,128]{2,1,0:T(8,128)(2,1)} %get-tuple-element.152), calls=%async_computation.2 | async-start | bytes 786432 | tf_op jit(solution)/shard_map/all_to_all | solution.py:1032
  220.7 59.6 %reduce-scatter.2.cloned.1.call-start = ((), (), s32[]{:S(2)}) async-start(), calls=%async_computation.7 | async-start | bytes 2621440 | tf_op jit(solution)/shard_map/reduce_scatter | solution.py:1067
  221.4 33.5 %collective-permute-start.45 = (bf16[256,1152]{1,0:T(8,128)(2,1)}, bf16[256,1152]{1,0:T(8,128)(2,1)}, u32[]{:S(2)}, u32[]{:S(2)}) collective-permute-start(bf16[256,1152]{1,0:T(8,128)(2,1)} %get-tuple-element.150), channel_id=1, source_target_pairs={{0,16},{1,17},{2,18},{3,19},{4,20},{5,21},{6,22},{7,23},{8,24},{9,... | collective-permute-start | bytes 1769480 | tf_op jit(solution)/shard_map/ppermute | solution.py:324
  226.4 35.1 %collective-permute-start.43 = (bf16[2,192,1024]{2,1,0:T(8,128)(2,1)}, bf16[2,192,1024]{2,1,0:T(8,128)(2,1)}, u32[]{:S(2)}, u32[]{:S(2)}) collective-permute-start(bf16[2,192,1024]{2,1,0:T(8,128)(2,1)} %slice.80), channel_id=1, source_target_pairs={{0,1},{1,0},{2,3},{3,2},{4,5},{5,4},{6,7},{7,6},{8,9},{9,8},{10,11... | collective-permute-start | bytes 2359304 | tf_op jit(solution)/shard_map/ppermute | solution.py:324
  259.9 20.1 %collective-permute-start.46 = (bf16[1536,256]{1,0:T(8,128)(2,1)S(1)}, bf16[1536,256]{1,0:T(8,128)(2,1)S(1)}, u32[]{:S(2)}, u32[]{:S(2)}) collective-permute-start(bf16[1536,256]{1,0:T(8,128)(2,1)S(1)} %add_convert_fusion), channel_id=1, source_target_pairs={{0,16},{1,17},{2,18},{3,19},{4,20},{5,21},{6,22},{7,23},{8,24},{9,... | collective-permute-start | bytes 2359304 | tf_op jit(solution)/shard_map/ppermute | solution.py:324
  294.0 28.9 %all-to-all-start.3 = ((bf16[8,192,256]{2,1,0:T(8,128)(2,1)}), bf16[8,192,256]{2,1,0:T(8,128)(2,1)}, u32[]{:S(2)}, u32[]{:S(2)}) async-start(bf16[8,192,256]{2,1,0:T(8,128)(2,1)} %get-tuple-element.177), calls=%async_computation.4 | async-start | bytes 1572864 | tf_op jit(solution)/shard_map/all_to_all | solution.py:1090
  307.4 15.5 %collective-permute-start.53 = (bf16[32,1152]{1,0:T(8,128)(2,1)}, bf16[32,1152]{1,0:T(8,128)(2,1)S(1)}, u32[]{:S(2)}, u32[]{:S(2)}) collective-permute-start(bf16[32,1152]{1,0:T(8,128)(2,1)} %get-tuple-element.191), channel_id=1, source_target_pairs={{0,2},{1,3},{2,0},{3,1},{4,6},{5,7},{6,4},{7,5},{8,10},{9,11},{10,... | collective-permute-start | bytes 221192 | tf_op jit(solution)/shard_map/ppermute | solution.py:324
  307.5 16.9 %collective-permute-start.54 = (bf16[32,1152]{1,0:T(8,128)(2,1)}, bf16[32,1152]{1,0:T(8,128)(2,1)S(1)}, u32[]{:S(2)}, u32[]{:S(2)}) collective-permute-start(bf16[32,1152]{1,0:T(8,128)(2,1)} %get-tuple-element.193), channel_id=1, source_target_pairs={{0,4},{1,5},{2,6},{3,7},{4,0},{5,1},{6,2},{7,3},{8,12},{9,13},{10,... | collective-permute-start | bytes 221192 | tf_op jit(solution)/shard_map/ppermute | solution.py:324
  309.3 15.1 %collective-permute-start.55 = (bf16[32,1152]{1,0:T(8,128)(2,1)}, bf16[32,1152]{1,0:T(8,128)(2,1)S(1)}, u32[]{:S(2)}, u32[]{:S(2)}) collective-permute-start(bf16[32,1152]{1,0:T(8,128)(2,1)} %get-tuple-element.195), channel_id=1, source_target_pairs={{0,6},{1,7},{2,4},{3,5},{4,2},{5,3},{6,0},{7,1},{8,14},{9,15},{10,... | collective-permute-start | bytes 221192 | tf_op jit(solution)/shard_map/ppermute | solution.py:324
  314.0 15.8 %collective-permute-start.51 = (bf16[192,1024]{1,0:T(8,128)(2,1)S(1)}, bf16[192,1024]{1,0:T(8,128)(2,1)}, u32[]{:S(2)}, u32[]{:S(2)}) collective-permute-start(bf16[192,1024]{1,0:T(8,128)(2,1)S(1)} %fusion.3), channel_id=1, source_target_pairs={{0,16},{1,17},{2,18},{3,19},{4,20},{5,21},{6,22},{7,23},{8,24},{9,... | collective-permute-start | bytes 1179656 | tf_op jit(solution)/shard_map/ppermute | solution.py:324
  (79 other events, 526.7 us)
Sparse Core Ops, SparseCore 0:
  31.3 50.4 all-gather.5
  88.8 65.4 all-gather.3
  223.8 45.3 reduce-scatter.1
